TPU v7x, 32 devices: a whole 2x2x4 slice. The times are simulated.
32 devices in a mesh: groups: 2 (over y), space: 4 (over z), dp: 2 (over x), chan: 2 (over core).
Axes of the slice: x: 2, y: 2, z: 4, core: 2. Of those that a mesh axis runs over, the one named last changes fastest.
Arguments:
- coarse: bfloat16 [4, 4, 4, 8, 512], P(('groups', 'dp'), 'space'), parts along dimension 0, may hold values from -6 to 6
- skip: bfloat16 [4, 8, 16, 8, 256], P(('groups', 'dp'), 'space', None, None, 'chan'), parts along dimension 0, may hold values from -6 to 6
- up_weight: bfloat16 [8, 512, 2, 128], P(None, 'space', 'chan', 'dp'), may hold values from -0.25 to 0.25
- up_bias: float32 [256], P('chan'), may hold values from -3 to 3
- first_weight: bfloat16 [27, 512, 2, 128], P(None, 'space', 'chan', 'dp'), may hold values from -0.0546875 to 0.0546875
- first_bias: float32 [256], P('chan'), may hold values from -3 to 3
- second_weight: bfloat16 [27, 256, 2, 128], P(None, 'space', 'chan', 'dp'), may hold values from -0.078125 to 0.078125
- second_bias: float32 [256], P('chan'), may hold values from -3 to 3
Outputs:
- refined: bfloat16 [4, 8, 16, 8, 256], P(('groups', 'dp'), 'space', None, None, 'chan'), parts along dimension 0
There are 2 independent parts, one for each index of `groups`. A program takes and returns all parts, laid end to end along the dimension named above; an argument that names none is the same for every part. Nothing has to cross between parts.
All inputs are finite; a program needn't handle non-finite values.
Results may differ from a plain program's by a relative error of at most 0.0045.
Values may be sent and summed in bfloat16 or wider, within the bound.
No kernel may reach another device: no remote copies, remote signals or barrier semaphores. Data moves between devices by JAX's collectives and lax.ppermute only.
A program may use at most 64 MiB of HBM per device.

v0:
```python
import jax
import jax.numpy as jnp
from jax import lax
from jax.sharding import PartitionSpec as P


def padded_2(array, sides, width):
    for axis, dim in sides:
        peers, length = (lax.axis_size(axis), array.shape[dim])
        up = [(i, (i + 1) % peers) for i in range(peers - 1)]
        down = [(j, i) for i, j in up]
        last = lax.slice_in_dim(array, length - width, length, axis=dim)
        first = lax.slice_in_dim(array, 0, width, axis=dim)
        before = lax.ppermute(last, axis, up)
        after = lax.ppermute(first, axis, down)
        array = jnp.concatenate([before, array, after], axis=dim)
    return array


def alternate(total, bias):
    samples, depth_cells, width_cells, height_cells, taps, outputs = total.shape
    grid = total.reshape(samples, depth_cells, width_cells, height_cells, 2, 2, 2, outputs)
    grid = grid.transpose(0, 2, 4, 3, 5, 1, 6, 7)
    grid = grid.reshape(samples, 2 * width_cells, 2 * height_cells, 2 * depth_cells, outputs)
    return (grid + bias).astype(jnp.bfloat16)


def upsample_block(coarse, up_weight):
    columns = lax.all_gather(up_weight, "dp", axis=3, tiled=True)[:, :, 0, :]
    initial = jnp.zeros(coarse.shape[:4] + (8, columns.shape[2]), jnp.float32)

    def accumulate(summed, weight_rows, offset):
        return jnp.einsum(
            "szxyi,kio->szxyko", coarse, weight_rows, preferred_element_type=jnp.float32
        )

    return accumulate(initial, lax.all_gather(columns, "space", axis=1, tiled=True), jnp.int32(0))


def spatial_conv(padded, weight_block):
    kernel = weight_block.reshape(3, 3, 3, weight_block.shape[1], weight_block.shape[2])
    return lax.conv_general_dilated(
        padded,
        kernel,
        (1, 1, 1),
        [(0, 0), (1, 1), (1, 1)],
        dimension_numbers=("NDHWC", "DHWIO", "NDHWC"),
        preferred_element_type=jnp.float32,
    )


def folded_conv(padded, columns, base_shape):
    initial = jnp.zeros(base_shape + (columns.shape[2],), jnp.float32)

    def accumulate(summed, weight_rows, offset):
        sliced = lax.dynamic_slice_in_dim(padded, offset, weight_rows.shape[1], 4)
        return summed + spatial_conv(sliced, weight_rows)

    return (accumulate, initial)


def body(coarse, skip, up_weight, up_bias, first_weight, first_bias, second_weight, second_bias):
    slabs = lax.all_to_all(coarse, "space", split_axis=2, concat_axis=1, tiled=True)
    upsampled = alternate(upsample_block(slabs, up_weight), up_bias)
    up_full, skip_full = (
        lax.all_gather(upsampled, "chan", axis=4, tiled=True),
        lax.all_gather(skip, "chan", axis=4, tiled=True),
    )
    joined = jnp.concatenate([up_full, skip_full], axis=4)
    padded = padded_2(joined, (("space", 1),), 1)
    base_shape = joined.shape[:4]
    first_columns = lax.all_gather(first_weight, "dp", axis=3, tiled=True)[:, :, 0, :]
    accumulate, initial = folded_conv(padded, first_columns, base_shape)
    first = accumulate(
        initial, lax.all_gather(first_columns, "space", axis=1, tiled=True), jnp.int32(0)
    )
    hidden = jax.nn.silu(first + first_bias).astype(jnp.bfloat16)
    hidden_full = lax.all_gather(hidden, "chan", axis=4, tiled=True)
    hidden_padded = padded_2(hidden_full, (("space", 1),), 1)
    second_columns = lax.all_gather(second_weight, "dp", axis=3, tiled=True)[:, :, 0, :]
    accumulate_two, initial_two = folded_conv(hidden_padded, second_columns, base_shape)
    second = accumulate_two(
        initial_two, lax.all_gather(second_columns, "space", axis=1, tiled=True), jnp.int32(0)
    )
    return (second + second_bias).astype(jnp.bfloat16)


def solution(mesh):
    return jax.shard_map(
        body,
        mesh=mesh,
        in_specs=(
            P(("groups", "dp"), "space", None, None, None),
            P(("groups", "dp"), "space", None, None, "chan"),
            P(None, "space", "chan", "dp"),
            P("chan"),
            P(None, "space", "chan", "dp"),
            P("chan"),
            P(None, "space", "chan", "dp"),
            P("chan"),
        ),
        out_specs=P(("groups", "dp"), "space", None, None, "chan"),
        check_vma=False,
    )
```

profile of v0, /device:TPU:0, one launch (start us, length us, event | category | flops | bytes accessed | tf_op | source)
XLA Modules:
  0.0 174.1 jit_solution(9554793296026758286)
XLA Ops:
  6.5 0.0 all-gather.7.cloned.1.call-start
  6.5 9.0 %all_gather.27 = bf16[8,128,1,128]{1,3,2,0:T(8,128)(2,1)} all-gather(bf16[8,128,1,64]{1,3,2,0:T(8,128)(2,1)} %param.10), channel_id=1, replica_groups=mesh['groups'=2,'space'=4,'dp'=2,'chan'=2] {'dp'}, dimensions={3}, use_global_device_ids=true | all-gather | bytes 393216 | tf_op jit(solution)/shard_map/all_gather | solution.py:29
  15.5 0.0 copy-start
  15.5 0.0 all-gather.7.cloned.1.call-update
  15.5 0.0 all-gather.9.cloned.1.call-start
  15.6 13.1 %all_gather.31 = bf16[27,128,1,128]{1,3,2,0:T(8,128)(2,1)} all-gather(bf16[27,128,1,64]{1,3,2,0:T(8,128)(2,1)} %param.12), channel_id=1, replica_groups=mesh['groups'=2,'space'=4,'dp'=2,'chan'=2] {'dp'}, dimensions={3}, use_global_device_ids=true | all-gather | bytes 1327104 | tf_op jit(solution)/shard_map/all_gather | solution.py:72
  28.7 0.0 copy-start.1
  28.7 0.0 all-gather.9.cloned.1.call-update
  28.7 5.6 %all-to-all-start = ((bf16[1,1,4,8,512]{4,3,1,0,2:T(8,128)(2,1)}), bf16[1,1,4,8,512]{4,3,1,0,2:T(8,128)(2,1)S(1)}, u32[]{:S(2)}, u32[]{:S(2)}) async-start(bf16[1,1,4,8,512]{4,3,1,0,2:T(8,128)(2,1)} %bitcast.32), calls=%async_computation | async-start | bytes 65536 | tf_op jit(solution)/shard_map/all_to_all | solution.py:63
  34.3 0.0 all-gather.11.cloned.1.call-start
  34.3 1.8 %copy.38 = bf16[27,64,1,64]{1,0,2,3:T(8,128)(2,1)S(1)} copy(bf16[27,64,1,64]{3,1,2,0:T(8,128)(2,1)} %param.14) | data formatting | bytes 442368 | tf_op args[6]
  36.0 12.9 %all_gather.34 = bf16[27,64,1,128]{1,0,2,3:T(8,128)(2,1)S(1)} all-gather(bf16[27,64,1,64]{1,0,2,3:T(8,128)(2,1)S(1)} %copy.38), channel_id=1, replica_groups=mesh['groups'=2,'space'=4,'dp'=2,'chan'=2] {'dp'}, dimensions={3}, use_global_device_ids=true | all-gather | bytes 663552 | tf_op jit(solution)/shard_map/all_gather | solution.py:80
  48.9 1.7 copy.39
  50.6 0.0 all-gather.11.cloned.1.call-update
  50.7 0.0 copy-done
  50.7 1.9 %all_gather.30 = bf16[1,2,16,8,256]{4,3,2,1,0:T(8,128)(2,1)S(1)} all-gather(bf16[1,2,16,8,128]{4,3,2,1,0:T(8,128)(2,1)S(1)} %copy-done), channel_id=1, replica_groups=mesh['groups'=2,'space'=4,'dp'=2,'chan'=2] {'chan'}, dimensions={4}, use_global_device_ids=true | all-gather | bytes 196608 | tf_op jit(solution)/shard_map/all_gather | solution.py:67
  52.6 0.0 all-to-all-done
  52.6 0.0 all-gather.7.cloned.1.call-done
  52.6 1.6 convolution_bitcast_fusion
  54.2 0.1 copy.34
  54.3 0.0 copy-done.1
  54.3 1.9 %all_gather.29 = bf16[1,2,16,8,256]{4,3,2,1,0:T(8,128)(2,1)S(1)} all-gather(bf16[1,2,16,8,128]{4,3,2,1,0:T(8,128)(2,1)S(1)} %add_convert_fusion.1), channel_id=1, replica_groups=mesh['groups'=2,'space'=4,'dp'=2,'chan'=2] {'chan'}, dimensions={4}, use_global_device_ids=true | all-gather | bytes 196608 | tf_op jit(solution)/shard_map/all_gather | solution.py:66
  56.3 3.7 %collective-permute-start = (bf16[1,1,16,8,512]{4,3,2,1,0:T(8,128)(2,1)S(1)}, bf16[1,1,16,8,512]{4,3,2,1,0:T(8,128)(2,1)S(1)}, u32[]{:S(2)}, u32[]{:S(2)}) collective-permute-start(bf16[1,1,16,8,512]{4,3,2,1,0:T(8,128)(2,1)S(1)} %get-tuple-element.5), channel_id=1, source_target_pairs={{0,4},{4,8},{8,12},{1,5},{5,9},{9,13},{2,6},{6,10},{10,14},{3,7},{... | collective-permute-start | bytes 393224 | tf_op jit(solution)/shard_map/ppermute | solution.py:14
  59.9 1.3 collective-permute-start.1
  61.2 5.1 %collective-permute-done = bf16[1,1,16,8,512]{4,3,2,1,0:T(8,128)(2,1)S(1)} collective-permute-done((bf16[1,1,16,8,512]{4,3,2,1,0:T(8,128)(2,1)S(1)}, bf16[1,1,16,8,512]{4,3,2,1,0:T(8,128)(2,1)S(1)}, u32[]{:S(2)}, u32[]{:S(2)}) %collective-permute-start) | collective-permute-done | bytes 131104 | tf_op jit(solution)/shard_map/ppermute | solution.py:14
  66.3 5.5 %collective-permute-done.1 = bf16[1,1,16,8,512]{4,3,2,1,0:T(8,128)(2,1)S(1)} collective-permute-done((bf16[1,1,16,8,512]{4,3,2,1,0:T(8,128)(2,1)S(1)}, bf16[1,1,16,8,512]{4,3,2,1,0:T(8,128)(2,1)S(1)}, u32[]{:S(2)}, u32[]{:S(2)}) %collective-permute-start.1) | collective-permute-done | bytes 131104 | tf_op jit(solution)/shard_map/ppermute | solution.py:15
  71.8 0.1 pad_maximum_fusion
  71.9 50.7 %all-gather.9.cloned.1.call-done = bf16[27,512,1,128]{1,3,2,0:T(8,128)(2,1)} async-done(((bf16[27,128,1,128]{1,3,2,0:T(8,128)(2,1)}), bf16[27,512,1,128]{1,3,2,0:T(8,128)(2,1)}) %all-gather.9.cloned.1.call-update) | async-done | bytes 3538960 | tf_op jit(solution)/shard_map/all_gather | solution.py:75
  122.6 0.0 copy-start.2
  122.6 7.8 %fusion = f32[1,2,16,8,128]{4,0,3,2,1:T(1,128)S(1)} fusion(bf16[3,3,3,512,128]{3,4,2,1,0:T(8,128)(2,1)} %bitcast.33, bf16[1,4,16,8,512]{4,3,2,1,0:T(8,128)(2,1)S(1)} %pad_maximum_fusion), kind=kOutput, calls=%fused_computation.1 | convolution fusion | flops 795869184 | bytes 4194304 | tf_op jit(solution)/shard_map/conv_general_dilated | solution.py:42
  130.4 0.0 copy-done.2
  130.5 1.9 %all_gather.33 = bf16[1,2,16,8,256]{4,3,2,1,0:T(8,128)(2,1)S(1)} all-gather(bf16[1,2,16,8,128]{4,3,2,1,0:T(8,128)(2,1)S(1)} %multiply_convert_fusion), channel_id=1, replica_groups=mesh['groups'=2,'space'=4,'dp'=2,'chan'=2] {'chan'}, dimensions={4}, use_global_device_ids=true | all-gather | bytes 196608 | tf_op jit(solution)/shard_map/all_gather | solution.py:78
  132.4 1.3 collective-permute-start.2
  133.7 1.3 collective-permute-start.3
  135.0 2.3 %collective-permute-done.2 = bf16[1,1,16,8,256]{4,3,2,1,0:T(8,128)(2,1)S(1)} collective-permute-done((bf16[1,1,16,8,256]{4,3,2,1,0:T(8,128)(2,1)S(1)}, bf16[1,1,16,8,256]{4,3,2,1,0:T(8,128)(2,1)S(1)}, u32[]{:S(2)}, u32[]{:S(2)}) %collective-permute-start.2) | collective-permute-done | bytes 65568 | tf_op jit(solution)/shard_map/ppermute | solution.py:14
  137.3 6.4 %collective-permute-done.3 = bf16[1,1,16,8,256]{4,3,2,1,0:T(8,128)(2,1)S(1)} collective-permute-done((bf16[1,1,16,8,256]{4,3,2,1,0:T(8,128)(2,1)S(1)}, bf16[1,1,16,8,256]{4,3,2,1,0:T(8,128)(2,1)S(1)}, u32[]{:S(2)}, u32[]{:S(2)}) %collective-permute-start.3) | collective-permute-done | bytes 65568 | tf_op jit(solution)/shard_map/ppermute | solution.py:15
  143.8 18.8 %all-gather.11.cloned.1.call-done = bf16[27,256,1,128]{3,1,2,0:T(8,128)(2,1)} async-done(((bf16[27,64,1,128]{3,1,2,0:T(8,128)(2,1)}), bf16[27,256,1,128]{3,1,2,0:T(8,128)(2,1)}) %all-gather.11.cloned.1.call-update) | async-done | bytes 1769488 | tf_op jit(solution)/shard_map/all_gather | solution.py:83
  162.6 0.0 copy-start.3
  162.6 4.3 %fusion.2 = f32[1,2,16,8,128]{4,0,3,2,1:T(1,128)S(1)} fusion(bf16[3,3,3,256,128]{4,3,2,1,0:T(8,128)(2,1)} %bitcast.34, bf16[1,4,16,8,256]{4,3,2,1,0:T(8,128)(2,1)S(1)} %pad_maximum_fusion.1), kind=kOutput, calls=%fused_computation.4 | convolution fusion | flops 397934592 | bytes 2162688 | tf_op jit(solution)/shard_map/conv_general_dilated | solution.py:42
  166.9 0.0 copy-done.3
  166.9 0.6 add_convert_fusion
  (7 shorter events, 0.1 us)
Async XLA Ops:
  6.5 46.0 %all-gather.7.cloned.1.call-start = ((), (), s32[]{:S(2)}) async-start(), calls=%async_computation.1 | async-start | bytes 1310720 | tf_op jit(solution)/shard_map/all_gather | solution.py:37
  15.5 35.2 %copy-start = (bf16[1,2,16,8,128]{4,3,2,1,0:T(8,128)(2,1)S(1)}, bf16[1,2,16,8,128]{4,3,2,1,0:T(8,128)(2,1)}, u32[]{:S(2)}) copy-start(bf16[1,2,16,8,128]{4,3,2,1,0:T(8,128)(2,1)} %param.9) | copy-start | bytes 196612
  15.5 107.0 %all-gather.9.cloned.1.call-start = ((), (), s32[]{:S(2)}) async-start(), calls=%async_computation.2 | async-start | bytes 4423680 | tf_op jit(solution)/shard_map/all_gather | solution.py:75
  28.7 25.6 %copy-start.1 = (f32[128]{0:T(128)S(1)}, f32[128]{0:T(128)}, u32[]{:S(2)}) copy-start(f32[128]{0:T(128)} %param.11) | copy-start | bytes 1540
  28.7 23.9 %all-to-all-start = ((bf16[1,1,4,8,512]{4,3,1,0,2:T(8,128)(2,1)}), bf16[1,1,4,8,512]{4,3,1,0,2:T(8,128)(2,1)S(1)}, u32[]{:S(2)}, u32[]{:S(2)}) async-start(bf16[1,1,4,8,512]{4,3,1,0,2:T(8,128)(2,1)} %bitcast.32), calls=%async_computation | async-start | bytes 65536 | tf_op jit(solution)/shard_map/all_to_all | solution.py:63
  34.3 128.3 %all-gather.11.cloned.1.call-start = ((), (), s32[]{:S(2)}) async-start(), calls=%async_computation.3 | async-start | bytes 2211840 | tf_op jit(solution)/shard_map/all_gather | solution.py:83
  56.3 10.0 %collective-permute-start = (bf16[1,1,16,8,512]{4,3,2,1,0:T(8,128)(2,1)S(1)}, bf16[1,1,16,8,512]{4,3,2,1,0:T(8,128)(2,1)S(1)}, u32[]{:S(2)}, u32[]{:S(2)}) collective-permute-start(bf16[1,1,16,8,512]{4,3,2,1,0:T(8,128)(2,1)S(1)} %get-tuple-element.5), channel_id=1, source_target_pairs={{0,4},{4,8},{8,12},{1,5},{5,9},{9,13},{2,6},{6,10},{10,14},{3,7},{... | collective-permute-start | bytes 393224 | tf_op jit(solution)/shard_map/ppermute | solution.py:14
  59.9 11.9 %collective-permute-start.1 = (bf16[1,1,16,8,512]{4,3,2,1,0:T(8,128)(2,1)S(1)}, bf16[1,1,16,8,512]{4,3,2,1,0:T(8,128)(2,1)S(1)}, u32[]{:S(2)}, u32[]{:S(2)}) collective-permute-start(bf16[1,1,16,8,512]{4,3,2,1,0:T(8,128)(2,1)S(1)} %get-tuple-element.6), channel_id=1, source_target_pairs={{4,0},{8,4},{12,8},{5,1},{9,5},{13,9},{6,2},{10,6},{14,10},{7,3},{... | collective-permute-start | bytes 393224 | tf_op jit(solution)/shard_map/ppermute | solution.py:15
  122.6 7.8 %copy-start.2 = (f32[128]{0:T(128)S(1)}, f32[128]{0:T(128)}, u32[]{:S(2)}) copy-start(f32[128]{0:T(128)} %param.13) | copy-start | bytes 1540
  132.4 4.9 %collective-permute-start.2 = (bf16[1,1,16,8,256]{4,3,2,1,0:T(8,128)(2,1)S(1)}, bf16[1,1,16,8,256]{4,3,2,1,0:T(8,128)(2,1)S(1)}, u32[]{:S(2)}, u32[]{:S(2)}) collective-permute-start(bf16[1,1,16,8,256]{4,3,2,1,0:T(8,128)(2,1)S(1)} %get-tuple-element.7), channel_id=1, source_target_pairs={{0,4},{4,8},{8,12},{1,5},{5,9},{9,13},{2,6},{6,10},{10,14},{3,7},{... | collective-permute-start | bytes 196616 | tf_op jit(solution)/shard_map/ppermute | solution.py:14
  133.7 10.1 %collective-permute-start.3 = (bf16[1,1,16,8,256]{4,3,2,1,0:T(8,128)(2,1)S(1)}, bf16[1,1,16,8,256]{4,3,2,1,0:T(8,128)(2,1)S(1)}, u32[]{:S(2)}, u32[]{:S(2)}) collective-permute-start(bf16[1,1,16,8,256]{4,3,2,1,0:T(8,128)(2,1)S(1)} %get-tuple-element.8), channel_id=1, source_target_pairs={{4,0},{8,4},{12,8},{5,1},{9,5},{13,9},{6,2},{10,6},{14,10},{7,3},{... | collective-permute-start | bytes 196616 | tf_op jit(solution)/shard_map/ppermute | solution.py:15
  162.6 4.3 %copy-start.3 = (f32[128]{0:T(128)S(1)}, f32[128]{0:T(128)}, u32[]{:S(2)}) copy-start(f32[128]{0:T(128)} %param.15) | copy-start | bytes 1540
Sparse Core Ops, SparseCore 0:
  15.7 31.1 all-gather.6
  48.5 74.0 all-gather.8
  124.1 38.3 all-gather.10
where the time goes:
time: 175 us; the launch traced here: 174 us
  waiting for transfers between devices  88.8 us (51%)
  blocking collectives  40.6 us (23%)
  matrix products  13.8 us (8%)
  between operations  13.2 us (8%)
  starting transfers between devices  13.1 us (7%)
  local copies, waits for them, and re-layouts  3.63 us (2%)
    all_gather x1, waiting for transfers between devices, body(): lax.all_gather(first_columns, 'space', axis=1, tiled=True)  50.7 us
    all_gather x1, waiting for transfers between devices, body(): lax.all_gather(second_columns, 'space', axis=1, tiled=True)  18.8 us
    all_gather x1, blocking collectives, body(): lax.all_gather(first_weight, 'dp', axis=3, tiled=True)[:, :, 0, :]  13.1 us
    all_gather x1, blocking collectives, body(): lax.all_gather(second_weight, 'dp', axis=3, tiled=True)[:, :, 0, :]  12.9 us
    conv_general_dilated x2, matrix products, spatial_conv(): lax.conv_general_dilated(padded, kernel, (1, 1, 1), [(0, 0), (1, 1), (1,...  12.1 us
    ppermute x2, waiting for transfers between devices, padded_2(): after = lax.ppermute(first, axis, down)  12 us
    all_gather x1, blocking collectives, upsample_block(): columns = lax.all_gather(up_weight, 'dp', axis=3, tiled=True)[:, :, 0, :]  8.97 us
    ppermute x2, waiting for transfers between devices, padded_2(): before = lax.ppermute(last, axis, up)  7.41 us
  transfers between devices with their start and end apart: 8, of which 6 were waited for; matrix products, arithmetic and copies ran while one was open for 8% of the time, Pallas kernels for 0%

commit v1 on v0

--- a/solution.py
+++ b/solution.py
@@ -85,9 +85,122 @@
     return (second + second_bias).astype(jnp.bfloat16)
 
 
+def swapped(array, axis):
+    return lax.ppermute(array, axis, [(0, 1), (1, 0)])
+
+
+def ordered(index, own, other, axis=0):
+    first = jnp.where(index == 0, own, other)
+    second = jnp.where(index == 0, other, own)
+    return jnp.stack([first, second], axis=axis)
+
+
+def line_routes():
+    early, late = ([], [])
+    for s in range(4):
+        for d in range(2):
+            for c in range(2):
+                source = (s * 2 + d) * 2 + c
+                up_target = (c * 2 + d) * 2 + s % 2
+                skip_target = ((2 + c) * 2 + d) * 2 + s % 2
+                early.append((source, up_target if s < 2 else skip_target))
+                late.append((source, skip_target if s < 2 else up_target))
+    return early, late
+
+
+def conv_block(features, weight):
+    return lax.conv_general_dilated(
+        features[None],
+        weight,
+        (1, 1, 1),
+        [(1, 1), (1, 1), (1, 1)],
+        dimension_numbers=("NDHWC", "DHWOI", "NDHWC"),
+        preferred_element_type=jnp.float32,
+    )[0]
+
+
+def stationary(
+    coarse, skip, up_weight, up_bias, first_weight, first_bias, second_weight, second_bias
+):
+    s, d, c = (lax.axis_index(a) for a in ("space", "dp", "chan"))
+    group = ("space", "dp", "chan")
+    _, _, cx, cy, cin = coarse.shape
+    cz = 4
+    _, bx, fy, fz, half = skip.shape
+    fx = 4 * bx
+    cells = cx * cy
+    block = bx * fy * fz
+    taps = up_weight.shape[0]
+    kb = up_weight.shape[1]
+    own_n = up_weight.shape[3]
+    lanes = 128
+    up_rows = taps * own_n
+    first_own = first_weight[:, :, 0, :].transpose(0, 2, 1)
+    second_own = second_weight[:, :, 0, :]
+    first_other = swapped(first_own, "dp")
+    up_rows_own = up_weight[:, :, 0, :].transpose(0, 2, 1).reshape(up_rows, kb)
+    coarse_rows = coarse.reshape(cells, cin // kb, kb).transpose(1, 0, 2).reshape(-1, kb)
+    up_packet = jnp.concatenate([up_rows_own, coarse_rows], axis=0)
+    skip_rows = skip.reshape(block, half)
+    skip_packet = jnp.pad(skip_rows, ((0, up_packet.shape[0] - block), (0, 0)))
+    early_route, late_route = line_routes()
+    early = lax.ppermute(jnp.where(s < 2, up_packet, skip_packet), group, early_route)
+    late = lax.ppermute(jnp.where(s < 2, skip_packet, up_packet), group, late_route)
+    weights = []
+    for packet in (early, late):
+        own = packet[:up_rows]
+        other = swapped(own, "dp")
+        both = ordered(d, own.reshape(taps, own_n, kb), other.reshape(taps, own_n, kb), 1)
+        weights.append(both.reshape(taps, 2 * own_n, kb))
+    weights = jnp.stack(weights)
+    second_other = swapped(second_own, "dp")
+    slabs = jnp.stack([early[up_rows:], late[up_rows:]]).reshape(2, 2, 2, cells, kb)
+    mine = lax.dynamic_index_in_dim(slabs, c, 2, keepdims=False)
+    theirs = lax.dynamic_index_in_dim(slabs, 1 - c, 2, keepdims=False)
+    slabs = ordered(c, mine, swapped(theirs, "chan"), 1)
+    up = jnp.einsum("zwkmi,ktoi->zwmto", slabs, weights, preferred_element_type=jnp.float32)
+    up = up + jnp.where(c == s, up_bias, 0.0)
+    up = up.reshape(cz, cx, cy, 2, 2, 2, half).transpose(1, 3, 2, 4, 0, 5, 6)
+    up = up.reshape(fx * fy * fz, half)
+    blocks = jnp.stack([late[:block], early[:block]])
+    nothing = jnp.zeros_like(blocks)
+    placed = ordered(c, blocks, nothing, 1).reshape(fx * fy * fz, half)
+    part = jnp.where(s < 2, up, placed.astype(jnp.float32))
+    joined = (part + swapped(part, "chan")).astype(jnp.bfloat16)
+    joined = joined.reshape(fx, fy, fz, half)
+    first_kernel = jnp.concatenate([first_own, first_other], axis=1)
+    first = conv_block(joined, first_kernel.reshape(3, 3, 3, half, half))
+    bias = first_bias.reshape(2, own_n)
+    bias = jnp.where(d == 0, bias.reshape(-1), bias[::-1].reshape(-1))
+    first = (first + jnp.where(s == 0, bias, 0.0)).astype(jnp.bfloat16)
+    first = first.reshape(2, 2, block, 2, own_n).transpose(0, 3, 2, 1, 4)
+    first = first.reshape(2, 2, block, half)
+    mine = lax.dynamic_index_in_dim(first, c, 0, keepdims=False)
+    theirs = lax.dynamic_index_in_dim(first, 1 - c, 0, keepdims=False)
+    chunks = ordered(c, mine, swapped(theirs, "chan"), 0)
+    chunks = ordered(d, chunks[:, 0], chunks[:, 1], 1).reshape(4, block, half)
+    terms = lax.all_to_all(chunks, "space", split_axis=0, concat_axis=0, tiled=True)
+    hidden = jax.nn.silu(jnp.sum(terms.astype(jnp.float32), axis=0)).astype(jnp.bfloat16)
+    hidden = ordered(c, hidden, swapped(hidden, "chan"), 0)
+    hidden = hidden.reshape(2, block, 2, own_n).transpose(0, 2, 1, 3)
+    hidden = hidden.reshape(fx, fy, fz, own_n)
+    second_kernel = jnp.concatenate([second_own, second_other], axis=2).transpose(0, 2, 1)
+    second = conv_block(hidden, second_kernel.reshape(3, 3, 3, half, own_n))
+    second = second.astype(jnp.bfloat16).reshape(4, block, half)
+    terms = lax.all_to_all(second, "space", split_axis=0, concat_axis=0, tiled=True)
+    total = jnp.sum(terms.astype(jnp.float32), axis=0)
+    total = jnp.where(d == 0, total, jnp.roll(total, own_n, axis=1))
+    return (total + second_bias).astype(jnp.bfloat16).reshape(skip.shape)
+
+
+def keeps_weights(mesh):
+    sizes = tuple(mesh.shape[a] for a in ("space", "dp", "chan"))
+    return sizes == (4, 2, 2)
+
+
 def solution(mesh):
     return jax.shard_map(
-        body,
+        stationary if keeps_weights(mesh) else body,
         mesh=mesh,
         in_specs=(
             P(("groups", "dp"), "space", None, None, None),

time: 175 us -> 71.8 us (0.41)
  waiting for transfers between devices: 88.8 us -> 25.8 us
  blocking collectives: 40.6 us -> 12.6 us
  between operations: 13.2 us -> 0.33 us
  matrix products: 13.8 us -> 10.1 us
  other arithmetic: 0.8 us -> 4.35 us
  starting transfers between devices: 13.1 us -> 15.5 us
    all_gather x3 -> x0, waiting for transfers between devices: 69.4 us -> none  [the longest x1 50.7 us: body(): lax.all_gather(first_columns, 'space', axis=1, tiled=True)]
    all_gather x6 -> x0, blocking collectives: 40.6 us -> none  [the longest x1 13.1 us: body(): lax.all_gather(first_weight, 'dp', axis=3, tiled=True)[:, :, 0, :]]
    all_to_all x0 -> x1, blocking collectives: none -> 12.6 us  [stationary(): lax.all_to_all(second, 'space', split_axis=0, concat_axis=0, tiled=True)]
    all_to_all x1, waiting for transfers between devices: 0.01 us -> 7.89 us  [stationary(): lax.all_to_all(chunks, 'space', split_axis=0, concat_axis=0, tiled=True)]
    ppermute x4 -> x10, starting transfers between devices: 7.53 us -> 11.9 us  [the longest x8 7.16 us: swapped(): return lax.ppermute(array, axis, [(0, 1), (1, 0)])]
    conv_general_dilated x2, matrix products: 12.1 us -> 9.79 us  [conv_block(): lax.conv_general_dilated(features[None], weight, (1, 1, 1), [(1, 1), (1,...]
    all_to_all x1, starting transfers between devices: 5.56 us -> 3.58 us  [stationary(): lax.all_to_all(chunks, 'space', split_axis=0, concat_axis=0, tiled=True)]
    select_n x0 -> x8, other arithmetic: none -> 1.9 us  [the longest x1 1.01 us: stationary(): jnp.where(s < 2, up_packet, skip_packet)]
  transfers between devices with their start and end apart: 8 -> 11, of which waited for: 6 -> 7; matrix products, arithmetic and copies ran while one was open for 8% -> 3% of each run, Pallas kernels for 0% -> 0%
where the time goes in v1:
time: 71.8 us; the launch traced here: 71.5 us
  waiting for transfers between devices  25.8 us (36%)
  starting transfers between devices  15.5 us (22%)
  blocking collectives  12.6 us (18%)
  matrix products  10.1 us (14%)
  other arithmetic  4.35 us (6%)
  local copies, waits for them, and re-layouts  2.84 us (4%)
    all_to_all x1, blocking collectives, stationary(): lax.all_to_all(second, 'space', split_axis=0, concat_axis=0, tiled=True)  12.6 us
    ppermute x8, waiting for transfers between devices, swapped(): return lax.ppermute(array, axis, [(0, 1), (1, 0)])  12 us
    conv_general_dilated x2, matrix products, conv_block(): lax.conv_general_dilated(features[None], weight, (1, 1, 1), [(1, 1), (1,...  9.79 us
    all_to_all x1, waiting for transfers between devices, stationary(): lax.all_to_all(chunks, 'space', split_axis=0, concat_axis=0, tiled=True)  7.89 us
    ppermute x8, starting transfers between devices, swapped(): return lax.ppermute(array, axis, [(0, 1), (1, 0)])  7.16 us
    ppermute x1, waiting for transfers between devices, stationary(): lax.ppermute(jnp.where(s < 2, skip_packet, up_packet), group, late_route)  5.85 us
    ppermute x1, starting transfers between devices, stationary(): lax.ppermute(jnp.where(s < 2, skip_packet, up_packet), group, late_route)  4.1 us
    all_to_all x1, starting transfers between devices, stationary(): lax.all_to_all(chunks, 'space', split_axis=0, concat_axis=0, tiled=True)  3.58 us
  transfers between devices with their start and end apart: 11, of which 7 were waited for; matrix products, arithmetic and copies ran while one was open for 3% of the time, Pallas kernels for 0%

profile of v1, /device:TPU:0, one launch (start us, length us, event | category | flops | bytes accessed | tf_op | source)
XLA Modules:
  0.0 71.5 jit_solution(1625862388693715160)
XLA Ops:
  0.0 0.8 %reshape.250 = bf16[32,4,128]{2,1,0:T(4,128)(2,1)S(1)} reshape(bf16[1,1,4,8,512]{4,3,2,1,0:T(8,128)(2,1)} %param.8) | data formatting | bytes 65536 | tf_op jit(solution)/shard_map/reshape | solution.py:142
  0.8 1.0 %pad_select_fusion.1 = (bf16[640,128]{1,0:T(8,128)(2,1)S(1)}, bf16[640,128]{1,0:T(8,128)(2,1)S(1)}) fusion(bf16[256,128]{1,0:T(8,128)(2,1)} %bitcast.136, pred[]{:T(512)S(6)} %lt.15, bf16[128,128]{1,0:T(8,128)(2,1)S(1)} %bitcast.135, bf16[512,128]{1,0:T(8,128)(2,1)} %bitcast.134), kind=kLoop, calls=%fused_computation.24 | loop fusion | flops 491520 | bytes 557057 | tf_op jit(solution)/shard_map/jit(_where)/select_n | solution.py:147
  1.8 0.7 collective-permute-start
  2.5 4.1 %collective-permute-start.1 = (bf16[640,128]{1,0:T(8,128)(2,1)S(1)}, bf16[640,128]{1,0:T(8,128)(2,1)S(1)}, u32[]{:S(2)}, u32[]{:S(2)}) collective-permute-start(bf16[640,128]{1,0:T(8,128)(2,1)S(1)} %get-tuple-element.14), channel_id=1, source_target_pairs={{0,8},{1,12},{2,10},{3,14},{4,9},{5,13},{6,11},{7,15},{8,0},{9,4},... | collective-permute-start | bytes 491528 | tf_op jit(solution)/shard_map/ppermute | solution.py:148
  6.6 1.5 %collective-permute-start.6 = (bf16[27,64,128]{2,1,0:T(8,128)(2,1)}, bf16[27,64,128]{2,1,0:T(8,128)(2,1)S(1)}, u32[]{:S(2)}, u32[]{:S(2)}) collective-permute-start(bf16[27,64,128]{2,1,0:T(8,128)(2,1)} %bitcast.121), channel_id=1, source_target_pairs={{0,2},{2,0},{1,3},{3,1},{4,6},{6,4},{5,7},{7,5},{8,10},{10,8},{9,1... | collective-permute-start | bytes 1327112 | tf_op jit(solution)/shard_map/ppermute | solution.py:89
  8.1 0.7 broadcast_select_fusion.12
  8.7 0.0 collective-permute-done
  8.7 5.9 %collective-permute-done.1 = bf16[640,128]{1,0:T(8,128)(2,1)S(1)} collective-permute-done((bf16[640,128]{1,0:T(8,128)(2,1)S(1)}, bf16[640,128]{1,0:T(8,128)(2,1)S(1)}, u32[]{:S(2)}, u32[]{:S(2)}) %collective-permute-start.1) | collective-permute-done | bytes 163872 | tf_op jit(solution)/shard_map/ppermute | solution.py:148
  14.6 0.1 collective-permute-start.2
  14.7 2.0 %collective-permute-start.3 = (bf16[512,128]{1,0:T(8,128)(2,1)S(1)}, bf16[512,128]{1,0:T(8,128)(2,1)S(1)}, u32[]{:S(2)}, u32[]{:S(2)}) collective-permute-start(bf16[512,128]{1,0:T(8,128)(2,1)S(1)} %slice.44), channel_id=1, source_target_pairs={{0,2},{2,0},{1,3},{3,1},{4,6},{6,4},{5,7},{7,5},{8,10},{10,8},{9,1... | collective-permute-start | bytes 393224 | tf_op jit(solution)/shard_map/ppermute | solution.py:89
  16.8 0.1 collective-permute-start.4
  17.0 0.0 collective-permute-done.2
  17.0 4.2 %collective-permute-done.3 = bf16[512,128]{1,0:T(8,128)(2,1)S(1)} collective-permute-done((bf16[512,128]{1,0:T(8,128)(2,1)S(1)}, bf16[512,128]{1,0:T(8,128)(2,1)S(1)}, u32[]{:S(2)}, u32[]{:S(2)}) %collective-permute-start.3) | collective-permute-done | bytes 131104 | tf_op jit(solution)/shard_map/ppermute | solution.py:89
  21.2 2.8 %collective-permute-done.4 = bf16[512,128]{1,0:T(8,128)(2,1)S(1)} collective-permute-done((bf16[512,128]{1,0:T(8,128)(2,1)S(1)}, bf16[512,128]{1,0:T(8,128)(2,1)S(1)}, u32[]{:S(2)}, u32[]{:S(2)}) %collective-permute-start.4) | collective-permute-done | bytes 131104 | tf_op jit(solution)/shard_map/ppermute | solution.py:89
  24.0 0.1 broadcast_select_fusion.3
  24.1 0.3 fusion
  24.4 0.0 copy-start.3
  24.5 0.0 copy-start
  24.5 0.4 copy.17
  24.9 0.1 convert_select_fusion
  24.9 1.4 %collective-permute-start.5 = (f32[1024,128]{1,0:T(8,128)S(1)}, f32[1024,128]{1,0:T(8,128)S(1)}, u32[]{:S(2)}, u32[]{:S(2)}) collective-permute-start(f32[1024,128]{1,0:T(8,128)S(1)} %convert_select_fusion), channel_id=1, source_target_pairs={{0,1},{1,0},{2,3},{3,2},{4,5},{5,4},{6,7},{7,6},{8,9},{9,8},{10,11... | collective-permute-start | bytes 1572872 | tf_op jit(solution)/shard_map/ppermute | solution.py:89
  26.3 0.1 reshape.256
  26.4 0.1 reshape.257
  26.5 0.1 add.59
  26.6 0.1 pad_maximum_fusion
  26.7 1.2 %collective-permute-done.5 = f32[1024,128]{1,0:T(8,128)S(1)} collective-permute-done((f32[1024,128]{1,0:T(8,128)S(1)}, f32[1024,128]{1,0:T(8,128)S(1)}, u32[]{:S(2)}, u32[]{:S(2)}) %collective-permute-start.5) | collective-permute-done | bytes 524320 | tf_op jit(solution)/shard_map/ppermute | solution.py:89
  27.8 0.1 add_convert_fusion.1
  27.9 6.1 %convolution_reduce_fusion = f32[8,16,8,128]{3,2,1,0:T(8,128)S(1)} fusion(bf16[3,3,3,128,128]{4,3,2,1,0:T(8,128)(2,1)S(1)} %bitcast.114, bf16[1,8,16,8,128]{4,3,2,1,0:T(8,128)(2,1)S(1)} %bitcast.130), kind=kOutput, calls=%fused_computation.1 | convolution fusion | flops 729546752 | bytes 1671168 | tf_op jit(solution)/shard_map/conv_general_dilated | solution.py:112
  34.0 0.6 squeeze.33
  34.7 0.4 fusion.1
  35.0 0.4 copy.19
  35.4 0.0 copy-start.1
  35.5 0.4 collective-permute-start.7
  35.9 1.0 %collective-permute-done.7 = bf16[2,256,128]{1,2,0:T(8,128)(2,1)S(1)} collective-permute-done((bf16[2,256,128]{1,2,0:T(8,128)(2,1)S(1)}, bf16[2,256,128]{1,2,0:T(8,128)(2,1)S(1)}, u32[]{:S(2)}, u32[]{:S(2)}) %collective-permute-start.7) | collective-permute-done | bytes 131104 | tf_op jit(solution)/shard_map/ppermute | solution.py:89
  36.9 0.7 %pad_maximum_fusion.5 = bf16[2,2,256,128]{2,3,1,0:T(8,128)(2,1)} fusion(bf16[2,1,256,128]{2,3,1,0:T(8,128)(2,1)S(1)} %get-tuple-element.12, bf16[2,1,256,128]{2,3,1,0:T(8,128)(2,1)S(1)} %get-tuple-element.11), kind=kLoop, calls=%fused_computation.22 | loop fusion | flops 131072 | bytes 524288 | tf_op jit(solution)/shard_map/stack | solution.py:95
  37.7 3.6 %all-to-all-start = ((bf16[4,256,128]{1,2,0:T(8,128)(2,1)}), bf16[4,256,128]{1,2,0:T(8,128)(2,1)S(1)}, u32[]{:S(2)}, u32[]{:S(2)}) async-start(bf16[4,256,128]{1,2,0:T(8,128)(2,1)} %bitcast.46), calls=%async_computation | async-start | bytes 524288 | tf_op jit(solution)/shard_map/all_to_all | solution.py:182
  41.3 1.6 %collective-permute-start.9 = (bf16[27,64,64]{2,1,0:T(8,128)(2,1)S(1)}, bf16[27,64,64]{2,1,0:T(8,128)(2,1)S(1)}, u32[]{:S(2)}, u32[]{:S(2)}) collective-permute-start(bf16[27,64,64]{2,1,0:T(8,128)(2,1)S(1)} %bitcast.123), channel_id=1, source_target_pairs={{0,2},{2,0},{1,3},{3,1},{4,6},{6,4},{5,7},{7,5},{8,10},{10,8},{9,1... | collective-permute-start | bytes 663560 | tf_op jit(solution)/shard_map/ppermute | solution.py:89
  42.8 7.9 %all-to-all-done = bf16[4,256,128]{1,2,0:T(8,128)(2,1)S(1)} async-done(((bf16[4,256,128]{1,2,0:T(8,128)(2,1)}), bf16[4,256,128]{1,2,0:T(8,128)(2,1)S(1)}, u32[]{:S(2)}, u32[]{:S(2)}) %all-to-all-start) | async-done | bytes 262176 | tf_op jit(solution)/shard_map/all_to_all | solution.py:182
  50.8 0.1 collective-permute-start.8
  50.9 2.9 %collective-permute-done.9 = bf16[27,64,64]{2,1,0:T(8,128)(2,1)S(1)} collective-permute-done((bf16[27,64,64]{2,1,0:T(8,128)(2,1)S(1)}, bf16[27,64,64]{2,1,0:T(8,128)(2,1)S(1)}, u32[]{:S(2)}, u32[]{:S(2)}) %collective-permute-start.9) | collective-permute-done | bytes 221216 | tf_op jit(solution)/shard_map/ppermute | solution.py:89
  53.8 0.2 pad_maximum_fusion.1
  54.0 0.1 broadcast_select_fusion.9
  54.1 0.2 copy.20
  54.3 3.7 %convolution_convert_fusion = bf16[1,8,16,8,128]{4,0,3,2,1:T(2,128)(2,1)S(1)} fusion(bf16[3,3,3,128,64]{3,4,2,1,0:T(8,128)(2,1)S(1)} %bitcast.125, bf16[1,8,16,8,64]{4,3,2,1,0:T(8,128)(2,1)S(1)} %bitcast.131), kind=kOutput, calls=%fused_computation.2 | convolution fusion | flops 364904448 | bytes 835584 | tf_op jit(solution)/shard_map/conv_general_dilated | solution.py:112
  58.0 0.0 copy-start.2
  58.0 12.6 %all_to_all.10 = bf16[4,256,128]{2,1,0:T(8,128)(2,1)S(1)} all-to-all(bf16[4,256,128]{2,1,0:T(8,128)(2,1)S(1)} %bitcast.109), channel_id=1, replica_groups=mesh['groups'=2,'space'=4,'dp'=2,'chan'=2] {'space'}, dimensions={0} | all-to-all | bytes 524288 | tf_op jit(solution)/shard_map/all_to_all | solution.py:190
  70.7 0.1 fusion.18
  70.8 0.7 %fusion.8 = bf16[1,2,16,8,128]{4,3,2,1,0:T(8,128)(2,1)} fusion(f32[1,2,16,8,128]{4,3,2,1,0:T(8,128)S(1)} %bitcast.107, f32[1,2,16,8,64]{4,3,2,1,0:T(8,128)S(1)} %bitcast.116, f32[1,2,16,8,64]{4,3,2,1,0:T(8,128)S(1)} %bitcast.115, f32[128]{0:T(128)S(1)} %copy-done.2, pred[]{:T(512)S(6)} %eq.8), kind=kLoop, calls=%fused_computation.32 | loop fusion | flops 131072 | bytes 328193 | tf_op jit(solution)/shard_map/convert_element_type | solution.py:193
  (29 shorter events, 0.5 us)
Async XLA Ops:
  1.8 6.9 %collective-permute-start = (bf16[640,128]{1,0:T(8,128)(2,1)S(1)}, bf16[640,128]{1,0:T(8,128)(2,1)S(1)}, u32[]{:S(2)}, u32[]{:S(2)}) collective-permute-start(bf16[640,128]{1,0:T(8,128)(2,1)S(1)} %get-tuple-element.13), channel_id=1, source_target_pairs={{0,0},{1,4},{2,2},{3,6},{4,1},{5,5},{6,3},{7,7},{8,8},{9,12},{10,1... | collective-permute-start | bytes 491528 | tf_op jit(solution)/shard_map/ppermute | solution.py:147
  2.5 12.1 %collective-permute-start.1 = (bf16[640,128]{1,0:T(8,128)(2,1)S(1)}, bf16[640,128]{1,0:T(8,128)(2,1)S(1)}, u32[]{:S(2)}, u32[]{:S(2)}) collective-permute-start(bf16[640,128]{1,0:T(8,128)(2,1)S(1)} %get-tuple-element.14), channel_id=1, source_target_pairs={{0,8},{1,12},{2,10},{3,14},{4,9},{5,13},{6,11},{7,15},{8,0},{9,4},... | collective-permute-start | bytes 491528 | tf_op jit(solution)/shard_map/ppermute | solution.py:148
  6.6 20.0 %collective-permute-start.6 = (bf16[27,64,128]{2,1,0:T(8,128)(2,1)}, bf16[27,64,128]{2,1,0:T(8,128)(2,1)S(1)}, u32[]{:S(2)}, u32[]{:S(2)}) collective-permute-start(bf16[27,64,128]{2,1,0:T(8,128)(2,1)} %bitcast.121), channel_id=1, source_target_pairs={{0,2},{2,0},{1,3},{3,1},{4,6},{6,4},{5,7},{7,5},{8,10},{10,8},{9,1... | collective-permute-start | bytes 1327112 | tf_op jit(solution)/shard_map/ppermute | solution.py:89
  14.6 2.4 %collective-permute-start.2 = (bf16[2,2,32,128]{3,2,1,0:T(8,128)(2,1)S(1)}, bf16[2,2,32,128]{3,2,1,0:T(8,128)(2,1)S(1)}, u32[]{:S(2)}, u32[]{:S(2)}) collective-permute-start(bf16[2,2,32,128]{3,2,1,0:T(8,128)(2,1)S(1)} %fusion.14), channel_id=1, source_target_pairs={{0,1},{1,0},{2,3},{3,2},{4,5},{5,4},{6,7},{7,6},{8,9},{9,8},{10,11... | collective-permute-start | bytes 98312 | tf_op jit(solution)/shard_map/ppermute | solution.py:89
  14.7 6.5 %collective-permute-start.3 = (bf16[512,128]{1,0:T(8,128)(2,1)S(1)}, bf16[512,128]{1,0:T(8,128)(2,1)S(1)}, u32[]{:S(2)}, u32[]{:S(2)}) collective-permute-start(bf16[512,128]{1,0:T(8,128)(2,1)S(1)} %slice.44), channel_id=1, source_target_pairs={{0,2},{2,0},{1,3},{3,1},{4,6},{6,4},{5,7},{7,5},{8,10},{10,8},{9,1... | collective-permute-start | bytes 393224 | tf_op jit(solution)/shard_map/ppermute | solution.py:89
  16.8 7.2 %collective-permute-start.4 = (bf16[512,128]{1,0:T(8,128)(2,1)S(1)}, bf16[512,128]{1,0:T(8,128)(2,1)S(1)}, u32[]{:S(2)}, u32[]{:S(2)}) collective-permute-start(bf16[512,128]{1,0:T(8,128)(2,1)S(1)} %slice.45), channel_id=1, source_target_pairs={{0,2},{2,0},{1,3},{3,1},{4,6},{6,4},{5,7},{7,5},{8,10},{10,8},{9,1... | collective-permute-start | bytes 393224 | tf_op jit(solution)/shard_map/ppermute | solution.py:89
  24.4 1.9 %copy-start.3 = (f32[128]{0:T(128)S(1)}, f32[128]{0:T(128)}, u32[]{:S(2)}) copy-start(f32[128]{0:T(128)} %param.13) | copy-start | bytes 1540
  24.5 2.1 %copy-start = (bf16[27,128,1,64]{1,3,2,0:T(8,128)(2,1)S(1)}, bf16[27,128,1,64]{1,3,2,0:T(8,128)(2,1)}, u32[]{:S(2)}) copy-start(bf16[27,128,1,64]{1,3,2,0:T(8,128)(2,1)} %param.12) | copy-start | bytes 1327108
  24.9 2.9 %collective-permute-start.5 = (f32[1024,128]{1,0:T(8,128)S(1)}, f32[1024,128]{1,0:T(8,128)S(1)}, u32[]{:S(2)}, u32[]{:S(2)}) collective-permute-start(f32[1024,128]{1,0:T(8,128)S(1)} %convert_select_fusion), channel_id=1, source_target_pairs={{0,1},{1,0},{2,3},{3,2},{4,5},{5,4},{6,7},{7,6},{8,9},{9,8},{10,11... | collective-permute-start | bytes 1572872 | tf_op jit(solution)/shard_map/ppermute | solution.py:89
  35.4 5.8 %copy-start.1 = (bf16[27,64,1,64]{3,1,2,0:T(8,128)(2,1)S(1)}, bf16[27,64,1,64]{3,1,2,0:T(8,128)(2,1)}, u32[]{:S(2)}) copy-start(bf16[27,64,1,64]{3,1,2,0:T(8,128)(2,1)} %param.14) | copy-start | bytes 663556
  35.5 1.4 %collective-permute-start.7 = (bf16[2,256,128]{1,2,0:T(8,128)(2,1)S(1)}, bf16[2,256,128]{1,2,0:T(8,128)(2,1)S(1)}, u32[]{:S(2)}, u32[]{:S(2)}) collective-permute-start(bf16[2,256,128]{1,2,0:T(8,128)(2,1)S(1)} %dynamic-slice_bitcast_fusion), channel_id=1, source_target_pairs={{0,1},{1,0},{2,3},{3,2},{4,5},{5,4},{6,7},{7,6},{8,9},{9,8},{10,11... | collective-permute-start | bytes 393224 | tf_op jit(solution)/shard_map/ppermute | solution.py:89
  37.7 13.1 %all-to-all-start = ((bf16[4,256,128]{1,2,0:T(8,128)(2,1)}), bf16[4,256,128]{1,2,0:T(8,128)(2,1)S(1)}, u32[]{:S(2)}, u32[]{:S(2)}) async-start(bf16[4,256,128]{1,2,0:T(8,128)(2,1)} %bitcast.46), calls=%async_computation | async-start | bytes 524288 | tf_op jit(solution)/shard_map/all_to_all | solution.py:182
  41.3 12.5 %collective-permute-start.9 = (bf16[27,64,64]{2,1,0:T(8,128)(2,1)S(1)}, bf16[27,64,64]{2,1,0:T(8,128)(2,1)S(1)}, u32[]{:S(2)}, u32[]{:S(2)}) collective-permute-start(bf16[27,64,64]{2,1,0:T(8,128)(2,1)S(1)} %bitcast.123), channel_id=1, source_target_pairs={{0,2},{2,0},{1,3},{3,1},{4,6},{6,4},{5,7},{7,5},{8,10},{10,8},{9,1... | collective-permute-start | bytes 663560 | tf_op jit(solution)/shard_map/ppermute | solution.py:89
  50.8 3.2 %collective-permute-start.8 = (bf16[256,128]{0,1:T(8,128)(2,1)S(1)}, bf16[256,128]{0,1:T(8,128)(2,1)S(1)}, u32[]{:S(2)}, u32[]{:S(2)}) collective-permute-start(bf16[256,128]{0,1:T(8,128)(2,1)S(1)} %multiply_convert_fusion), channel_id=1, source_target_pairs={{0,1},{1,0},{2,3},{3,2},{4,5},{5,4},{6,7},{7,6},{8,9},{9,8},{10,11... | collective-permute-start | bytes 196616 | tf_op jit(solution)/shard_map/ppermute | solution.py:89
  58.0 12.8 %copy-start.2 = (f32[128]{0:T(128)S(1)}, f32[128]{0:T(128)}, u32[]{:S(2)}) copy-start(f32[128]{0:T(128)} %param.15) | copy-start | bytes 1540

commit v2 on v1

--- a/solution.py
+++ b/solution.py
@@ -1,6 +1,8 @@
 import jax
 import jax.numpy as jnp
 from jax import lax
+from jax.experimental import pallas as pl
+from jax.experimental.pallas import tpu as pltpu
 from jax.sharding import PartitionSpec as P
 
 
@@ -108,15 +110,142 @@
     return early, late
 
 
-def conv_block(features, weight):
-    return lax.conv_general_dilated(
-        features[None],
-        weight,
-        (1, 1, 1),
-        [(1, 1), (1, 1), (1, 1)],
-        dimension_numbers=("NDHWC", "DHWOI", "NDHWC"),
-        preferred_element_type=jnp.float32,
-    )[0]
+NT = (((1,), (1,)), ((), ()))
+NN = (((1,), (0,)), ((), ()))
+
+
+def first_kernel(mine, theirs, own, other, bias, out, even, odd):
+    planes = even.shape[0] - 2
+    rows, width = even.shape[1:]
+    half = mine.shape[1]
+    quad = planes // 4
+    blank = jnp.zeros((1,) + odd.shape[1:], odd.dtype)
+    odd[0:1] = blank
+    odd[planes + 1 : planes + 2] = blank
+    even[0:1] = blank[:, :rows]
+    even[planes + 1 : planes + 2] = blank[:, :rows]
+    cell = lax.broadcasted_iota(jnp.int32, (rows, half), 0) % 8
+    edge = jnp.zeros((8, width), jnp.float32)
+    for x in range(planes):
+        plane = mine[x * rows : (x + 1) * rows] + theirs[x * rows : (x + 1) * rows]
+        plane = plane.astype(jnp.bfloat16).astype(jnp.float32)
+        below = jnp.where(cell == 0, 0.0, pltpu.roll(plane, 1, 0))
+        above = jnp.where(cell == 7, 0.0, pltpu.roll(plane, rows - 1, 0))
+        taps = jnp.concatenate([below, plane, above], axis=1)
+        even[x + 1] = taps.astype(jnp.bfloat16)
+        odd[x + 1] = jnp.concatenate([edge, taps, edge], axis=0).astype(jnp.bfloat16)
+    lane = lax.broadcasted_iota(jnp.int32, (2 * quad * rows, half), 1)
+    for q in range(2):
+        total = jnp.broadcast_to(bias[...], (4 * quad * rows // 2, half))
+        total = None
+        for dx in range(3):
+            for dy in range(3):
+                at = pl.ds(q * 2 * quad + dx, 2 * quad)
+                if dy == 1:
+                    left = even[at]
+                else:
+                    left = odd[at, pl.ds(8 * dy, rows)]
+                left = left.reshape(2 * quad * rows, width)
+                tap = (dx * 3 + dy) * 3
+                right = jnp.concatenate(
+                    [jnp.concatenate([own[tap + dz], other[tap + dz]], axis=0) for dz in range(3)],
+                    axis=1,
+                )
+                term = lax.dot_general(left, right, NT, preferred_element_type=jnp.float32)
+                total = term if total is None else total + term
+        total = total + bias[...]
+        low, high = (total[: quad * rows], total[quad * rows :])
+        lane = lax.broadcasted_iota(jnp.int32, low.shape, 1)
+        swap = half // 2
+        out[q, 0] = jnp.where(lane < swap, low, pltpu.roll(high, swap, 1)).astype(jnp.bfloat16)
+        out[q, 1] = jnp.where(lane < swap, pltpu.roll(low, swap, 1), high).astype(jnp.bfloat16)
+
+
+def first_conv(mine, theirs, own, other, bias, planes, fz):
+    cells, half = mine.shape
+    rows = cells // planes
+    return pl.pallas_call(
+        first_kernel,
+        out_shape=jax.ShapeDtypeStruct((2, 2, cells // 4, half), jnp.bfloat16),
+        in_specs=[pl.BlockSpec(memory_space=pltpu.VMEM)] * 5,
+        out_specs=pl.BlockSpec(memory_space=pltpu.VMEM),
+        scratch_shapes=[
+            pltpu.VMEM((planes + 2, rows, 3 * half), jnp.bfloat16),
+            pltpu.VMEM((planes + 2, rows + 16, 3 * half), jnp.bfloat16),
+        ],
+        compiler_params=pltpu.CompilerParams(vmem_limit_bytes=32 * 2**20),
+    )(mine, theirs, own, other, bias)
+
+
+def second_kernel(hidden, own, other, out, even, odd):
+    planes = even.shape[0] - 2
+    rows, width = even.shape[1:]
+    lanes = hidden.shape[2]
+    k = lanes // 2
+    swap = lanes // 2
+    d = lax.axis_index("dp")
+    blank = jnp.zeros((1,) + odd.shape[1:], odd.dtype)
+    odd[0:1] = blank
+    odd[planes + 1 : planes + 2] = blank
+    even[0:1] = blank[:, :rows]
+    even[planes + 1 : planes + 2] = blank[:, :rows]
+    cell = lax.broadcasted_iota(jnp.int32, (rows, lanes), 0) % 8
+    lane = lax.broadcasted_iota(jnp.int32, (rows, lanes), 1)
+    low = lane < swap
+    edge = jnp.zeros((8, width), jnp.float32)
+    per = hidden.shape[1] // rows
+    for q in range(2):
+        for r in range(per):
+            packed = hidden[q, r * rows : (r + 1) * rows].astype(jnp.float32)
+            turned = pltpu.roll(packed, swap, 1)
+            for u in range(2):
+                here, there = (packed, turned) if u == 0 else (turned, packed)
+                below = jnp.where(cell == 0, 0.0, pltpu.roll(here, 1, 0))
+                above = jnp.where(cell == 7, 0.0, pltpu.roll(here, rows - 1, 0))
+                taps = jnp.concatenate(
+                    [jnp.where(low, below, there), jnp.where(low, above, 0.0)], axis=1
+                )
+                x = (q * 2 + u) * per + r
+                even[x + 1] = taps.astype(jnp.bfloat16)
+                odd[x + 1] = jnp.concatenate([edge, taps, edge], axis=0).astype(jnp.bfloat16)
+    lane_w = lax.broadcasted_iota(jnp.int32, (3 * k, lanes), 1)
+    for q in range(2):
+        total = None
+        for dx in range(3):
+            for dy in range(3):
+                at = pl.ds(q * planes // 2 + dx, planes // 2)
+                if dy == 1:
+                    left = even[at]
+                else:
+                    left = odd[at, pl.ds(8 * dy, rows)]
+                left = left.reshape(planes // 2 * rows, width)[:, : 3 * k]
+                tap = (dx * 3 + dy) * 3
+                one = own[tap : tap + 3].reshape(3 * k, k)
+                two = other[tap : tap + 3].reshape(3 * k, k)
+                right = jnp.concatenate(
+                    [jnp.where(d == 0, one, two), jnp.where(d == 0, two, one)], axis=1
+                )
+                term = lax.dot_general(left, right, NN, preferred_element_type=jnp.float32)
+                total = term if total is None else total + term
+        n = planes // 2 * rows
+        out[q * n : (q + 1) * n] = total.astype(jnp.bfloat16)
+
+
+def second_conv(hidden, own, other, planes):
+    _, rows2, lanes = hidden.shape
+    cells = rows2 * 4
+    rows = cells // planes
+    return pl.pallas_call(
+        second_kernel,
+        out_shape=jax.ShapeDtypeStruct((cells, lanes), jnp.bfloat16),
+        in_specs=[pl.BlockSpec(memory_space=pltpu.VMEM)] * 3,
+        out_specs=pl.BlockSpec(memory_space=pltpu.VMEM),
+        scratch_shapes=[
+            pltpu.VMEM((planes + 2, rows, 2 * lanes), jnp.bfloat16),
+            pltpu.VMEM((planes + 2, rows + 16, 2 * lanes), jnp.bfloat16),
+        ],
+        compiler_params=pltpu.CompilerParams(vmem_limit_bytes=32 * 2**20),
+    )(hidden, own, other)
 
 
 def stationary(
@@ -166,15 +295,10 @@
     nothing = jnp.zeros_like(blocks)
     placed = ordered(c, blocks, nothing, 1).reshape(fx * fy * fz, half)
     part = jnp.where(s < 2, up, placed.astype(jnp.float32))
-    joined = (part + swapped(part, "chan")).astype(jnp.bfloat16)
-    joined = joined.reshape(fx, fy, fz, half)
-    first_kernel = jnp.concatenate([first_own, first_other], axis=1)
-    first = conv_block(joined, first_kernel.reshape(3, 3, 3, half, half))
     bias = first_bias.reshape(2, own_n)
     bias = jnp.where(d == 0, bias.reshape(-1), bias[::-1].reshape(-1))
-    first = (first + jnp.where(s == 0, bias, 0.0)).astype(jnp.bfloat16)
-    first = first.reshape(2, 2, block, 2, own_n).transpose(0, 3, 2, 1, 4)
-    first = first.reshape(2, 2, block, half)
+    bias = jnp.where(s == 0, bias, 0.0)[None]
+    first = first_conv(part, swapped(part, "chan"), first_own, first_other, bias, fx, fz)
     mine = lax.dynamic_index_in_dim(first, c, 0, keepdims=False)
     theirs = lax.dynamic_index_in_dim(first, 1 - c, 0, keepdims=False)
     chunks = ordered(c, mine, swapped(theirs, "chan"), 0)
@@ -182,14 +306,10 @@
     terms = lax.all_to_all(chunks, "space", split_axis=0, concat_axis=0, tiled=True)
     hidden = jax.nn.silu(jnp.sum(terms.astype(jnp.float32), axis=0)).astype(jnp.bfloat16)
     hidden = ordered(c, hidden, swapped(hidden, "chan"), 0)
-    hidden = hidden.reshape(2, block, 2, own_n).transpose(0, 2, 1, 3)
-    hidden = hidden.reshape(fx, fy, fz, own_n)
-    second_kernel = jnp.concatenate([second_own, second_other], axis=2).transpose(0, 2, 1)
-    second = conv_block(hidden, second_kernel.reshape(3, 3, 3, half, own_n))
-    second = second.astype(jnp.bfloat16).reshape(4, block, half)
+    second = second_conv(hidden, second_own, second_other, fx)
+    second = second.reshape(4, block, half)
     terms = lax.all_to_all(second, "space", split_axis=0, concat_axis=0, tiled=True)
     total = jnp.sum(terms.astype(jnp.float32), axis=0)
-    total = jnp.where(d == 0, total, jnp.roll(total, own_n, axis=1))
     return (total + second_bias).astype(jnp.bfloat16).reshape(skip.shape)
 
 

time: 71.8 us -> 80.7 us (1.12)
  blocking collectives: 12.6 us -> 23.6 us
  waiting for transfers between devices: 25.8 us -> 36.3 us
  matrix products: 10.1 us -> 0.31 us
  starting transfers between devices: 15.5 us -> 10.5 us
  Pallas kernels: 0 us -> 3.63 us
  other arithmetic: 4.35 us -> 2.07 us
  local copies, waits for them, and re-layouts: 2.84 us -> 3.74 us
    ppermute x8, waiting for transfers between devices: 12 us -> 29 us  [swapped(): return lax.ppermute(array, axis, [(0, 1), (1, 0)])]
    all_to_all x0 -> x1, blocking collectives: none -> 12.2 us  [stationary(): lax.all_to_all(chunks, 'space', split_axis=0, concat_axis=0, tiled=True)]
    conv_general_dilated x2 -> x0, matrix products: 9.79 us -> none  [conv_block(): lax.conv_general_dilated(features[None], weight, (1, 1, 1), [(1, 1), (1,...]
    all_to_all x1 -> x0, waiting for transfers between devices: 7.89 us -> none  [stationary(): lax.all_to_all(chunks, 'space', split_axis=0, concat_axis=0, tiled=True)]
    pallas_call x0 -> x2, Pallas kernels: none -> 3.63 us  [the longest x1 2.13 us: first_conv(): pl.pallas_call(first_kernel, out_shape=jax.ShapeDtypeStruct((2, 2, cells...]
    all_to_all x1 -> x0, starting transfers between devices: 3.58 us -> none  [stationary(): lax.all_to_all(chunks, 'space', split_axis=0, concat_axis=0, tiled=True)]
    unnamed x9 -> x12, local copies, waits for them, and re-layouts: 0.06 us -> 2.26 us
    ppermute x1, waiting for transfers between devices: 5.85 us -> 7.34 us  [stationary(): lax.ppermute(jnp.where(s < 2, skip_packet, up_packet), group, late_route)]
  transfers between devices with their start and end apart: 11 -> 10, of which waited for: 7 -> 6; matrix products, arithmetic and copies ran while one was open for 3% -> 0% of each run, Pallas kernels for 0% -> 0%
where the time goes in v2:
time: 80.7 us; the launch traced here: 80.4 us
  waiting for transfers between devices  36.3 us (45%)
  blocking collectives  23.6 us (29%)
  starting transfers between devices  10.5 us (13%)
  local copies, waits for them, and re-layouts  3.74 us (5%)
  Pallas kernels  3.63 us (4%)
  other arithmetic  2.07 us (3%)
    ppermute x8, waiting for transfers between devices, swapped(): return lax.ppermute(array, axis, [(0, 1), (1, 0)])  29 us
    all_to_all x1, blocking collectives, stationary(): lax.all_to_all(chunks, 'space', split_axis=0, concat_axis=0, tiled=True)  12.2 us
    all_to_all x1, blocking collectives, stationary(): lax.all_to_all(second, 'space', split_axis=0, concat_axis=0, tiled=True)  11.4 us
    ppermute x1, waiting for transfers between devices, stationary(): lax.ppermute(jnp.where(s < 2, skip_packet, up_packet), group, late_route)  7.34 us
    ppermute x8, starting transfers between devices, swapped(): return lax.ppermute(array, axis, [(0, 1), (1, 0)])  5.75 us
    ppermute x1, starting transfers between devices, stationary(): lax.ppermute(jnp.where(s < 2, skip_packet, up_packet), group, late_route)  4.1 us
    unnamed x12, local copies, waits for them, and re-layouts  2.26 us
    pallas_call x1, Pallas kernels, first_conv(): pl.pallas_call(first_kernel, out_shape=jax.ShapeDtypeStruct((2, 2, cells...  2.13 us
  transfers between devices with their start and end apart: 10, of which 6 were waited for; matrix products, arithmetic and copies ran while one was open for 0% of the time, Pallas kernels for 0%

profile of v2, /device:TPU:0, one launch (start us, length us, event | category | flops | bytes accessed | tf_op | source)
XLA Modules:
  0.0 80.4 jit_solution(4811645860278626547)
XLA Ops:
  0.0 0.0 copy-start.2
  0.0 0.8 %reshape.202 = bf16[32,4,128]{2,1,0:T(4,128)(2,1)S(1)} reshape(bf16[1,1,4,8,512]{4,3,2,1,0:T(8,128)(2,1)} %param.8) | data formatting | bytes 65536 | tf_op jit(solution)/shard_map/reshape | solution.py:271
  0.8 0.1 copy-done.2
  0.9 0.9 %pad_select_fusion.1 = (bf16[640,128]{1,0:T(8,128)(2,1)S(1)}, bf16[640,128]{1,0:T(8,128)(2,1)S(1)}) fusion(bf16[256,128]{1,0:T(8,128)(2,1)} %bitcast.118, pred[]{:T(512)S(6)} %lt.15, bf16[128,128]{1,0:T(8,128)(2,1)S(1)} %bitcast.116, bf16[512,128]{1,0:T(8,128)(2,1)S(1)} %bitcast.115), kind=kLoop, calls=%fused_computation.15 | loop fusion | flops 491520 | bytes 557057 | tf_op jit(solution)/shard_map/jit(_where)/select_n | solution.py:276
  1.8 0.7 collective-permute-start
  2.5 4.1 %collective-permute-start.1 = (bf16[640,128]{1,0:T(8,128)(2,1)S(1)}, bf16[640,128]{1,0:T(8,128)(2,1)S(1)}, u32[]{:S(2)}, u32[]{:S(2)}) collective-permute-start(bf16[640,128]{1,0:T(8,128)(2,1)S(1)} %get-tuple-element.14), channel_id=1, source_target_pairs={{0,8},{1,12},{2,10},{3,14},{4,9},{5,13},{6,11},{7,15},{8,0},{9,4},... | collective-permute-start | bytes 491528 | tf_op jit(solution)/shard_map/ppermute | solution.py:277
  6.6 0.0 copy-start.5
  6.6 0.7 copy-done.5
  7.3 0.0 collective-permute-done
  7.3 7.3 %collective-permute-done.1 = bf16[640,128]{1,0:T(8,128)(2,1)S(1)} collective-permute-done((bf16[640,128]{1,0:T(8,128)(2,1)S(1)}, bf16[640,128]{1,0:T(8,128)(2,1)S(1)}, u32[]{:S(2)}, u32[]{:S(2)}) %collective-permute-start.1) | collective-permute-done | bytes 163872 | tf_op jit(solution)/shard_map/ppermute | solution.py:277
  14.6 0.1 collective-permute-start.2
  14.7 2.0 %collective-permute-start.3 = (bf16[512,128]{1,0:T(8,128)(2,1)S(1)}, bf16[512,128]{1,0:T(8,128)(2,1)S(1)}, u32[]{:S(2)}, u32[]{:S(2)}) collective-permute-start(bf16[512,128]{1,0:T(8,128)(2,1)S(1)} %slice.34), channel_id=1, source_target_pairs={{0,2},{2,0},{1,3},{3,1},{4,6},{6,4},{5,7},{7,5},{8,10},{10,8},{9,1... | collective-permute-start | bytes 393224 | tf_op jit(solution)/shard_map/ppermute | solution.py:91
  16.8 0.1 collective-permute-start.4
  17.0 0.0 collective-permute-done.2
  17.0 4.1 %collective-permute-done.3 = bf16[512,128]{1,0:T(8,128)(2,1)S(1)} collective-permute-done((bf16[512,128]{1,0:T(8,128)(2,1)S(1)}, bf16[512,128]{1,0:T(8,128)(2,1)S(1)}, u32[]{:S(2)}, u32[]{:S(2)}) %collective-permute-start.3) | collective-permute-done | bytes 131104 | tf_op jit(solution)/shard_map/ppermute | solution.py:91
  21.2 2.6 %collective-permute-done.4 = bf16[512,128]{1,0:T(8,128)(2,1)S(1)} collective-permute-done((bf16[512,128]{1,0:T(8,128)(2,1)S(1)}, bf16[512,128]{1,0:T(8,128)(2,1)S(1)}, u32[]{:S(2)}, u32[]{:S(2)}) %collective-permute-start.4) | collective-permute-done | bytes 131104 | tf_op jit(solution)/shard_map/ppermute | solution.py:91
  23.7 0.1 broadcast_select_fusion.3
  23.9 0.3 fusion
  24.2 0.4 copy.17
  24.6 0.0 copy-start
  24.6 0.1 convert_select_fusion.mine
  24.7 0.1 collective-permute-start.5
  24.7 0.9 %copy-done = bf16[27,128,1,64]{1,3,2,0:T(8,128)(2,1)S(1)} copy-done((bf16[27,128,1,64]{1,3,2,0:T(8,128)(2,1)S(1)}, bf16[27,128,1,64]{1,3,2,0:T(8,128)(2,1)}, u32[]{:S(2)}) %copy-start) | copy-done | bytes 442392
  25.6 0.0 copy-start.4
  25.6 1.7 %collective-permute-start.6 = (bf16[27,64,128]{2,1,0:T(8,128)(2,1)S(1)}, bf16[27,64,128]{2,1,0:T(8,128)(2,1)S(1)}, u32[]{:S(2)}, u32[]{:S(2)}) collective-permute-start(bf16[27,64,128]{2,1,0:T(8,128)(2,1)S(1)} %bitcast.97), channel_id=1, source_target_pairs={{0,2},{2,0},{1,3},{3,1},{4,6},{6,4},{5,7},{7,5},{8,10},{10,8},{9,1... | collective-permute-start | bytes 1327112 | tf_op jit(solution)/shard_map/ppermute | solution.py:91
  27.3 0.0 copy-done.4
  27.3 0.1 reshape.207
  27.5 0.1 reshape.208
  27.6 10.0 %collective-permute-done.6.other = bf16[27,64,128]{2,1,0:T(8,128)(2,1)S(1)} collective-permute-done((bf16[27,64,128]{2,1,0:T(8,128)(2,1)S(1)}, bf16[27,64,128]{2,1,0:T(8,128)(2,1)S(1)}, u32[]{:S(2)}, u32[]{:S(2)}) %collective-permute-start.6) | collective-permute-done | bytes 442400 | tf_op jit(solution)/shard_map/ppermute | solution.py:91
  37.5 0.0 collective-permute-done.5.theirs
  37.6 2.1 %shard_map.82 = bf16[2,2,256,128]{3,2,1,0:T(8,128)(2,1)S(1)} custom-call(f32[1024,128]{1,0:T(8,128)S(1)} %convert_select_fusion.mine, f32[1024,128]{1,0:T(8,128)S(1)} %collective-permute-done.5.theirs, bf16[27,64,128]{2,1,0:T(8,128)(2,1)S(1)} %bitcast.98, bf16[27,64,128]{2,1,0:T(8,128)(2,1)S(1)} %collective-permute-done.6.other, f32[1,128]{1,0:T(1,128)S(1)} %fusion.12.bias), custom_call_target="tpu_custom_call" | custom-call | tf_op jit(solution)/shard_map/pallas_call | solution.py:167
  39.7 0.1 collective-permute-start.7
  39.8 1.3 %collective-permute-done.7 = bf16[2,256,128]{2,1,0:T(8,128)(2,1)S(1)} collective-permute-done((bf16[2,256,128]{2,1,0:T(8,128)(2,1)S(1)}, bf16[2,256,128]{2,1,0:T(8,128)(2,1)S(1)}, u32[]{:S(2)}, u32[]{:S(2)}) %collective-permute-start.7) | collective-permute-done | bytes 131104 | tf_op jit(solution)/shard_map/ppermute | solution.py:91
  41.2 0.0 copy-start.1
  41.2 12.2 %all_to_all.10 = bf16[4,256,128]{2,1,0:T(8,128)(2,1)S(1)} all-to-all(bf16[4,256,128]{2,1,0:T(8,128)(2,1)S(1)} %bitcast.103), channel_id=1, replica_groups=mesh['groups'=2,'space'=4,'dp'=2,'chan'=2] {'space'}, dimensions={0} | all-to-all | bytes 524288 | tf_op jit(solution)/shard_map/all_to_all | solution.py:306
  53.6 0.1 collective-permute-start.8
  53.6 0.0 copy-done.1
  53.6 1.6 %collective-permute-start.9 = (bf16[27,64,64]{2,1,0:T(8,128)(2,1)S(1)}, bf16[27,64,64]{2,1,0:T(8,128)(2,1)S(1)}, u32[]{:S(2)}, u32[]{:S(2)}) collective-permute-start(bf16[27,64,64]{2,1,0:T(8,128)(2,1)S(1)} %bitcast.99), channel_id=1, source_target_pairs={{0,2},{2,0},{1,3},{3,1},{4,6},{6,4},{5,7},{7,5},{8,10},{10,8},{9,1... | collective-permute-start | bytes 663560 | tf_op jit(solution)/shard_map/ppermute | solution.py:91
  55.2 0.0 collective-permute-done.8
  55.2 0.1 select_bitcast_fusion.1
  55.3 10.9 %collective-permute-done.9.other = bf16[27,64,64]{2,1,0:T(8,128)(2,1)S(1)} collective-permute-done((bf16[27,64,64]{2,1,0:T(8,128)(2,1)S(1)}, bf16[27,64,64]{2,1,0:T(8,128)(2,1)S(1)}, u32[]{:S(2)}, u32[]{:S(2)}) %collective-permute-start.9) | collective-permute-done | bytes 221216 | tf_op jit(solution)/shard_map/ppermute | solution.py:91
  66.2 1.5 %shard_map.83 = bf16[1024,128]{1,0:T(8,128)(2,1)S(1)} custom-call(bf16[2,256,128]{2,1,0:T(8,128)(2,1)S(1)} %pad_maximum_fusion.7.hidden, bf16[27,64,64]{2,1,0:T(8,128)(2,1)S(1)} %bitcast.100, bf16[27,64,64]{2,1,0:T(8,128)(2,1)S(1)} %collective-permute-done.9.other), custom_call_target="tpu_custom_call" | custom-call | tf_op jit(solution)/shard_map/pallas_call | solution.py:238
  67.7 11.4 %all_to_all.11 = bf16[4,256,128]{2,1,0:T(8,128)(2,1)S(1)} all-to-all(bf16[4,256,128]{2,1,0:T(8,128)(2,1)S(1)} %bitcast.96), channel_id=1, replica_groups=mesh['groups'=2,'space'=4,'dp'=2,'chan'=2] {'space'}, dimensions={0} | all-to-all | bytes 524288 | tf_op jit(solution)/shard_map/all_to_all | solution.py:311
  79.1 0.0 copy-start.3
  79.1 0.6 copy-done.3
  79.8 0.6 add_convert_fusion
  (24 shorter events, 0.4 us)
Async XLA Ops:
  0.0 0.9 %copy-start.2 = (bf16[8,128,1,64]{1,3,2,0:T(8,128)(2,1)S(1)}, bf16[8,128,1,64]{1,3,2,0:T(8,128)(2,1)}, u32[]{:S(2)}) copy-start(bf16[8,128,1,64]{1,3,2,0:T(8,128)(2,1)} %param.10) | copy-start | bytes 393220
  1.8 5.4 %collective-permute-start = (bf16[640,128]{1,0:T(8,128)(2,1)S(1)}, bf16[640,128]{1,0:T(8,128)(2,1)S(1)}, u32[]{:S(2)}, u32[]{:S(2)}) collective-permute-start(bf16[640,128]{1,0:T(8,128)(2,1)S(1)} %get-tuple-element.13), channel_id=1, source_target_pairs={{0,0},{1,4},{2,2},{3,6},{4,1},{5,5},{6,3},{7,7},{8,8},{9,12},{10,1... | collective-permute-start | bytes 491528 | tf_op jit(solution)/shard_map/ppermute | solution.py:276
  2.5 12.1 %collective-permute-start.1 = (bf16[640,128]{1,0:T(8,128)(2,1)S(1)}, bf16[640,128]{1,0:T(8,128)(2,1)S(1)}, u32[]{:S(2)}, u32[]{:S(2)}) collective-permute-start(bf16[640,128]{1,0:T(8,128)(2,1)S(1)} %get-tuple-element.14), channel_id=1, source_target_pairs={{0,8},{1,12},{2,10},{3,14},{4,9},{5,13},{6,11},{7,15},{8,0},{9,4},... | collective-permute-start | bytes 491528 | tf_op jit(solution)/shard_map/ppermute | solution.py:277
  6.6 0.7 copy-start.5
  14.6 2.4 %collective-permute-start.2 = (bf16[2,2,32,128]{3,2,1,0:T(8,128)(2,1)S(1)}, bf16[2,2,32,128]{3,2,1,0:T(8,128)(2,1)S(1)}, u32[]{:S(2)}, u32[]{:S(2)}) collective-permute-start(bf16[2,2,32,128]{3,2,1,0:T(8,128)(2,1)S(1)} %fusion.9), channel_id=1, source_target_pairs={{0,1},{1,0},{2,3},{3,2},{4,5},{5,4},{6,7},{7,6},{8,9},{9,8},{10,11... | collective-permute-start | bytes 98312 | tf_op jit(solution)/shard_map/ppermute | solution.py:91
  14.7 6.4 %collective-permute-start.3 = (bf16[512,128]{1,0:T(8,128)(2,1)S(1)}, bf16[512,128]{1,0:T(8,128)(2,1)S(1)}, u32[]{:S(2)}, u32[]{:S(2)}) collective-permute-start(bf16[512,128]{1,0:T(8,128)(2,1)S(1)} %slice.34), channel_id=1, source_target_pairs={{0,2},{2,0},{1,3},{3,1},{4,6},{6,4},{5,7},{7,5},{8,10},{10,8},{9,1... | collective-permute-start | bytes 393224 | tf_op jit(solution)/shard_map/ppermute | solution.py:91
  16.8 6.9 %collective-permute-start.4 = (bf16[512,128]{1,0:T(8,128)(2,1)S(1)}, bf16[512,128]{1,0:T(8,128)(2,1)S(1)}, u32[]{:S(2)}, u32[]{:S(2)}) collective-permute-start(bf16[512,128]{1,0:T(8,128)(2,1)S(1)} %slice.35), channel_id=1, source_target_pairs={{0,2},{2,0},{1,3},{3,1},{4,6},{6,4},{5,7},{7,5},{8,10},{10,8},{9,1... | collective-permute-start | bytes 393224 | tf_op jit(solution)/shard_map/ppermute | solution.py:91
  24.6 1.0 %copy-start = (bf16[27,128,1,64]{1,3,2,0:T(8,128)(2,1)S(1)}, bf16[27,128,1,64]{1,3,2,0:T(8,128)(2,1)}, u32[]{:S(2)}) copy-start(bf16[27,128,1,64]{1,3,2,0:T(8,128)(2,1)} %param.12) | copy-start | bytes 1327108
  24.7 12.9 %collective-permute-start.5 = (f32[1024,128]{1,0:T(8,128)S(1)}, f32[1024,128]{1,0:T(8,128)S(1)}, u32[]{:S(2)}, u32[]{:S(2)}) collective-permute-start(f32[1024,128]{1,0:T(8,128)S(1)} %convert_select_fusion.mine), channel_id=1, source_target_pairs={{0,1},{1,0},{2,3},{3,2},{4,5},{5,4},{6,7},{7,6},{8,9},{9,8},{10,11... | collective-permute-start | bytes 1572872 | tf_op jit(solution)/shard_map/ppermute | solution.py:91
  25.6 1.7 %copy-start.4 = (f32[128]{0:T(128)S(1)}, f32[128]{0:T(128)}, u32[]{:S(2)}) copy-start(f32[128]{0:T(128)} %param.13) | copy-start | bytes 1540
  25.6 11.9 %collective-permute-start.6 = (bf16[27,64,128]{2,1,0:T(8,128)(2,1)S(1)}, bf16[27,64,128]{2,1,0:T(8,128)(2,1)S(1)}, u32[]{:S(2)}, u32[]{:S(2)}) collective-permute-start(bf16[27,64,128]{2,1,0:T(8,128)(2,1)S(1)} %bitcast.97), channel_id=1, source_target_pairs={{0,2},{2,0},{1,3},{3,1},{4,6},{6,4},{5,7},{7,5},{8,10},{10,8},{9,1... | collective-permute-start | bytes 1327112 | tf_op jit(solution)/shard_map/ppermute | solution.py:91
  39.7 1.4 %collective-permute-start.7 = (bf16[2,256,128]{2,1,0:T(8,128)(2,1)S(1)}, bf16[2,256,128]{2,1,0:T(8,128)(2,1)S(1)}, u32[]{:S(2)}, u32[]{:S(2)}) collective-permute-start(bf16[2,256,128]{2,1,0:T(8,128)(2,1)S(1)} %dynamic-slice_bitcast_fusion), channel_id=1, source_target_pairs={{0,1},{1,0},{2,3},{3,2},{4,5},{5,4},{6,7},{7,6},{8,9},{9,8},{10,11... | collective-permute-start | bytes 393224 | tf_op jit(solution)/shard_map/ppermute | solution.py:91
  41.2 12.4 %copy-start.1 = (bf16[27,64,1,64]{3,1,2,0:T(8,128)(2,1)S(1)}, bf16[27,64,1,64]{3,1,2,0:T(8,128)(2,1)}, u32[]{:S(2)}) copy-start(bf16[27,64,1,64]{3,1,2,0:T(8,128)(2,1)} %param.14) | copy-start | bytes 663556
  53.6 1.6 %collective-permute-start.8 = (bf16[256,128]{1,0:T(8,128)(2,1)S(1)}, bf16[256,128]{1,0:T(8,128)(2,1)S(1)}, u32[]{:S(2)}, u32[]{:S(2)}) collective-permute-start(bf16[256,128]{1,0:T(8,128)(2,1)S(1)} %multiply_convert_fusion), channel_id=1, source_target_pairs={{0,1},{1,0},{2,3},{3,2},{4,5},{5,4},{6,7},{7,6},{8,9},{9,8},{10,11... | collective-permute-start | bytes 196616 | tf_op jit(solution)/shard_map/ppermute | solution.py:91
  53.6 12.6 %collective-permute-start.9 = (bf16[27,64,64]{2,1,0:T(8,128)(2,1)S(1)}, bf16[27,64,64]{2,1,0:T(8,128)(2,1)S(1)}, u32[]{:S(2)}, u32[]{:S(2)}) collective-permute-start(bf16[27,64,64]{2,1,0:T(8,128)(2,1)S(1)} %bitcast.99), channel_id=1, source_target_pairs={{0,2},{2,0},{1,3},{3,1},{4,6},{6,4},{5,7},{7,5},{8,10},{10,8},{9,1... | collective-permute-start | bytes 663560 | tf_op jit(solution)/shard_map/ppermute | solution.py:91
  79.1 0.7 copy-start.3

commit v3 on v2

--- a/solution.py
+++ b/solution.py
@@ -97,6 +97,157 @@
     return jnp.stack([first, second], axis=axis)
 
 
+def pack_kernel(weight, coarse, skip, first, biases, early, late, half, held, sems):
+    s = lax.axis_index("space")
+    g = lax.axis_index("groups")
+    kb = early.shape[1]
+    rows, deep = (weight.shape[0], coarse.shape[0])
+    span = half.shape[0]
+
+    def fill(up_packet, skip_packet):
+        moves = [(weight, up_packet.at[pl.ds(0, rows)])]
+        for i in range(coarse.shape[1] // kb):
+            place = up_packet.at[pl.ds(rows + i * deep, deep)]
+            moves.append((coarse.at[:, pl.ds(i * kb, kb)], place))
+        moves.append((skip, skip_packet.at[pl.ds(0, skip.shape[0])]))
+        rest = skip_packet.shape[0] - skip.shape[0]
+        moves.append((weight.at[pl.ds(0, rest)], skip_packet.at[pl.ds(skip.shape[0], rest)]))
+        moves.append((first.at[pl.ds(g * (first.shape[0] - span), span)], half))
+        for i, bias in enumerate(biases):
+            moves.append((bias, held.at[pl.ds(i, 1)]))
+        copies = [
+            pltpu.make_async_copy(source, place, sems.at[i])
+            for i, (source, place) in enumerate(moves)
+        ]
+        for copy in copies:
+            copy.start()
+        for copy in copies:
+            copy.wait()
+
+    @pl.when(s < 2)
+    def _():
+        fill(early, late)
+
+    @pl.when(s >= 2)
+    def _():
+        fill(late, early)
+
+
+def packed(weight, coarse, skip, first, biases):
+    rows, kb = weight.shape
+    deep, cin = coarse.shape
+    count = len(biases)
+    packet = jax.ShapeDtypeStruct((rows + deep * (cin // kb), kb), jnp.bfloat16)
+    span = (first.shape[0] + 1) // 2
+    half = jax.ShapeDtypeStruct((span,) + first.shape[1:], jnp.bfloat16)
+    held = jax.ShapeDtypeStruct((count,) + biases[0].shape[1:], jnp.float32)
+
+    def kernel(*refs):
+        pack_kernel(*refs[:4], refs[4 : 4 + count], *refs[4 + count :])
+
+    return pl.pallas_call(
+        kernel,
+        out_shape=(packet, packet, half, held),
+        in_specs=[pl.BlockSpec(memory_space=pltpu.HBM)] * (4 + count),
+        out_specs=[pl.BlockSpec(memory_space=pltpu.VMEM)] * 4,
+        scratch_shapes=[pltpu.SemaphoreType.DMA((4 + cin // kb + count,))],
+        compiler_params=pltpu.CompilerParams(vmem_limit_bytes=60 * 2**20),
+    )(weight, coarse, skip, first, *biases)
+
+
+def dense_kernel(weight, out):
+    deep = weight.shape[1] // 2
+    for tap in range(weight.shape[0]):
+        out[tap] = jnp.concatenate([weight[tap, :deep], weight[tap, deep:]], axis=1)
+
+
+def dense(weight):
+    taps, rows, lanes = weight.shape
+    return pl.pallas_call(
+        dense_kernel,
+        out_shape=jax.ShapeDtypeStruct((taps, rows // 2, 2 * lanes), weight.dtype),
+        in_specs=[pl.BlockSpec(memory_space=pltpu.VMEM)],
+        out_specs=pl.BlockSpec(memory_space=pltpu.VMEM),
+        compiler_params=pltpu.CompilerParams(vmem_limit_bytes=16 * 2**20),
+    )(weight)
+
+
+def up_kernel(early, late, early_other, late_other, slabs, held, part):
+    s, d, c = (lax.axis_index(a) for a in ("space", "dp", "chan"))
+    rows, kb = early_other.shape
+    deep = slabs.shape[2]
+    taps = 8
+    own_n = rows // taps
+    half = part.shape[1]
+    block = part.shape[0] // 4
+
+    @pl.when(s < 2)
+    def _():
+        lefts, rights = ([], [])
+        for k in range(2):
+            pieces = []
+            for parity in range(2):
+                for i, packet in enumerate((early, late)):
+                    low = packet[pl.ds(rows + 2 * k * deep, deep)]
+                    high = packet[pl.ds(rows + (2 * k + 1) * deep, deep)]
+                    mine = jnp.where(c == 0, low, high)
+                    pieces.append(jnp.where(c == parity, mine, slabs[i, k]))
+            lefts.append(jnp.concatenate(pieces, axis=0))
+            packet, other = ((early, early_other), (late, late_other))[k]
+            pieces = []
+            for tap in range(taps):
+                one = packet[pl.ds(tap * own_n, own_n)]
+                two = other[pl.ds(tap * own_n, own_n)]
+                pieces += [jnp.where(d == 0, one, two), jnp.where(d == 0, two, one)]
+            rights.append(jnp.concatenate(pieces, axis=0))
+        left = jnp.concatenate(lefts, axis=1)
+        right = jnp.concatenate(rights, axis=1)
+        bias = held[0:1] * jnp.where(c == s, 1.0, 0.0)
+        for tap in range(taps):
+            a, b, cc = (tap // 4, tap // 2 % 2, tap % 2)
+            total = lax.dot_general(
+                left,
+                right[tap * 2 * own_n : (tap + 1) * 2 * own_n],
+                NT,
+                preferred_element_type=jnp.float32,
+            )
+            total = total + bias
+            for parity in range(2):
+                for i in range(2):
+                    z = 2 * (parity + 2 * i) + cc
+                    for x in range(deep // 8):
+                        at = (parity * 2 + i) * deep + x * 8
+                        start = ((2 * x + a) * 16 + b) * 8 + z
+                        part[pl.ds(start, 8, 16)] = total[at : at + 8]
+
+    @pl.when(s >= 2)
+    def _():
+        for i, packet in enumerate((late, early)):
+            values = packet[pl.ds(0, block)].astype(jnp.float32)
+            for parity in range(2):
+                place = pl.ds((2 * i + parity) * block, block)
+                part[place] = jnp.where(c == parity, values, 0.0)
+
+
+def up_part(early, late, early_other, late_other, slabs, held, cells):
+    return pl.pallas_call(
+        up_kernel,
+        out_shape=jax.ShapeDtypeStruct((cells, held.shape[1]), jnp.float32),
+        in_specs=[pl.BlockSpec(memory_space=pltpu.VMEM)] * 6,
+        out_specs=pl.BlockSpec(memory_space=pltpu.VMEM),
+        compiler_params=pltpu.CompilerParams(vmem_limit_bytes=32 * 2**20),
+    )(early, late, early_other, late_other, slabs, held)
+
+
+def reduced(chunk_for, s):
+    total = chunk_for(s).astype(jnp.float32)
+    for step in (3, 2, 1):
+        routes = [(i, i ^ step) for i in range(4)]
+        term = lax.ppermute(chunk_for(s ^ step), "space", routes)
+        total = total + term.astype(jnp.float32)
+    return total
+
+
 def line_routes():
     early, late = ([], [])
     for s in range(4):
@@ -114,7 +265,7 @@
 NN = (((1,), (0,)), ((), ()))
 
 
-def first_kernel(mine, theirs, own, other, bias, out, even, odd):
+def first_kernel(mine, theirs, own, near, far, held, out, even, odd):
     planes = even.shape[0] - 2
     rows, width = even.shape[1:]
     half = mine.shape[1]
@@ -134,9 +285,22 @@
         taps = jnp.concatenate([below, plane, above], axis=1)
         even[x + 1] = taps.astype(jnp.bfloat16)
         odd[x + 1] = jnp.concatenate([edge, taps, edge], axis=0).astype(jnp.bfloat16)
-    lane = lax.broadcasted_iota(jnp.int32, (2 * quad * rows, half), 1)
+    s, d, g = (lax.axis_index(a) for a in ("space", "dp", "groups"))
+    swap = half // 2
+    bias = jnp.broadcast_to(held[1:2], (8, half))
+    bias = jnp.where(d == 0, bias, pltpu.roll(bias, swap, 1))[0:1]
+    bias = bias * jnp.where(s == 0, 1.0, 0.0)
+    span, taps = (near.shape[0], own.shape[0])
+    other = []
+    for tap in range(taps):
+        if tap < span:
+            lower, upper = (near[tap], far[tap])
+        else:
+            lower, upper = (far[tap - taps + span], near[tap - taps + span])
+        if tap == span - 1:
+            upper = near[0]
+        other.append(jnp.where(g == 0, lower, upper))
     for q in range(2):
-        total = jnp.broadcast_to(bias[...], (4 * quad * rows // 2, half))
         total = None
         for dx in range(3):
             for dy in range(3):
@@ -153,31 +317,30 @@
                 )
                 term = lax.dot_general(left, right, NT, preferred_element_type=jnp.float32)
                 total = term if total is None else total + term
-        total = total + bias[...]
+        total = total + bias
         low, high = (total[: quad * rows], total[quad * rows :])
         lane = lax.broadcasted_iota(jnp.int32, low.shape, 1)
-        swap = half // 2
         out[q, 0] = jnp.where(lane < swap, low, pltpu.roll(high, swap, 1)).astype(jnp.bfloat16)
         out[q, 1] = jnp.where(lane < swap, pltpu.roll(low, swap, 1), high).astype(jnp.bfloat16)
 
 
-def first_conv(mine, theirs, own, other, bias, planes, fz):
+def first_conv(mine, theirs, own, near, far, held, planes):
     cells, half = mine.shape
     rows = cells // planes
     return pl.pallas_call(
         first_kernel,
         out_shape=jax.ShapeDtypeStruct((2, 2, cells // 4, half), jnp.bfloat16),
-        in_specs=[pl.BlockSpec(memory_space=pltpu.VMEM)] * 5,
+        in_specs=[pl.BlockSpec(memory_space=pltpu.VMEM)] * 6,
         out_specs=pl.BlockSpec(memory_space=pltpu.VMEM),
         scratch_shapes=[
             pltpu.VMEM((planes + 2, rows, 3 * half), jnp.bfloat16),
             pltpu.VMEM((planes + 2, rows + 16, 3 * half), jnp.bfloat16),
         ],
         compiler_params=pltpu.CompilerParams(vmem_limit_bytes=32 * 2**20),
-    )(mine, theirs, own, other, bias)
-
-
-def second_kernel(hidden, own, other, out, even, odd):
+    )(mine, theirs, own, near, far, held)
+
+
+def second_kernel(hidden, own, other, held, out, even, odd):
     planes = even.shape[0] - 2
     rows, width = even.shape[1:]
     lanes = hidden.shape[2]
@@ -208,7 +371,17 @@
                 x = (q * 2 + u) * per + r
                 even[x + 1] = taps.astype(jnp.bfloat16)
                 odd[x + 1] = jnp.concatenate([edge, taps, edge], axis=0).astype(jnp.bfloat16)
-    lane_w = lax.broadcasted_iota(jnp.int32, (3 * k, lanes), 1)
+    lane = lax.broadcasted_iota(jnp.int32, own.shape[1:], 1)
+    low = lane < swap
+    rights = []
+    for tap in range(0, own.shape[0], 3):
+        rows_in = []
+        for dz in range(3):
+            one = jnp.where(d == 0, own[tap + dz], other[tap + dz])
+            two = jnp.where(d == 0, other[tap + dz], own[tap + dz])
+            rows_in.append(jnp.where(low, one, pltpu.roll(two, swap, 1)))
+            rows_in.append(jnp.where(low, pltpu.roll(one, swap, 1), two))
+        rights.append(jnp.concatenate(rows_in, axis=0))
     for q in range(2):
         total = None
         for dx in range(3):
@@ -219,33 +392,29 @@
                 else:
                     left = odd[at, pl.ds(8 * dy, rows)]
                 left = left.reshape(planes // 2 * rows, width)[:, : 3 * k]
-                tap = (dx * 3 + dy) * 3
-                one = own[tap : tap + 3].reshape(3 * k, k)
-                two = other[tap : tap + 3].reshape(3 * k, k)
-                right = jnp.concatenate(
-                    [jnp.where(d == 0, one, two), jnp.where(d == 0, two, one)], axis=1
-                )
+                right = rights[dx * 3 + dy]
                 term = lax.dot_general(left, right, NN, preferred_element_type=jnp.float32)
                 total = term if total is None else total + term
+        total = total + held[2:3] * jnp.where(lax.axis_index("space") == 0, 1.0, 0.0)
         n = planes // 2 * rows
         out[q * n : (q + 1) * n] = total.astype(jnp.bfloat16)
 
 
-def second_conv(hidden, own, other, planes):
+def second_conv(hidden, own, other, held, planes):
     _, rows2, lanes = hidden.shape
     cells = rows2 * 4
     rows = cells // planes
     return pl.pallas_call(
         second_kernel,
         out_shape=jax.ShapeDtypeStruct((cells, lanes), jnp.bfloat16),
-        in_specs=[pl.BlockSpec(memory_space=pltpu.VMEM)] * 3,
+        in_specs=[pl.BlockSpec(memory_space=pltpu.VMEM)] * 4,
         out_specs=pl.BlockSpec(memory_space=pltpu.VMEM),
         scratch_shapes=[
             pltpu.VMEM((planes + 2, rows, 2 * lanes), jnp.bfloat16),
             pltpu.VMEM((planes + 2, rows + 16, 2 * lanes), jnp.bfloat16),
         ],
         compiler_params=pltpu.CompilerParams(vmem_limit_bytes=32 * 2**20),
-    )(hidden, own, other)
+    )(hidden, own, other, held)
 
 
 def stationary(
@@ -254,68 +423,56 @@
     s, d, c = (lax.axis_index(a) for a in ("space", "dp", "chan"))
     group = ("space", "dp", "chan")
     _, _, cx, cy, cin = coarse.shape
-    cz = 4
     _, bx, fy, fz, half = skip.shape
     fx = 4 * bx
     cells = cx * cy
     block = bx * fy * fz
-    taps = up_weight.shape[0]
-    kb = up_weight.shape[1]
-    own_n = up_weight.shape[3]
-    lanes = 128
+    taps, kb, _, own_n = up_weight.shape
     up_rows = taps * own_n
     first_own = first_weight[:, :, 0, :].transpose(0, 2, 1)
-    second_own = second_weight[:, :, 0, :]
-    first_other = swapped(first_own, "dp")
-    up_rows_own = up_weight[:, :, 0, :].transpose(0, 2, 1).reshape(up_rows, kb)
-    coarse_rows = coarse.reshape(cells, cin // kb, kb).transpose(1, 0, 2).reshape(-1, kb)
-    up_packet = jnp.concatenate([up_rows_own, coarse_rows], axis=0)
-    skip_rows = skip.reshape(block, half)
-    skip_packet = jnp.pad(skip_rows, ((0, up_packet.shape[0] - block), (0, 0)))
+    early, late, near, held = packed(
+        up_weight[:, :, 0, :].transpose(0, 2, 1).reshape(up_rows, kb),
+        coarse.reshape(cells, cin),
+        skip.reshape(block, half),
+        first_own,
+        [bias.reshape(1, half) for bias in (up_bias, first_bias, second_bias)],
+    )
     early_route, late_route = line_routes()
-    early = lax.ppermute(jnp.where(s < 2, up_packet, skip_packet), group, early_route)
-    late = lax.ppermute(jnp.where(s < 2, skip_packet, up_packet), group, late_route)
-    weights = []
-    for packet in (early, late):
-        own = packet[:up_rows]
-        other = swapped(own, "dp")
-        both = ordered(d, own.reshape(taps, own_n, kb), other.reshape(taps, own_n, kb), 1)
-        weights.append(both.reshape(taps, 2 * own_n, kb))
-    weights = jnp.stack(weights)
+    late = lax.ppermute(late, group, late_route)
+    early = lax.ppermute(early, group, early_route)
+    near = swapped(near, "dp")
+    early_other = swapped(early[:up_rows], "dp")
+    far = swapped(near, "groups")
+    late, early_other = lax.optimization_barrier((late, early_other))
+    late_other = swapped(late[:up_rows], "dp")
+    second_raw, early = lax.optimization_barrier((second_weight[:, :, 0, :], early))
+    second_own = dense(second_raw)
+    second_own, late_other = lax.optimization_barrier((second_own, late_other))
     second_other = swapped(second_own, "dp")
     slabs = jnp.stack([early[up_rows:], late[up_rows:]]).reshape(2, 2, 2, cells, kb)
-    mine = lax.dynamic_index_in_dim(slabs, c, 2, keepdims=False)
     theirs = lax.dynamic_index_in_dim(slabs, 1 - c, 2, keepdims=False)
-    slabs = ordered(c, mine, swapped(theirs, "chan"), 1)
-    up = jnp.einsum("zwkmi,ktoi->zwmto", slabs, weights, preferred_element_type=jnp.float32)
-    up = up + jnp.where(c == s, up_bias, 0.0)
-    up = up.reshape(cz, cx, cy, 2, 2, 2, half).transpose(1, 3, 2, 4, 0, 5, 6)
-    up = up.reshape(fx * fy * fz, half)
-    blocks = jnp.stack([late[:block], early[:block]])
-    nothing = jnp.zeros_like(blocks)
-    placed = ordered(c, blocks, nothing, 1).reshape(fx * fy * fz, half)
-    part = jnp.where(s < 2, up, placed.astype(jnp.float32))
-    bias = first_bias.reshape(2, own_n)
-    bias = jnp.where(d == 0, bias.reshape(-1), bias[::-1].reshape(-1))
-    bias = jnp.where(s == 0, bias, 0.0)[None]
-    first = first_conv(part, swapped(part, "chan"), first_own, first_other, bias, fx, fz)
+    slabs, far = lax.optimization_barrier((swapped(theirs, "chan"), far))
+    part = up_part(early, late, early_other, late_other, slabs, held, fx * fy * fz)
+    first = first_conv(part, swapped(part, "chan"), first_own, near, far, held, fx)
     mine = lax.dynamic_index_in_dim(first, c, 0, keepdims=False)
     theirs = lax.dynamic_index_in_dim(first, 1 - c, 0, keepdims=False)
-    chunks = ordered(c, mine, swapped(theirs, "chan"), 0)
-    chunks = ordered(d, chunks[:, 0], chunks[:, 1], 1).reshape(4, block, half)
-    terms = lax.all_to_all(chunks, "space", split_axis=0, concat_axis=0, tiled=True)
-    hidden = jax.nn.silu(jnp.sum(terms.astype(jnp.float32), axis=0)).astype(jnp.bfloat16)
+    theirs, second_other = lax.optimization_barrier((swapped(theirs, "chan"), second_other))
+    chunks = jnp.stack([mine, theirs]).reshape(4, block, half)
+
+    def chunk_for(plane):
+        place = 2 * ((plane // 2) ^ c) + ((plane % 2) ^ d)
+        return lax.dynamic_index_in_dim(chunks, place, 0, keepdims=False)
+
+    hidden = jax.nn.silu(reduced(chunk_for, s)).astype(jnp.bfloat16)
     hidden = ordered(c, hidden, swapped(hidden, "chan"), 0)
-    second = second_conv(hidden, second_own, second_other, fx)
-    second = second.reshape(4, block, half)
-    terms = lax.all_to_all(second, "space", split_axis=0, concat_axis=0, tiled=True)
-    total = jnp.sum(terms.astype(jnp.float32), axis=0)
-    return (total + second_bias).astype(jnp.bfloat16).reshape(skip.shape)
+    second = second_conv(hidden, second_own, second_other, held, fx).reshape(4, block, half)
+    total = reduced(lambda plane: lax.dynamic_index_in_dim(second, plane, 0, keepdims=False), s)
+    return total.astype(jnp.bfloat16).reshape(skip.shape)
 
 
 def keeps_weights(mesh):
-    sizes = tuple(mesh.shape[a] for a in ("space", "dp", "chan"))
-    return sizes == (4, 2, 2)
+    sizes = tuple(mesh.shape[a] for a in ("groups", "space", "dp", "chan"))
+    return sizes == (2, 4, 2, 2)
 
 
 def solution(mesh):

time: 80.7 us -> 54.8 us (0.68)
  blocking collectives: 23.6 us -> 0 us
  starting transfers between devices: 10.5 us -> 21.3 us
  waiting for transfers between devices: 36.3 us -> 25.6 us
  local copies, waits for them, and re-layouts: 3.74 us -> 0.26 us
  Pallas kernels: 3.63 us -> 6.31 us
  other arithmetic: 2.07 us -> 0.8 us
    all_to_all x2 -> x0, blocking collectives: 23.6 us -> none  [the longest x1 12.2 us: stationary(): lax.all_to_all(chunks, 'space', split_axis=0, concat_axis=0, tiled=True)]
    ppermute x8 -> x9, waiting for transfers between devices: 29 us -> 11.2 us  [swapped(): return lax.ppermute(array, axis, [(0, 1), (1, 0)])]
    ppermute x2 -> x8, starting transfers between devices: 4.77 us -> 14.3 us  [the longest x6 10.2 us: reduced(): term = lax.ppermute(chunk_for(s ^ step), 'space', routes)]
    ppermute x2 -> x8, waiting for transfers between devices: 7.34 us -> 14.5 us  [the longest x6 9.3 us: reduced(): term = lax.ppermute(chunk_for(s ^ step), 'space', routes)]
    pallas_call x0 -> x3, Pallas kernels: none -> 2.64 us  [the longest x1 2.1 us: packed(): pl.pallas_call(kernel, out_shape=(packet, packet, half, held), in_specs=[...]
    unnamed x12 -> x10, local copies, waits for them, and re-layouts: 2.26 us -> 0.03 us
    reshape x4 -> x0, local copies, waits for them, and re-layouts: 1.38 us -> none  [the longest x1 0.81 us: stationary(): coarse.reshape(cells, cin // kb, kb).transpose(1, 0, 2).reshape(-1, kb)]
    ppermute x8 -> x9, starting transfers between devices: 5.75 us -> 6.95 us  [swapped(): return lax.ppermute(array, axis, [(0, 1), (1, 0)])]
  transfers between devices with their start and end apart: 10 -> 17, of which waited for: 6 -> 11; matrix products, arithmetic and copies ran while one was open for 0% -> 0% of each run, Pallas kernels for 0% -> 4%
where the time goes in v3:
time: 54.8 us; the launch traced here: 54.5 us
  waiting for transfers between devices  25.6 us (47%)
  starting transfers between devices  21.3 us (39%)
  Pallas kernels  6.31 us (12%)
  other arithmetic  0.8 us (1%)
    ppermute x9, waiting for transfers between devices, swapped(): return lax.ppermute(array, axis, [(0, 1), (1, 0)])  11.2 us
    ppermute x6, starting transfers between devices, reduced(): term = lax.ppermute(chunk_for(s ^ step), 'space', routes)  10.2 us
    ppermute x6, waiting for transfers between devices, reduced(): term = lax.ppermute(chunk_for(s ^ step), 'space', routes)  9.3 us
    ppermute x9, starting transfers between devices, swapped(): return lax.ppermute(array, axis, [(0, 1), (1, 0)])  6.95 us
    ppermute x1, waiting for transfers between devices, stationary(): late = lax.ppermute(late, group, late_route)  5.17 us
    ppermute x1, starting transfers between devices, stationary(): late = lax.ppermute(late, group, late_route)  2.59 us
    pallas_call x1, Pallas kernels, first_conv(): pl.pallas_call(first_kernel, out_shape=jax.ShapeDtypeStruct((2, 2, cells...  2.16 us
    pallas_call x1, Pallas kernels, packed(): pl.pallas_call(kernel, out_shape=(packet, packet, half, held), in_specs=[...  2.1 us
  transfers between devices with their start and end apart: 17, of which 11 were waited for; matrix products, arithmetic and copies ran while one was open for 0% of the time, Pallas kernels for 4%

profile of v3, /device:TPU:0, one launch (start us, length us, event | category | flops | bytes accessed | tf_op | source)
XLA Modules:
  0.0 54.5 jit_solution(14027821400280853937)
XLA Ops:
  0.0 2.1 %shard_map.82 = (bf16[640,128]{1,0:T(8,128)(2,1)}, bf16[640,128]{1,0:T(8,128)(2,1)}, bf16[14,64,128]{2,1,0:T(8,128)(2,1)}, f32[3,128]{1,0:T(4,128)}) custom-call(bf16[512,128]{1,0:T(8,128)(2,1)} %bitcast.57, bf16[32,512]{1,0:T(8,128)(2,1)} %bitcast.60, bf16[256,128]{1,0:T(8,128)(2,1)} %bitcast.59, bf16[27,64,128]{2,1,0:T(8,128)(2,1)} %bitcast.48, ...), custom_call_target="tpu_custom_call" | custom-call | tf_op jit(solution)/shard_map/pallas_call | solution.py:148
  2.1 0.0 copy-start.3
  2.1 3.0 %collective-permute-start.5 = (bf16[14,64,128]{2,1,0:T(8,128)(2,1)}, bf16[14,64,128]{2,1,0:T(8,128)(2,1)S(1)}, u32[]{:S(2)}, u32[]{:S(2)}) collective-permute-start(bf16[14,64,128]{2,1,0:T(8,128)(2,1)} %get-tuple-element.26), channel_id=1, source_target_pairs={{0,2},{2,0},{1,3},{3,1},{4,6},{6,4},{5,7},{7,5},{8,10},{10,8},{9,1... | collective-permute-start | bytes 688136 | tf_op jit(solution)/shard_map/ppermute | solution.py:91
  5.1 1.6 %collective-permute-start = (bf16[640,128]{1,0:T(8,128)(2,1)}, bf16[640,128]{1,0:T(8,128)(2,1)S(1)}, u32[]{:S(2)}, u32[]{:S(2)}) collective-permute-start(bf16[640,128]{1,0:T(8,128)(2,1)} %get-tuple-element.19), channel_id=1, source_target_pairs={{0,0},{1,4},{2,2},{3,6},{4,1},{5,5},{6,3},{7,7},{8,8},{9,12},{10,1... | collective-permute-start | bytes 491528 | tf_op jit(solution)/shard_map/ppermute | solution.py:442
  6.7 2.6 %collective-permute-start.1 = (bf16[640,128]{1,0:T(8,128)(2,1)}, bf16[640,128]{1,0:T(8,128)(2,1)S(1)}, u32[]{:S(2)}, u32[]{:S(2)}) collective-permute-start(bf16[640,128]{1,0:T(8,128)(2,1)} %get-tuple-element.21), channel_id=1, source_target_pairs={{0,8},{1,12},{2,10},{3,14},{4,9},{5,13},{6,11},{7,15},{8,0},{9,4},... | collective-permute-start | bytes 491528 | tf_op jit(solution)/shard_map/ppermute | solution.py:441
  9.3 0.0 collective-permute-done.early
  9.3 0.6 %collective-permute-start.2 = (bf16[512,128]{1,0:T(8,128)(2,1)S(1)}, bf16[512,128]{1,0:T(8,128)(2,1)S(1)}, u32[]{:S(2)}, u32[]{:S(2)}) collective-permute-start(bf16[512,128]{1,0:T(8,128)(2,1)S(1)} %slice.16), channel_id=1, source_target_pairs={{0,2},{2,0},{1,3},{3,1},{4,6},{6,4},{5,7},{7,5},{8,10},{10,8},{9,1... | collective-permute-start | bytes 393224 | tf_op jit(solution)/shard_map/ppermute | solution.py:91
  9.9 1.0 %collective-permute-done.5.near = bf16[14,64,128]{2,1,0:T(8,128)(2,1)S(1)} collective-permute-done((bf16[14,64,128]{2,1,0:T(8,128)(2,1)}, bf16[14,64,128]{2,1,0:T(8,128)(2,1)S(1)}, u32[]{:S(2)}, u32[]{:S(2)}) %collective-permute-start.5) | collective-permute-done | bytes 229408 | tf_op jit(solution)/shard_map/ppermute | solution.py:91
  10.9 1.8 %collective-permute-start.6 = (bf16[14,64,128]{2,1,0:T(8,128)(2,1)S(1)}, bf16[14,64,128]{2,1,0:T(8,128)(2,1)S(1)}, u32[]{:S(2)}, u32[]{:S(2)}) collective-permute-start(bf16[14,64,128]{2,1,0:T(8,128)(2,1)S(1)} %collective-permute-done.5.near), channel_id=1, source_target_pairs={{0,16},{16,0},{1,17},{17,1},{2,18},{18,2},{3,19},{19,3},{4,20},{20... | collective-permute-start | bytes 688136 | tf_op jit(solution)/shard_map/ppermute | solution.py:91
  12.7 0.0 copy-done.1
  12.7 5.2 %collective-permute-done.1.late = bf16[640,128]{1,0:T(8,128)(2,1)S(1)} collective-permute-done((bf16[640,128]{1,0:T(8,128)(2,1)}, bf16[640,128]{1,0:T(8,128)(2,1)S(1)}, u32[]{:S(2)}, u32[]{:S(2)}) %collective-permute-start.1) | collective-permute-done | bytes 163872 | tf_op jit(solution)/shard_map/ppermute | solution.py:441
  17.9 0.0 collective-permute-done.2.early_other
  17.9 0.6 %collective-permute-start.3 = (bf16[512,128]{1,0:T(8,128)(2,1)S(1)}, bf16[512,128]{1,0:T(8,128)(2,1)S(1)}, u32[]{:S(2)}, u32[]{:S(2)}) collective-permute-start(bf16[512,128]{1,0:T(8,128)(2,1)S(1)} %slice.13), channel_id=1, source_target_pairs={{0,2},{2,0},{1,3},{3,1},{4,6},{6,4},{5,7},{7,5},{8,10},{10,8},{9,1... | collective-permute-start | bytes 393224 | tf_op jit(solution)/shard_map/ppermute | solution.py:91
  18.5 0.1 slice-done
  18.7 0.0 collective-permute-start.4
  18.7 0.0 copy-done.3
  18.7 0.0 copy-start.4
  18.7 0.1 shard_map.83.own
  18.9 4.1 %collective-permute-done.3.late_other = bf16[512,128]{1,0:T(8,128)(2,1)S(1)} collective-permute-done((bf16[512,128]{1,0:T(8,128)(2,1)S(1)}, bf16[512,128]{1,0:T(8,128)(2,1)S(1)}, u32[]{:S(2)}, u32[]{:S(2)}) %collective-permute-start.3) | collective-permute-done | bytes 131104 | tf_op jit(solution)/shard_map/ppermute | solution.py:91
  22.9 0.0 collective-permute-done.4.slabs
  23.0 0.0 collective-permute-done.6.far
  23.0 0.0 copy-done.4
  23.0 0.0 copy-start
  23.0 0.4 shard_map.84.mine
  23.4 0.1 collective-permute-start.7
  23.5 0.6 %collective-permute-start.9 = (bf16[27,32,128]{2,1,0:T(8,128)(2,1)S(1)}, bf16[27,32,128]{2,1,0:T(8,128)(2,1)S(1)}, u32[]{:S(2)}, u32[]{:S(2)}) collective-permute-start(bf16[27,32,128]{2,1,0:T(8,128)(2,1)S(1)} %shard_map.83.own), channel_id=1, source_target_pairs={{0,2},{2,0},{1,3},{3,1},{4,6},{6,4},{5,7},{7,5},{8,10},{10,8},{9,1... | collective-permute-start | bytes 663560 | tf_op jit(solution)/shard_map/ppermute | solution.py:91
  24.1 1.3 %collective-permute-done.7.theirs = f32[1024,128]{1,0:T(8,128)S(1)} collective-permute-done((f32[1024,128]{1,0:T(8,128)S(1)}, f32[1024,128]{1,0:T(8,128)S(1)}, u32[]{:S(2)}, u32[]{:S(2)}) %collective-permute-start.7) | collective-permute-done | bytes 524320 | tf_op jit(solution)/shard_map/ppermute | solution.py:91
  25.4 2.2 %shard_map.85 = bf16[2,2,256,128]{3,2,1,0:T(8,128)(2,1)S(1)} custom-call(f32[1024,128]{1,0:T(8,128)S(1)} %shard_map.84.mine, f32[1024,128]{1,0:T(8,128)S(1)} %collective-permute-done.7.theirs, bf16[27,64,128]{2,1,0:T(8,128)(2,1)S(1)} %bitcast.49, bf16[14,64,128]{2,1,0:T(8,128)(2,1)S(1)} %collective-permute-done.5.near, ...), custom_call_target="tpu_custom_call" | custom-call | tf_op jit(solution)/shard_map/pallas_call | solution.py:330
  27.6 0.2 collective-permute-start.8
  27.8 3.5 %collective-permute-done.9.other = bf16[27,32,128]{2,1,0:T(8,128)(2,1)S(1)} collective-permute-done((bf16[27,32,128]{2,1,0:T(8,128)(2,1)S(1)}, bf16[27,32,128]{2,1,0:T(8,128)(2,1)S(1)}, u32[]{:S(2)}, u32[]{:S(2)}) %collective-permute-start.9) | collective-permute-done | bytes 221216 | tf_op jit(solution)/shard_map/ppermute | solution.py:91
  31.3 0.0 collective-permute-done.8
  31.4 5.1 %collective-permute-start.10 = (bf16[256,128]{1,0:T(8,128)(2,1)S(1)}, bf16[256,128]{1,0:T(8,128)(2,1)S(1)}, u32[]{:S(2)}, u32[]{:S(2)}) collective-permute-start(bf16[256,128]{1,0:T(8,128)(2,1)S(1)} %get-tuple-element.36), channel_id=1, source_target_pairs={{0,12},{4,8},{8,4},{12,0},{1,13},{5,9},{9,5},{13,1},{2,14},{6,10},... | collective-permute-start | bytes 196616 | tf_op jit(solution)/shard_map/ppermute | solution.py:246
  36.5 0.0 collective-permute-start.11
  36.5 0.6 %collective-permute-start.12 = (bf16[256,128]{1,0:T(8,128)(2,1)S(1)}, bf16[256,128]{1,0:T(8,128)(2,1)S(1)}, u32[]{:S(2)}, u32[]{:S(2)}) collective-permute-start(bf16[256,128]{1,0:T(8,128)(2,1)S(1)} %get-tuple-element.37), channel_id=1, source_target_pairs={{0,4},{4,0},{8,12},{12,8},{1,5},{5,1},{9,13},{13,9},{2,6},{6,2},{1... | collective-permute-start | bytes 196616 | tf_op jit(solution)/shard_map/ppermute | solution.py:246
  37.1 2.2 %collective-permute-done.10 = bf16[256,128]{1,0:T(8,128)(2,1)S(1)} collective-permute-done((bf16[256,128]{1,0:T(8,128)(2,1)S(1)}, bf16[256,128]{1,0:T(8,128)(2,1)S(1)}, u32[]{:S(2)}, u32[]{:S(2)}) %collective-permute-start.10) | collective-permute-done | bytes 65568 | tf_op jit(solution)/shard_map/ppermute | solution.py:246
  39.3 2.4 %collective-permute-done.11 = bf16[256,128]{1,0:T(8,128)(2,1)S(1)} collective-permute-done((bf16[256,128]{1,0:T(8,128)(2,1)S(1)}, bf16[256,128]{1,0:T(8,128)(2,1)S(1)}, u32[]{:S(2)}, u32[]{:S(2)}) %collective-permute-start.11) | collective-permute-done | bytes 65568 | tf_op jit(solution)/shard_map/ppermute | solution.py:246
  41.7 0.3 collective-permute-done.12
  42.0 0.1 multiply_convert_fusion
  42.1 0.1 collective-permute-start.13
  42.2 1.2 %collective-permute-done.13 = bf16[256,128]{1,0:T(8,128)(2,1)S(1)} collective-permute-done((bf16[256,128]{1,0:T(8,128)(2,1)S(1)}, bf16[256,128]{1,0:T(8,128)(2,1)S(1)}, u32[]{:S(2)}, u32[]{:S(2)}) %collective-permute-start.13) | collective-permute-done | bytes 65568 | tf_op jit(solution)/shard_map/ppermute | solution.py:91
  43.4 1.5 %shard_map.86 = bf16[1024,128]{1,0:T(8,128)(2,1)S(1)} custom-call(bf16[2,256,128]{2,1,0:T(8,128)(2,1)S(1)} %pad_maximum_fusion.1.hidden, bf16[27,32,128]{2,1,0:T(8,128)(2,1)S(1)} %shard_map.83.own, bf16[27,32,128]{2,1,0:T(8,128)(2,1)S(1)} %collective-permute-done.9.other, f32[3,128]{1,0:T(4,128)S(1)} %copy-done.4), custom_call_target="tpu_custom_call" | custom-call | tf_op jit(solution)/shard_map/pallas_call | solution.py:407
  45.0 2.1 %collective-permute-start.14 = (bf16[256,128]{1,0:T(8,128)(2,1)S(1)}, bf16[256,128]{1,0:T(8,128)(2,1)S(1)}, u32[]{:S(2)}, u32[]{:S(2)}) collective-permute-start(bf16[256,128]{1,0:T(8,128)(2,1)S(1)} %get-tuple-element.33), channel_id=1, source_target_pairs={{0,12},{4,8},{8,4},{12,0},{1,13},{5,9},{9,5},{13,1},{2,14},{6,10},... | collective-permute-start | bytes 196616 | tf_op jit(solution)/shard_map/ppermute | solution.py:246
  47.1 0.4 collective-permute-start.15
  47.5 2.0 %collective-permute-start.16 = (bf16[256,128]{1,0:T(8,128)(2,1)S(1)}, bf16[256,128]{1,0:T(8,128)(2,1)S(1)}, u32[]{:S(2)}, u32[]{:S(2)}) collective-permute-start(bf16[256,128]{1,0:T(8,128)(2,1)S(1)} %get-tuple-element.34), channel_id=1, source_target_pairs={{0,4},{4,0},{8,12},{12,8},{1,5},{5,1},{9,13},{13,9},{2,6},{6,2},{1... | collective-permute-start | bytes 196616 | tf_op jit(solution)/shard_map/ppermute | solution.py:246
  49.4 2.4 %collective-permute-done.14 = bf16[256,128]{1,0:T(8,128)(2,1)S(1)} collective-permute-done((bf16[256,128]{1,0:T(8,128)(2,1)S(1)}, bf16[256,128]{1,0:T(8,128)(2,1)S(1)}, u32[]{:S(2)}, u32[]{:S(2)}) %collective-permute-start.14) | collective-permute-done | bytes 65568 | tf_op jit(solution)/shard_map/ppermute | solution.py:246
  51.8 2.0 %collective-permute-done.15 = bf16[256,128]{1,0:T(8,128)(2,1)S(1)} collective-permute-done((bf16[256,128]{1,0:T(8,128)(2,1)S(1)}, bf16[256,128]{1,0:T(8,128)(2,1)S(1)}, u32[]{:S(2)}, u32[]{:S(2)}) %collective-permute-start.15) | collective-permute-done | bytes 65568 | tf_op jit(solution)/shard_map/ppermute | solution.py:246
  53.9 0.0 collective-permute-done.16
  53.9 0.7 %fusion.2 = bf16[256,128]{1,0:T(8,128)(2,1)} fusion(bf16[256,128]{1,0:T(8,128)(2,1)S(1)} %collective-permute-done.16, bf16[256,128]{1,0:T(8,128)(2,1)S(1)} %collective-permute-done.15, bf16[256,128]{1,0:T(8,128)(2,1)S(1)} %collective-permute-done.14, bf16[4,256,128]{2,1,0:T(8,128)(2,1)S(1)} %bitcast.51, s32[]{:T(128)S(6)} %select_n.95), kind=kLoop, calls=%fused_computation.5 | loop fusion | flops 262144 | bytes 327684 | tf_op jit(solution)/shard_map/convert_element_type | solution.py:470
  (15 shorter events, 0.2 us)
Async XLA Ops:
  2.1 16.6 %copy-start.3 = (bf16[27,64,1,64]{3,1,2,0:T(8,128)(2,1)S(1)}, bf16[27,64,1,64]{3,1,2,0:T(8,128)(2,1)}, u32[]{:S(2)}) copy-start(bf16[27,64,1,64]{3,1,2,0:T(8,128)(2,1)} %param.14) | copy-start | bytes 663556
  2.1 8.8 %collective-permute-start.5 = (bf16[14,64,128]{2,1,0:T(8,128)(2,1)}, bf16[14,64,128]{2,1,0:T(8,128)(2,1)S(1)}, u32[]{:S(2)}, u32[]{:S(2)}) collective-permute-start(bf16[14,64,128]{2,1,0:T(8,128)(2,1)} %get-tuple-element.26), channel_id=1, source_target_pairs={{0,2},{2,0},{1,3},{3,1},{4,6},{6,4},{5,7},{7,5},{8,10},{10,8},{9,1... | collective-permute-start | bytes 688136 | tf_op jit(solution)/shard_map/ppermute | solution.py:91
  5.1 4.2 %collective-permute-start = (bf16[640,128]{1,0:T(8,128)(2,1)}, bf16[640,128]{1,0:T(8,128)(2,1)S(1)}, u32[]{:S(2)}, u32[]{:S(2)}) collective-permute-start(bf16[640,128]{1,0:T(8,128)(2,1)} %get-tuple-element.19), channel_id=1, source_target_pairs={{0,0},{1,4},{2,2},{3,6},{4,1},{5,5},{6,3},{7,7},{8,8},{9,12},{10,1... | collective-permute-start | bytes 491528 | tf_op jit(solution)/shard_map/ppermute | solution.py:442
  6.7 11.2 %collective-permute-start.1 = (bf16[640,128]{1,0:T(8,128)(2,1)}, bf16[640,128]{1,0:T(8,128)(2,1)S(1)}, u32[]{:S(2)}, u32[]{:S(2)}) collective-permute-start(bf16[640,128]{1,0:T(8,128)(2,1)} %get-tuple-element.21), channel_id=1, source_target_pairs={{0,8},{1,12},{2,10},{3,14},{4,9},{5,13},{6,11},{7,15},{8,0},{9,4},... | collective-permute-start | bytes 491528 | tf_op jit(solution)/shard_map/ppermute | solution.py:441
  9.3 3.4 %copy-start.1 = (bf16[640,128]{1,0:T(8,128)(2,1)}, bf16[640,128]{1,0:T(8,128)(2,1)S(1)}, u32[]{:S(2)}) copy-start(bf16[640,128]{1,0:T(8,128)(2,1)S(1)} %collective-permute-done.early) | copy-start | bytes 491524
  9.3 8.6 %collective-permute-start.2 = (bf16[512,128]{1,0:T(8,128)(2,1)S(1)}, bf16[512,128]{1,0:T(8,128)(2,1)S(1)}, u32[]{:S(2)}, u32[]{:S(2)}) collective-permute-start(bf16[512,128]{1,0:T(8,128)(2,1)S(1)} %slice.16), channel_id=1, source_target_pairs={{0,2},{2,0},{1,3},{3,1},{4,6},{6,4},{5,7},{7,5},{8,10},{10,8},{9,1... | collective-permute-start | bytes 393224 | tf_op jit(solution)/shard_map/ppermute | solution.py:91
  10.9 12.0 %collective-permute-start.6 = (bf16[14,64,128]{2,1,0:T(8,128)(2,1)S(1)}, bf16[14,64,128]{2,1,0:T(8,128)(2,1)S(1)}, u32[]{:S(2)}, u32[]{:S(2)}) collective-permute-start(bf16[14,64,128]{2,1,0:T(8,128)(2,1)S(1)} %collective-permute-done.5.near), channel_id=1, source_target_pairs={{0,16},{16,0},{1,17},{17,1},{2,18},{18,2},{3,19},{19,3},{4,20},{20... | collective-permute-start | bytes 688136 | tf_op jit(solution)/shard_map/ppermute | solution.py:91
  17.9 0.8 %slice-start = ((bf16[640,128]{1,0:T(8,128)(2,1)}), bf16[128,128]{1,0:T(8,128)(2,1)S(1)}, s32[]{:S(2)}) async-start(bf16[640,128]{1,0:T(8,128)(2,1)} %copy-done.1), calls=%async_computation | async-start | bytes 65536 | tf_op jit(solution)/shard_map/slice | solution.py:452
  17.9 5.0 %collective-permute-start.3 = (bf16[512,128]{1,0:T(8,128)(2,1)S(1)}, bf16[512,128]{1,0:T(8,128)(2,1)S(1)}, u32[]{:S(2)}, u32[]{:S(2)}) collective-permute-start(bf16[512,128]{1,0:T(8,128)(2,1)S(1)} %slice.13), channel_id=1, source_target_pairs={{0,2},{2,0},{1,3},{3,1},{4,6},{6,4},{5,7},{7,5},{8,10},{10,8},{9,1... | collective-permute-start | bytes 393224 | tf_op jit(solution)/shard_map/ppermute | solution.py:91
  18.7 4.3 %copy-start.2 = (bf16[640,128]{1,0:T(8,128)(2,1)S(1)}, bf16[640,128]{1,0:T(8,128)(2,1)}, u32[]{:S(2)}) copy-start(bf16[640,128]{1,0:T(8,128)(2,1)} %copy-done.1) | copy-start | bytes 491524
  18.7 4.3 %collective-permute-start.4 = (bf16[2,2,32,128]{3,2,1,0:T(8,128)(2,1)S(1)}, bf16[2,2,32,128]{3,2,1,0:T(8,128)(2,1)S(1)}, u32[]{:S(2)}, u32[]{:S(2)}) collective-permute-start(bf16[2,2,32,128]{3,2,1,0:T(8,128)(2,1)S(1)} %fusion.6), channel_id=1, source_target_pairs={{0,1},{1,0},{2,3},{3,2},{4,5},{5,4},{6,7},{7,6},{8,9},{9,8},{10,11... | collective-permute-start | bytes 98312 | tf_op jit(solution)/shard_map/ppermute | solution.py:91
  18.7 4.3 %copy-start.4 = (f32[3,128]{1,0:T(4,128)S(1)}, f32[3,128]{1,0:T(4,128)}, u32[]{:S(2)}) copy-start(f32[3,128]{1,0:T(4,128)} %get-tuple-element.28.held) | copy-start | bytes 4612
  23.0 2.4 %copy-start = (bf16[27,128,1,64]{1,3,2,0:T(8,128)(2,1)S(1)}, bf16[27,128,1,64]{1,3,2,0:T(8,128)(2,1)}, u32[]{:S(2)}) copy-start(bf16[27,128,1,64]{1,3,2,0:T(8,128)(2,1)} %param.12) | copy-start | bytes 1327108
  23.4 2.0 %collective-permute-start.7 = (f32[1024,128]{1,0:T(8,128)S(1)}, f32[1024,128]{1,0:T(8,128)S(1)}, u32[]{:S(2)}, u32[]{:S(2)}) collective-permute-start(f32[1024,128]{1,0:T(8,128)S(1)} %shard_map.84.mine), channel_id=1, source_target_pairs={{0,1},{1,0},{2,3},{3,2},{4,5},{5,4},{6,7},{7,6},{8,9},{9,8},{10,11... | collective-permute-start | bytes 1572872 | tf_op jit(solution)/shard_map/ppermute | solution.py:91
  23.5 7.8 %collective-permute-start.9 = (bf16[27,32,128]{2,1,0:T(8,128)(2,1)S(1)}, bf16[27,32,128]{2,1,0:T(8,128)(2,1)S(1)}, u32[]{:S(2)}, u32[]{:S(2)}) collective-permute-start(bf16[27,32,128]{2,1,0:T(8,128)(2,1)S(1)} %shard_map.83.own), channel_id=1, source_target_pairs={{0,2},{2,0},{1,3},{3,1},{4,6},{6,4},{5,7},{7,5},{8,10},{10,8},{9,1... | collective-permute-start | bytes 663560 | tf_op jit(solution)/shard_map/ppermute | solution.py:91
  27.6 3.7 %collective-permute-start.8 = (bf16[2,256,128]{2,1,0:T(8,128)(2,1)S(1)}, bf16[2,256,128]{2,1,0:T(8,128)(2,1)S(1)}, u32[]{:S(2)}, u32[]{:S(2)}) collective-permute-start(bf16[2,256,128]{2,1,0:T(8,128)(2,1)S(1)} %get-tuple-element.40), channel_id=1, source_target_pairs={{0,1},{1,0},{2,3},{3,2},{4,5},{5,4},{6,7},{7,6},{8,9},{9,8},{10,11... | collective-permute-start | bytes 393224 | tf_op jit(solution)/shard_map/ppermute | solution.py:91
  31.4 7.9 %collective-permute-start.10 = (bf16[256,128]{1,0:T(8,128)(2,1)S(1)}, bf16[256,128]{1,0:T(8,128)(2,1)S(1)}, u32[]{:S(2)}, u32[]{:S(2)}) collective-permute-start(bf16[256,128]{1,0:T(8,128)(2,1)S(1)} %get-tuple-element.36), channel_id=1, source_target_pairs={{0,12},{4,8},{8,4},{12,0},{1,13},{5,9},{9,5},{13,1},{2,14},{6,10},... | collective-permute-start | bytes 196616 | tf_op jit(solution)/shard_map/ppermute | solution.py:246
  36.5 5.2 %collective-permute-start.11 = (bf16[256,128]{1,0:T(8,128)(2,1)S(1)}, bf16[256,128]{1,0:T(8,128)(2,1)S(1)}, u32[]{:S(2)}, u32[]{:S(2)}) collective-permute-start(bf16[256,128]{1,0:T(8,128)(2,1)S(1)} %get-tuple-element.38), channel_id=1, source_target_pairs={{0,8},{4,12},{8,0},{12,4},{1,9},{5,13},{9,1},{13,5},{2,10},{6,14},... | collective-permute-start | bytes 196616 | tf_op jit(solution)/shard_map/ppermute | solution.py:246
  36.5 5.5 %collective-permute-start.12 = (bf16[256,128]{1,0:T(8,128)(2,1)S(1)}, bf16[256,128]{1,0:T(8,128)(2,1)S(1)}, u32[]{:S(2)}, u32[]{:S(2)}) collective-permute-start(bf16[256,128]{1,0:T(8,128)(2,1)S(1)} %get-tuple-element.37), channel_id=1, source_target_pairs={{0,4},{4,0},{8,12},{12,8},{1,5},{5,1},{9,13},{13,9},{2,6},{6,2},{1... | collective-permute-start | bytes 196616 | tf_op jit(solution)/shard_map/ppermute | solution.py:246
  42.1 1.3 %collective-permute-start.13 = (bf16[256,128]{1,0:T(8,128)(2,1)S(1)}, bf16[256,128]{1,0:T(8,128)(2,1)S(1)}, u32[]{:S(2)}, u32[]{:S(2)}) collective-permute-start(bf16[256,128]{1,0:T(8,128)(2,1)S(1)} %multiply_convert_fusion), channel_id=1, source_target_pairs={{0,1},{1,0},{2,3},{3,2},{4,5},{5,4},{6,7},{7,6},{8,9},{9,8},{10,11... | collective-permute-start | bytes 196616 | tf_op jit(solution)/shard_map/ppermute | solution.py:91
  45.0 6.9 %collective-permute-start.14 = (bf16[256,128]{1,0:T(8,128)(2,1)S(1)}, bf16[256,128]{1,0:T(8,128)(2,1)S(1)}, u32[]{:S(2)}, u32[]{:S(2)}) collective-permute-start(bf16[256,128]{1,0:T(8,128)(2,1)S(1)} %get-tuple-element.33), channel_id=1, source_target_pairs={{0,12},{4,8},{8,4},{12,0},{1,13},{5,9},{9,5},{13,1},{2,14},{6,10},... | collective-permute-start | bytes 196616 | tf_op jit(solution)/shard_map/ppermute | solution.py:246
  47.1 6.8 %collective-permute-start.15 = (bf16[256,128]{1,0:T(8,128)(2,1)S(1)}, bf16[256,128]{1,0:T(8,128)(2,1)S(1)}, u32[]{:S(2)}, u32[]{:S(2)}) collective-permute-start(bf16[256,128]{1,0:T(8,128)(2,1)S(1)} %get-tuple-element.35), channel_id=1, source_target_pairs={{0,8},{4,12},{8,0},{12,4},{1,9},{5,13},{9,1},{13,5},{2,10},{6,14},... | collective-permute-start | bytes 196616 | tf_op jit(solution)/shard_map/ppermute | solution.py:246
  47.5 6.4 %collective-permute-start.16 = (bf16[256,128]{1,0:T(8,128)(2,1)S(1)}, bf16[256,128]{1,0:T(8,128)(2,1)S(1)}, u32[]{:S(2)}, u32[]{:S(2)}) collective-permute-start(bf16[256,128]{1,0:T(8,128)(2,1)S(1)} %get-tuple-element.34), channel_id=1, source_target_pairs={{0,4},{4,0},{8,12},{12,8},{1,5},{5,1},{9,13},{13,9},{2,6},{6,2},{1... | collective-permute-start | bytes 196616 | tf_op jit(solution)/shard_map/ppermute | solution.py:246

commit v4 on v3

--- a/solution.py
+++ b/solution.py
@@ -175,7 +175,7 @@
 def up_kernel(early, late, early_other, late_other, slabs, held, part):
     s, d, c = (lax.axis_index(a) for a in ("space", "dp", "chan"))
     rows, kb = early_other.shape
-    deep = slabs.shape[2]
+    deep = slabs.shape[1] // 4
     taps = 8
     own_n = rows // taps
     half = part.shape[1]
@@ -191,7 +191,10 @@
                     low = packet[pl.ds(rows + 2 * k * deep, deep)]
                     high = packet[pl.ds(rows + (2 * k + 1) * deep, deep)]
                     mine = jnp.where(c == 0, low, high)
-                    pieces.append(jnp.where(c == parity, mine, slabs[i, k]))
+                    low = slabs[i, pl.ds(2 * k * deep, deep)]
+                    high = slabs[i, pl.ds((2 * k + 1) * deep, deep)]
+                    theirs = jnp.where(c == 0, low, high)
+                    pieces.append(jnp.where(c == parity, mine, theirs))
             lefts.append(jnp.concatenate(pieces, axis=0))
             packet, other = ((early, early_other), (late, late_other))[k]
             pieces = []
@@ -249,7 +252,7 @@
 
 
 def line_routes():
-    early, late = ([], [])
+    early, late, cross = ([], [], [])
     for s in range(4):
         for d in range(2):
             for c in range(2):
@@ -258,7 +261,9 @@
                 skip_target = ((2 + c) * 2 + d) * 2 + s % 2
                 early.append((source, up_target if s < 2 else skip_target))
                 late.append((source, skip_target if s < 2 else up_target))
-    return early, late
+                if s < 2:
+                    cross.append((source, (c * 2 + 1 - d) * 2 + s % 2))
+    return early, late, cross
 
 
 NT = (((1,), (1,)), ((), ()))
@@ -430,40 +435,40 @@
     taps, kb, _, own_n = up_weight.shape
     up_rows = taps * own_n
     first_own = first_weight[:, :, 0, :].transpose(0, 2, 1)
+    up_rows_own = up_weight[:, :, 0, :].transpose(0, 2, 1).reshape(up_rows, kb)
     early, late, near, held = packed(
-        up_weight[:, :, 0, :].transpose(0, 2, 1).reshape(up_rows, kb),
+        up_rows_own,
         coarse.reshape(cells, cin),
         skip.reshape(block, half),
         first_own,
         [bias.reshape(1, half) for bias in (up_bias, first_bias, second_bias)],
     )
-    early_route, late_route = line_routes()
+    early_route, late_route, cross_route = line_routes()
     late = lax.ppermute(late, group, late_route)
+    late_other = swapped(late[:up_rows], "dp")
     early = lax.ppermute(early, group, early_route)
+    early_other = lax.ppermute(up_rows_own, group, cross_route)
     near = swapped(near, "dp")
-    early_other = swapped(early[:up_rows], "dp")
+    late_other, early, early_other = lax.optimization_barrier((late_other, early, early_other))
     far = swapped(near, "groups")
-    late, early_other = lax.optimization_barrier((late, early_other))
-    late_other = swapped(late[:up_rows], "dp")
-    second_raw, early = lax.optimization_barrier((second_weight[:, :, 0, :], early))
+    second_raw, late = lax.optimization_barrier((second_weight[:, :, 0, :], late))
     second_own = dense(second_raw)
     second_own, late_other = lax.optimization_barrier((second_own, late_other))
     second_other = swapped(second_own, "dp")
-    slabs = jnp.stack([early[up_rows:], late[up_rows:]]).reshape(2, 2, 2, cells, kb)
-    theirs = lax.dynamic_index_in_dim(slabs, 1 - c, 2, keepdims=False)
-    slabs, far = lax.optimization_barrier((swapped(theirs, "chan"), far))
+    slabs = swapped(jnp.stack([early[up_rows:], late[up_rows:]]), "chan")
     part = up_part(early, late, early_other, late_other, slabs, held, fx * fy * fz)
+    part, far = lax.optimization_barrier((part, far))
     first = first_conv(part, swapped(part, "chan"), first_own, near, far, held, fx)
     mine = lax.dynamic_index_in_dim(first, c, 0, keepdims=False)
     theirs = lax.dynamic_index_in_dim(first, 1 - c, 0, keepdims=False)
-    theirs, second_other = lax.optimization_barrier((swapped(theirs, "chan"), second_other))
-    chunks = jnp.stack([mine, theirs]).reshape(4, block, half)
+    chunks = jnp.stack([mine, swapped(theirs, "chan")]).reshape(4, block, half)
 
     def chunk_for(plane):
         place = 2 * ((plane // 2) ^ c) + ((plane % 2) ^ d)
         return lax.dynamic_index_in_dim(chunks, place, 0, keepdims=False)
 
     hidden = jax.nn.silu(reduced(chunk_for, s)).astype(jnp.bfloat16)
+    hidden, second_other = lax.optimization_barrier((hidden, second_other))
     hidden = ordered(c, hidden, swapped(hidden, "chan"), 0)
     second = second_conv(hidden, second_own, second_other, held, fx).reshape(4, block, half)
     total = reduced(lambda plane: lax.dynamic_index_in_dim(second, plane, 0, keepdims=False), s)

time: 54.8 us -> 52.2 us (0.953)
  waiting for transfers between devices: 25.6 us -> 21.5 us
  starting transfers between devices: 21.3 us -> 23.1 us
    ppermute x0 -> x1, starting transfers between devices: none -> 2.43 us  [stationary(): early_other = lax.ppermute(up_rows_own, group, cross_route)]
    ppermute x1, waiting for transfers between devices: 5.17 us -> 3.23 us  [stationary(): late = lax.ppermute(late, group, late_route)]
    ppermute x1, starting transfers between devices: 2.59 us -> 4.13 us  [stationary(): late = lax.ppermute(late, group, late_route)]
    ppermute x6, waiting for transfers between devices: 9.3 us -> 7.76 us  [reduced(): term = lax.ppermute(chunk_for(s ^ step), 'space', routes)]
    ppermute x6, starting transfers between devices: 10.2 us -> 8.9 us  [reduced(): term = lax.ppermute(chunk_for(s ^ step), 'space', routes)]
    ppermute x9 -> x8, starting transfers between devices: 6.95 us -> 6.1 us  [swapped(): return lax.ppermute(array, axis, [(0, 1), (1, 0)])]
    ppermute x9 -> x8, waiting for transfers between devices: 11.2 us -> 10.5 us  [swapped(): return lax.ppermute(array, axis, [(0, 1), (1, 0)])]
  transfers between devices with their start and end apart: 17 -> 17, of which waited for: 11 -> 13; matrix products, arithmetic and copies ran while one was open for 0% -> 0% of each run, Pallas kernels for 4% -> 1%
where the time goes in v4:
time: 52.2 us; the launch traced here: 52 us
  starting transfers between devices  23.1 us (44%)
  waiting for transfers between devices  21.5 us (41%)
  Pallas kernels  6.32 us (12%)
  other arithmetic  0.8 us (2%)
    ppermute x8, waiting for transfers between devices, swapped(): return lax.ppermute(array, axis, [(0, 1), (1, 0)])  10.5 us
    ppermute x6, starting transfers between devices, reduced(): term = lax.ppermute(chunk_for(s ^ step), 'space', routes)  8.9 us
    ppermute x6, waiting for transfers between devices, reduced(): term = lax.ppermute(chunk_for(s ^ step), 'space', routes)  7.76 us
    ppermute x8, starting transfers between devices, swapped(): return lax.ppermute(array, axis, [(0, 1), (1, 0)])  6.1 us
    ppermute x1, starting transfers between devices, stationary(): late = lax.ppermute(late, group, late_route)  4.13 us
    ppermute x1, waiting for transfers between devices, stationary(): late = lax.ppermute(late, group, late_route)  3.23 us
    ppermute x1, starting transfers between devices, stationary(): early_other = lax.ppermute(up_rows_own, group, cross_route)  2.43 us
    pallas_call x1, Pallas kernels, first_conv(): pl.pallas_call(first_kernel, out_shape=jax.ShapeDtypeStruct((2, 2, cells...  2.16 us
  transfers between devices with their start and end apart: 17, of which 13 were waited for; matrix products, arithmetic and copies ran while one was open for 0% of the time, Pallas kernels for 1%

profile of v4, /device:TPU:0, one launch (start us, length us, event | category | flops | bytes accessed | tf_op | source)
XLA Modules:
  0.0 52.0 jit_solution(1457904078895702469)
XLA Ops:
  0.0 0.0 copy-start.3
  0.0 0.0 copy-start.1
  0.0 2.1 %shard_map.82 = (bf16[640,128]{1,0:T(8,128)(2,1)}, bf16[640,128]{1,0:T(8,128)(2,1)}, bf16[14,64,128]{2,1,0:T(8,128)(2,1)}, f32[3,128]{1,0:T(4,128)}) custom-call(bf16[512,128]{1,0:T(8,128)(2,1)} %bitcast.53, bf16[32,512]{1,0:T(8,128)(2,1)} %bitcast.57, bf16[256,128]{1,0:T(8,128)(2,1)} %bitcast.56, bf16[27,64,128]{2,1,0:T(8,128)(2,1)} %bitcast.46, ...), custom_call_target="tpu_custom_call" | custom-call | tf_op jit(solution)/shard_map/pallas_call | solution.py:148
  2.1 4.1 %collective-permute-start = (bf16[640,128]{1,0:T(8,128)(2,1)}, bf16[640,128]{1,0:T(8,128)(2,1)S(1)}, u32[]{:S(2)}, u32[]{:S(2)}) collective-permute-start(bf16[640,128]{1,0:T(8,128)(2,1)} %get-tuple-element.20), channel_id=1, source_target_pairs={{0,8},{1,12},{2,10},{3,14},{4,9},{5,13},{6,11},{7,15},{8,0},{9,4},... | collective-permute-start | bytes 491528 | tf_op jit(solution)/shard_map/ppermute | solution.py:447
  6.3 1.5 %collective-permute-start.5 = (bf16[14,64,128]{2,1,0:T(8,128)(2,1)}, bf16[14,64,128]{2,1,0:T(8,128)(2,1)S(1)}, u32[]{:S(2)}, u32[]{:S(2)}) collective-permute-start(bf16[14,64,128]{2,1,0:T(8,128)(2,1)} %get-tuple-element.29), channel_id=1, source_target_pairs={{0,2},{2,0},{1,3},{3,1},{4,6},{6,4},{5,7},{7,5},{8,10},{10,8},{9,1... | collective-permute-start | bytes 688136 | tf_op jit(solution)/shard_map/ppermute | solution.py:91
  7.8 1.6 %collective-permute-start.2 = (bf16[640,128]{1,0:T(8,128)(2,1)}, bf16[640,128]{1,0:T(8,128)(2,1)S(1)}, u32[]{:S(2)}, u32[]{:S(2)}) collective-permute-start(bf16[640,128]{1,0:T(8,128)(2,1)} %get-tuple-element.21), channel_id=1, source_target_pairs={{0,0},{1,4},{2,2},{3,6},{4,1},{5,5},{6,3},{7,7},{8,8},{9,12},{10,1... | collective-permute-start | bytes 491528 | tf_op jit(solution)/shard_map/ppermute | solution.py:449
  9.3 0.0 copy-done.3
  9.3 2.4 %collective-permute-start.3 = (bf16[512,128]{1,0:T(8,128)(2,1)S(1)}, bf16[512,128]{1,0:T(8,128)(2,1)S(1)}, u32[]{:S(2)}, u32[]{:S(2)}) collective-permute-start(bf16[512,128]{1,0:T(8,128)(2,1)S(1)} %bitcast.54), channel_id=1, source_target_pairs={{0,2},{1,6},{2,0},{3,4},{4,3},{5,7},{6,1},{7,5},{16,18},{17,22},{1... | collective-permute-start | bytes 393224 | tf_op jit(solution)/shard_map/ppermute | solution.py:450
  11.8 3.2 %collective-permute-done.late = bf16[640,128]{1,0:T(8,128)(2,1)S(1)} collective-permute-done((bf16[640,128]{1,0:T(8,128)(2,1)}, bf16[640,128]{1,0:T(8,128)(2,1)S(1)}, u32[]{:S(2)}, u32[]{:S(2)}) %collective-permute-start) | collective-permute-done | bytes 163872 | tf_op jit(solution)/shard_map/ppermute | solution.py:447
  15.0 1.6 %collective-permute-start.1 = (bf16[512,128]{1,0:T(8,128)(2,1)S(1)}, bf16[512,128]{1,0:T(8,128)(2,1)S(1)}, u32[]{:S(2)}, u32[]{:S(2)}) collective-permute-start(bf16[512,128]{1,0:T(8,128)(2,1)S(1)} %slice.12), channel_id=1, source_target_pairs={{0,2},{2,0},{1,3},{3,1},{4,6},{6,4},{5,7},{7,5},{8,10},{10,8},{9,1... | collective-permute-start | bytes 393224 | tf_op jit(solution)/shard_map/ppermute | solution.py:91
  16.6 0.0 collective-permute-done.5.near
  16.6 1.5 %collective-permute-start.6 = (bf16[14,64,128]{2,1,0:T(8,128)(2,1)S(1)}, bf16[14,64,128]{2,1,0:T(8,128)(2,1)S(1)}, u32[]{:S(2)}, u32[]{:S(2)}) collective-permute-start(bf16[14,64,128]{2,1,0:T(8,128)(2,1)S(1)} %collective-permute-done.5.near), channel_id=1, source_target_pairs={{0,16},{16,0},{1,17},{17,1},{2,18},{18,2},{3,19},{19,3},{4,20},{20... | collective-permute-start | bytes 688136 | tf_op jit(solution)/shard_map/ppermute | solution.py:91
  18.1 0.0 collective-permute-done.3.early_other
  18.1 0.0 collective-permute-done.2.early
  18.1 2.9 %collective-permute-done.1.late_other = bf16[512,128]{1,0:T(8,128)(2,1)S(1)} collective-permute-done((bf16[512,128]{1,0:T(8,128)(2,1)S(1)}, bf16[512,128]{1,0:T(8,128)(2,1)S(1)}, u32[]{:S(2)}, u32[]{:S(2)}) %collective-permute-start.1) | collective-permute-done | bytes 131104 | tf_op jit(solution)/shard_map/ppermute | solution.py:91
  21.0 0.1 collective-permute-start.4
  21.1 0.0 copy-done.1
  21.1 0.0 copy-start.2
  21.1 0.1 shard_map.83.own
  21.2 1.1 %collective-permute-done.4.slabs = bf16[2,128,128]{2,1,0:T(8,128)(2,1)S(1)} collective-permute-done((bf16[2,128,128]{2,1,0:T(8,128)(2,1)S(1)}, bf16[2,128,128]{2,1,0:T(8,128)(2,1)S(1)}, u32[]{:S(2)}, u32[]{:S(2)}) %collective-permute-start.4) | collective-permute-done | bytes 65568 | tf_op jit(solution)/shard_map/ppermute | solution.py:91
  22.3 0.0 copy-done.2
  22.3 0.4 shard_map.84.mine
  22.7 0.2 collective-permute-done.6.far
  23.0 0.0 collective-permute-start.7
  23.0 1.9 %collective-permute-done.7.theirs = f32[1024,128]{1,0:T(8,128)S(1)} collective-permute-done((f32[1024,128]{1,0:T(8,128)S(1)}, f32[1024,128]{1,0:T(8,128)S(1)}, u32[]{:S(2)}, u32[]{:S(2)}) %collective-permute-start.7) | collective-permute-done | bytes 524320 | tf_op jit(solution)/shard_map/ppermute | solution.py:91
  24.9 0.0 copy-done
  24.9 2.2 %shard_map.85 = bf16[2,2,256,128]{3,2,1,0:T(8,128)(2,1)S(1)} custom-call(f32[1024,128]{1,0:T(8,128)S(1)} %shard_map.84.mine, f32[1024,128]{1,0:T(8,128)S(1)} %collective-permute-done.7.theirs, bf16[27,64,128]{2,1,0:T(8,128)(2,1)S(1)} %bitcast.47, bf16[14,64,128]{2,1,0:T(8,128)(2,1)S(1)} %collective-permute-done.5.near, ...), custom_call_target="tpu_custom_call" | custom-call | tf_op jit(solution)/shard_map/pallas_call | solution.py:335
  27.1 0.2 collective-permute-start.8
  27.3 1.2 %collective-permute-done.8 = bf16[2,256,128]{2,1,0:T(8,128)(2,1)S(1)} collective-permute-done((bf16[2,256,128]{2,1,0:T(8,128)(2,1)S(1)}, bf16[2,256,128]{2,1,0:T(8,128)(2,1)S(1)}, u32[]{:S(2)}, u32[]{:S(2)}) %collective-permute-start.8) | collective-permute-done | bytes 131104 | tf_op jit(solution)/shard_map/ppermute | solution.py:91
  28.6 1.5 %collective-permute-start.10 = (bf16[256,128]{1,0:T(8,128)(2,1)S(1)}, bf16[256,128]{1,0:T(8,128)(2,1)S(1)}, u32[]{:S(2)}, u32[]{:S(2)}) collective-permute-start(bf16[256,128]{1,0:T(8,128)(2,1)S(1)} %get-tuple-element.40), channel_id=1, source_target_pairs={{0,8},{4,12},{8,0},{12,4},{1,9},{5,13},{9,1},{13,5},{2,10},{6,14},... | collective-permute-start | bytes 196616 | tf_op jit(solution)/shard_map/ppermute | solution.py:249
  30.1 1.4 %collective-permute-start.11 = (bf16[256,128]{1,0:T(8,128)(2,1)S(1)}, bf16[256,128]{1,0:T(8,128)(2,1)S(1)}, u32[]{:S(2)}, u32[]{:S(2)}) collective-permute-start(bf16[256,128]{1,0:T(8,128)(2,1)S(1)} %get-tuple-element.39), channel_id=1, source_target_pairs={{0,4},{4,0},{8,12},{12,8},{1,5},{5,1},{9,13},{13,9},{2,6},{6,2},{1... | collective-permute-start | bytes 196616 | tf_op jit(solution)/shard_map/ppermute | solution.py:249
  31.5 1.5 %collective-permute-start.9 = (bf16[256,128]{1,0:T(8,128)(2,1)S(1)}, bf16[256,128]{1,0:T(8,128)(2,1)S(1)}, u32[]{:S(2)}, u32[]{:S(2)}) collective-permute-start(bf16[256,128]{1,0:T(8,128)(2,1)S(1)} %get-tuple-element.38), channel_id=1, source_target_pairs={{0,12},{4,8},{8,4},{12,0},{1,13},{5,9},{9,5},{13,1},{2,14},{6,10},... | collective-permute-start | bytes 196616 | tf_op jit(solution)/shard_map/ppermute | solution.py:249
  33.0 1.3 %collective-permute-start.12 = (bf16[27,32,128]{2,1,0:T(8,128)(2,1)S(1)}, bf16[27,32,128]{2,1,0:T(8,128)(2,1)S(1)}, u32[]{:S(2)}, u32[]{:S(2)}) collective-permute-start(bf16[27,32,128]{2,1,0:T(8,128)(2,1)S(1)} %shard_map.83.own), channel_id=1, source_target_pairs={{0,2},{2,0},{1,3},{3,1},{4,6},{6,4},{5,7},{7,5},{8,10},{10,8},{9,1... | collective-permute-start | bytes 663560 | tf_op jit(solution)/shard_map/ppermute | solution.py:91
  34.3 1.0 %collective-permute-done.10 = bf16[256,128]{1,0:T(8,128)(2,1)S(1)} collective-permute-done((bf16[256,128]{1,0:T(8,128)(2,1)S(1)}, bf16[256,128]{1,0:T(8,128)(2,1)S(1)}, u32[]{:S(2)}, u32[]{:S(2)}) %collective-permute-start.10) | collective-permute-done | bytes 65568 | tf_op jit(solution)/shard_map/ppermute | solution.py:249
  35.2 0.2 collective-permute-done.11
  35.5 2.2 %collective-permute-done.9 = bf16[256,128]{1,0:T(8,128)(2,1)S(1)} collective-permute-done((bf16[256,128]{1,0:T(8,128)(2,1)S(1)}, bf16[256,128]{1,0:T(8,128)(2,1)S(1)}, u32[]{:S(2)}, u32[]{:S(2)}) %collective-permute-start.9) | collective-permute-done | bytes 65568 | tf_op jit(solution)/shard_map/ppermute | solution.py:249
  37.6 0.1 multiply_convert_fusion
  37.7 1.9 %collective-permute-done.12.other = bf16[27,32,128]{2,1,0:T(8,128)(2,1)S(1)} collective-permute-done((bf16[27,32,128]{2,1,0:T(8,128)(2,1)S(1)}, bf16[27,32,128]{2,1,0:T(8,128)(2,1)S(1)}, u32[]{:S(2)}, u32[]{:S(2)}) %collective-permute-start.12) | collective-permute-done | bytes 221216 | tf_op jit(solution)/shard_map/ppermute | solution.py:91
  39.7 0.0 collective-permute-start.13
  39.7 1.3 %collective-permute-done.13 = bf16[256,128]{1,0:T(8,128)(2,1)S(1)} collective-permute-done((bf16[256,128]{1,0:T(8,128)(2,1)S(1)}, bf16[256,128]{1,0:T(8,128)(2,1)S(1)}, u32[]{:S(2)}, u32[]{:S(2)}) %collective-permute-start.13) | collective-permute-done | bytes 65568 | tf_op jit(solution)/shard_map/ppermute | solution.py:91
  40.9 1.5 %shard_map.86 = bf16[1024,128]{1,0:T(8,128)(2,1)S(1)} custom-call(bf16[2,256,128]{2,1,0:T(8,128)(2,1)S(1)} %pad_maximum_fusion.1.hidden, bf16[27,32,128]{2,1,0:T(8,128)(2,1)S(1)} %shard_map.83.own, bf16[27,32,128]{2,1,0:T(8,128)(2,1)S(1)} %collective-permute-done.12.other, f32[3,128]{1,0:T(4,128)S(1)} %copy-done.2), custom_call_target="tpu_custom_call" | custom-call | tf_op jit(solution)/shard_map/pallas_call | solution.py:412
  42.5 2.4 %collective-permute-start.14 = (bf16[256,128]{1,0:T(8,128)(2,1)S(1)}, bf16[256,128]{1,0:T(8,128)(2,1)S(1)}, u32[]{:S(2)}, u32[]{:S(2)}) collective-permute-start(bf16[256,128]{1,0:T(8,128)(2,1)S(1)} %get-tuple-element.35), channel_id=1, source_target_pairs={{0,12},{4,8},{8,4},{12,0},{1,13},{5,9},{9,5},{13,1},{2,14},{6,10},... | collective-permute-start | bytes 196616 | tf_op jit(solution)/shard_map/ppermute | solution.py:249
  44.9 0.0 collective-permute-start.15
  44.9 2.1 %collective-permute-start.16 = (bf16[256,128]{1,0:T(8,128)(2,1)S(1)}, bf16[256,128]{1,0:T(8,128)(2,1)S(1)}, u32[]{:S(2)}, u32[]{:S(2)}) collective-permute-start(bf16[256,128]{1,0:T(8,128)(2,1)S(1)} %get-tuple-element.36), channel_id=1, source_target_pairs={{0,4},{4,0},{8,12},{12,8},{1,5},{5,1},{9,13},{13,9},{2,6},{6,2},{1... | collective-permute-start | bytes 196616 | tf_op jit(solution)/shard_map/ppermute | solution.py:249
  47.0 2.4 %collective-permute-done.14 = bf16[256,128]{1,0:T(8,128)(2,1)S(1)} collective-permute-done((bf16[256,128]{1,0:T(8,128)(2,1)S(1)}, bf16[256,128]{1,0:T(8,128)(2,1)S(1)}, u32[]{:S(2)}, u32[]{:S(2)}) %collective-permute-start.14) | collective-permute-done | bytes 65568 | tf_op jit(solution)/shard_map/ppermute | solution.py:249
  49.3 2.0 %collective-permute-done.15 = bf16[256,128]{1,0:T(8,128)(2,1)S(1)} collective-permute-done((bf16[256,128]{1,0:T(8,128)(2,1)S(1)}, bf16[256,128]{1,0:T(8,128)(2,1)S(1)}, u32[]{:S(2)}, u32[]{:S(2)}) %collective-permute-start.15) | collective-permute-done | bytes 65568 | tf_op jit(solution)/shard_map/ppermute | solution.py:249
  51.3 0.0 collective-permute-done.16
  51.3 0.7 %fusion.2 = bf16[256,128]{1,0:T(8,128)(2,1)} fusion(bf16[256,128]{1,0:T(8,128)(2,1)S(1)} %collective-permute-done.16, bf16[256,128]{1,0:T(8,128)(2,1)S(1)} %collective-permute-done.15, bf16[256,128]{1,0:T(8,128)(2,1)S(1)} %collective-permute-done.14, bf16[4,256,128]{2,1,0:T(8,128)(2,1)S(1)} %bitcast.49, s32[]{:T(128)S(6)} %select_n.93), kind=kLoop, calls=%fused_computation.5 | loop fusion | flops 262144 | bytes 327684 | tf_op jit(solution)/shard_map/convert_element_type | solution.py:475
  (10 shorter events, 0.2 us)
Async XLA Ops:
  0.0 9.3 %copy-start.3 = (bf16[8,128,1,64]{1,3,2,0:T(8,128)(2,1)S(1)}, bf16[8,128,1,64]{1,3,2,0:T(8,128)(2,1)}, u32[]{:S(2)}) copy-start(bf16[8,128,1,64]{1,3,2,0:T(8,128)(2,1)} %param.10) | copy-start | bytes 393220
  0.0 21.1 %copy-start.1 = (bf16[27,64,1,64]{3,1,2,0:T(8,128)(2,1)S(1)}, bf16[27,64,1,64]{3,1,2,0:T(8,128)(2,1)}, u32[]{:S(2)}) copy-start(bf16[27,64,1,64]{3,1,2,0:T(8,128)(2,1)} %param.14) | copy-start | bytes 663556
  2.1 12.9 %collective-permute-start = (bf16[640,128]{1,0:T(8,128)(2,1)}, bf16[640,128]{1,0:T(8,128)(2,1)S(1)}, u32[]{:S(2)}, u32[]{:S(2)}) collective-permute-start(bf16[640,128]{1,0:T(8,128)(2,1)} %get-tuple-element.20), channel_id=1, source_target_pairs={{0,8},{1,12},{2,10},{3,14},{4,9},{5,13},{6,11},{7,15},{8,0},{9,4},... | collective-permute-start | bytes 491528 | tf_op jit(solution)/shard_map/ppermute | solution.py:447
  6.3 10.3 %collective-permute-start.5 = (bf16[14,64,128]{2,1,0:T(8,128)(2,1)}, bf16[14,64,128]{2,1,0:T(8,128)(2,1)S(1)}, u32[]{:S(2)}, u32[]{:S(2)}) collective-permute-start(bf16[14,64,128]{2,1,0:T(8,128)(2,1)} %get-tuple-element.29), channel_id=1, source_target_pairs={{0,2},{2,0},{1,3},{3,1},{4,6},{6,4},{5,7},{7,5},{8,10},{10,8},{9,1... | collective-permute-start | bytes 688136 | tf_op jit(solution)/shard_map/ppermute | solution.py:91
  7.8 10.3 %collective-permute-start.2 = (bf16[640,128]{1,0:T(8,128)(2,1)}, bf16[640,128]{1,0:T(8,128)(2,1)S(1)}, u32[]{:S(2)}, u32[]{:S(2)}) collective-permute-start(bf16[640,128]{1,0:T(8,128)(2,1)} %get-tuple-element.21), channel_id=1, source_target_pairs={{0,0},{1,4},{2,2},{3,6},{4,1},{5,5},{6,3},{7,7},{8,8},{9,12},{10,1... | collective-permute-start | bytes 491528 | tf_op jit(solution)/shard_map/ppermute | solution.py:449
  9.3 8.8 %collective-permute-start.3 = (bf16[512,128]{1,0:T(8,128)(2,1)S(1)}, bf16[512,128]{1,0:T(8,128)(2,1)S(1)}, u32[]{:S(2)}, u32[]{:S(2)}) collective-permute-start(bf16[512,128]{1,0:T(8,128)(2,1)S(1)} %bitcast.54), channel_id=1, source_target_pairs={{0,2},{1,6},{2,0},{3,4},{4,3},{5,7},{6,1},{7,5},{16,18},{17,22},{1... | collective-permute-start | bytes 393224 | tf_op jit(solution)/shard_map/ppermute | solution.py:450
  15.0 6.0 %collective-permute-start.1 = (bf16[512,128]{1,0:T(8,128)(2,1)S(1)}, bf16[512,128]{1,0:T(8,128)(2,1)S(1)}, u32[]{:S(2)}, u32[]{:S(2)}) collective-permute-start(bf16[512,128]{1,0:T(8,128)(2,1)S(1)} %slice.12), channel_id=1, source_target_pairs={{0,2},{2,0},{1,3},{3,1},{4,6},{6,4},{5,7},{7,5},{8,10},{10,8},{9,1... | collective-permute-start | bytes 393224 | tf_op jit(solution)/shard_map/ppermute | solution.py:91
  16.6 6.4 %collective-permute-start.6 = (bf16[14,64,128]{2,1,0:T(8,128)(2,1)S(1)}, bf16[14,64,128]{2,1,0:T(8,128)(2,1)S(1)}, u32[]{:S(2)}, u32[]{:S(2)}) collective-permute-start(bf16[14,64,128]{2,1,0:T(8,128)(2,1)S(1)} %collective-permute-done.5.near), channel_id=1, source_target_pairs={{0,16},{16,0},{1,17},{17,1},{2,18},{18,2},{3,19},{19,3},{4,20},{20... | collective-permute-start | bytes 688136 | tf_op jit(solution)/shard_map/ppermute | solution.py:91
  21.0 1.3 %collective-permute-start.4 = (bf16[2,128,128]{2,1,0:T(8,128)(2,1)S(1)}, bf16[2,128,128]{2,1,0:T(8,128)(2,1)S(1)}, u32[]{:S(2)}, u32[]{:S(2)}) collective-permute-start(bf16[2,128,128]{2,1,0:T(8,128)(2,1)S(1)} %pad_maximum_fusion.2), channel_id=1, source_target_pairs={{0,1},{1,0},{2,3},{3,2},{4,5},{5,4},{6,7},{7,6},{8,9},{9,8},{10,11... | collective-permute-start | bytes 196616 | tf_op jit(solution)/shard_map/ppermute | solution.py:91
  21.1 1.2 %copy-start.2 = (f32[3,128]{1,0:T(4,128)S(1)}, f32[3,128]{1,0:T(4,128)}, u32[]{:S(2)}) copy-start(f32[3,128]{1,0:T(4,128)} %get-tuple-element.28.held) | copy-start | bytes 4612
  22.3 2.6 %copy-start = (bf16[27,128,1,64]{1,3,2,0:T(8,128)(2,1)S(1)}, bf16[27,128,1,64]{1,3,2,0:T(8,128)(2,1)}, u32[]{:S(2)}) copy-start(bf16[27,128,1,64]{1,3,2,0:T(8,128)(2,1)} %param.12) | copy-start | bytes 1327108
  23.0 1.9 %collective-permute-start.7 = (f32[1024,128]{1,0:T(8,128)S(1)}, f32[1024,128]{1,0:T(8,128)S(1)}, u32[]{:S(2)}, u32[]{:S(2)}) collective-permute-start(f32[1024,128]{1,0:T(8,128)S(1)} %shard_map.84.mine), channel_id=1, source_target_pairs={{0,1},{1,0},{2,3},{3,2},{4,5},{5,4},{6,7},{7,6},{8,9},{9,8},{10,11... | collective-permute-start | bytes 1572872 | tf_op jit(solution)/shard_map/ppermute | solution.py:91
  27.1 1.4 %collective-permute-start.8 = (bf16[2,256,128]{2,1,0:T(8,128)(2,1)S(1)}, bf16[2,256,128]{2,1,0:T(8,128)(2,1)S(1)}, u32[]{:S(2)}, u32[]{:S(2)}) collective-permute-start(bf16[2,256,128]{2,1,0:T(8,128)(2,1)S(1)} %get-tuple-element.42), channel_id=1, source_target_pairs={{0,1},{1,0},{2,3},{3,2},{4,5},{5,4},{6,7},{7,6},{8,9},{9,8},{10,11... | collective-permute-start | bytes 393224 | tf_op jit(solution)/shard_map/ppermute | solution.py:91
  28.6 6.7 %collective-permute-start.10 = (bf16[256,128]{1,0:T(8,128)(2,1)S(1)}, bf16[256,128]{1,0:T(8,128)(2,1)S(1)}, u32[]{:S(2)}, u32[]{:S(2)}) collective-permute-start(bf16[256,128]{1,0:T(8,128)(2,1)S(1)} %get-tuple-element.40), channel_id=1, source_target_pairs={{0,8},{4,12},{8,0},{12,4},{1,9},{5,13},{9,1},{13,5},{2,10},{6,14},... | collective-permute-start | bytes 196616 | tf_op jit(solution)/shard_map/ppermute | solution.py:249
  30.1 5.4 %collective-permute-start.11 = (bf16[256,128]{1,0:T(8,128)(2,1)S(1)}, bf16[256,128]{1,0:T(8,128)(2,1)S(1)}, u32[]{:S(2)}, u32[]{:S(2)}) collective-permute-start(bf16[256,128]{1,0:T(8,128)(2,1)S(1)} %get-tuple-element.39), channel_id=1, source_target_pairs={{0,4},{4,0},{8,12},{12,8},{1,5},{5,1},{9,13},{13,9},{2,6},{6,2},{1... | collective-permute-start | bytes 196616 | tf_op jit(solution)/shard_map/ppermute | solution.py:249
  31.5 6.2 %collective-permute-start.9 = (bf16[256,128]{1,0:T(8,128)(2,1)S(1)}, bf16[256,128]{1,0:T(8,128)(2,1)S(1)}, u32[]{:S(2)}, u32[]{:S(2)}) collective-permute-start(bf16[256,128]{1,0:T(8,128)(2,1)S(1)} %get-tuple-element.38), channel_id=1, source_target_pairs={{0,12},{4,8},{8,4},{12,0},{1,13},{5,9},{9,5},{13,1},{2,14},{6,10},... | collective-permute-start | bytes 196616 | tf_op jit(solution)/shard_map/ppermute | solution.py:249
  33.0 6.6 %collective-permute-start.12 = (bf16[27,32,128]{2,1,0:T(8,128)(2,1)S(1)}, bf16[27,32,128]{2,1,0:T(8,128)(2,1)S(1)}, u32[]{:S(2)}, u32[]{:S(2)}) collective-permute-start(bf16[27,32,128]{2,1,0:T(8,128)(2,1)S(1)} %shard_map.83.own), channel_id=1, source_target_pairs={{0,2},{2,0},{1,3},{3,1},{4,6},{6,4},{5,7},{7,5},{8,10},{10,8},{9,1... | collective-permute-start | bytes 663560 | tf_op jit(solution)/shard_map/ppermute | solution.py:91
  39.7 1.3 %collective-permute-start.13 = (bf16[256,128]{1,0:T(8,128)(2,1)S(1)}, bf16[256,128]{1,0:T(8,128)(2,1)S(1)}, u32[]{:S(2)}, u32[]{:S(2)}) collective-permute-start(bf16[256,128]{1,0:T(8,128)(2,1)S(1)} %multiply_convert_fusion), channel_id=1, source_target_pairs={{0,1},{1,0},{2,3},{3,2},{4,5},{5,4},{6,7},{7,6},{8,9},{9,8},{10,11... | collective-permute-start | bytes 196616 | tf_op jit(solution)/shard_map/ppermute | solution.py:91
  42.5 6.8 %collective-permute-start.14 = (bf16[256,128]{1,0:T(8,128)(2,1)S(1)}, bf16[256,128]{1,0:T(8,128)(2,1)S(1)}, u32[]{:S(2)}, u32[]{:S(2)}) collective-permute-start(bf16[256,128]{1,0:T(8,128)(2,1)S(1)} %get-tuple-element.35), channel_id=1, source_target_pairs={{0,12},{4,8},{8,4},{12,0},{1,13},{5,9},{9,5},{13,1},{2,14},{6,10},... | collective-permute-start | bytes 196616 | tf_op jit(solution)/shard_map/ppermute | solution.py:249
  44.9 6.5 %collective-permute-start.15 = (bf16[256,128]{1,0:T(8,128)(2,1)S(1)}, bf16[256,128]{1,0:T(8,128)(2,1)S(1)}, u32[]{:S(2)}, u32[]{:S(2)}) collective-permute-start(bf16[256,128]{1,0:T(8,128)(2,1)S(1)} %get-tuple-element.37), channel_id=1, source_target_pairs={{0,8},{4,12},{8,0},{12,4},{1,9},{5,13},{9,1},{13,5},{2,10},{6,14},... | collective-permute-start | bytes 196616 | tf_op jit(solution)/shard_map/ppermute | solution.py:249
  44.9 6.5 %collective-permute-start.16 = (bf16[256,128]{1,0:T(8,128)(2,1)S(1)}, bf16[256,128]{1,0:T(8,128)(2,1)S(1)}, u32[]{:S(2)}, u32[]{:S(2)}) collective-permute-start(bf16[256,128]{1,0:T(8,128)(2,1)S(1)} %get-tuple-element.36), channel_id=1, source_target_pairs={{0,4},{4,0},{8,12},{12,8},{1,5},{5,1},{9,13},{13,9},{2,6},{6,2},{1... | collective-permute-start | bytes 196616 | tf_op jit(solution)/shard_map/ppermute | solution.py:249

commit v5 on v4

--- a/solution.py
+++ b/solution.py
@@ -179,7 +179,9 @@
     taps = 8
     own_n = rows // taps
     half = part.shape[1]
-    block = part.shape[0] // 4
+    all_cells = part.shape[0] - 8
+    block = all_cells // 4
+    part[pl.ds(all_cells, 8)] = jnp.broadcast_to(held[1:2], (8, half))
 
     @pl.when(s < 2)
     def _():
@@ -235,20 +237,28 @@
 def up_part(early, late, early_other, late_other, slabs, held, cells):
     return pl.pallas_call(
         up_kernel,
-        out_shape=jax.ShapeDtypeStruct((cells, held.shape[1]), jnp.float32),
+        out_shape=jax.ShapeDtypeStruct((cells + 8, held.shape[1]), jnp.float32),
         in_specs=[pl.BlockSpec(memory_space=pltpu.VMEM)] * 6,
         out_specs=pl.BlockSpec(memory_space=pltpu.VMEM),
         compiler_params=pltpu.CompilerParams(vmem_limit_bytes=32 * 2**20),
     )(early, late, early_other, late_other, slabs, held)
 
 
-def reduced(chunk_for, s):
-    total = chunk_for(s).astype(jnp.float32)
-    for step in (3, 2, 1):
-        routes = [(i, i ^ step) for i in range(4)]
-        term = lax.ppermute(chunk_for(s ^ step), "space", routes)
-        total = total + term.astype(jnp.float32)
-    return total
+def terms_of(chunks):
+    terms = []
+    for step, chunk in chunks:
+        terms.append(lax.ppermute(chunk, "space", [(i, i ^ step) for i in range(4)]))
+    return terms
+
+
+def summed(start, terms):
+    for term in terms:
+        start = start + term.astype(jnp.float32)
+    return start
+
+
+def pick(pair, index):
+    return lax.dynamic_index_in_dim(pair, index, 0, keepdims=False)
 
 
 def line_routes():
@@ -270,156 +280,182 @@
 NN = (((1,), (0,)), ((), ()))
 
 
-def first_kernel(mine, theirs, own, near, far, held, out, even, odd):
+def build_taps(planes_of, even, odd):
     planes = even.shape[0] - 2
     rows, width = even.shape[1:]
-    half = mine.shape[1]
-    quad = planes // 4
     blank = jnp.zeros((1,) + odd.shape[1:], odd.dtype)
     odd[0:1] = blank
     odd[planes + 1 : planes + 2] = blank
     even[0:1] = blank[:, :rows]
     even[planes + 1 : planes + 2] = blank[:, :rows]
-    cell = lax.broadcasted_iota(jnp.int32, (rows, half), 0) % 8
     edge = jnp.zeros((8, width), jnp.float32)
-    for x in range(planes):
-        plane = mine[x * rows : (x + 1) * rows] + theirs[x * rows : (x + 1) * rows]
-        plane = plane.astype(jnp.bfloat16).astype(jnp.float32)
-        below = jnp.where(cell == 0, 0.0, pltpu.roll(plane, 1, 0))
-        above = jnp.where(cell == 7, 0.0, pltpu.roll(plane, rows - 1, 0))
-        taps = jnp.concatenate([below, plane, above], axis=1)
+    for x, taps in planes_of():
         even[x + 1] = taps.astype(jnp.bfloat16)
         odd[x + 1] = jnp.concatenate([edge, taps, edge], axis=0).astype(jnp.bfloat16)
-    s, d, g = (lax.axis_index(a) for a in ("space", "dp", "groups"))
-    swap = half // 2
-    bias = jnp.broadcast_to(held[1:2], (8, half))
-    bias = jnp.where(d == 0, bias, pltpu.roll(bias, swap, 1))[0:1]
-    bias = bias * jnp.where(s == 0, 1.0, 0.0)
+
+
+def half_product(q, even, odd, right_of, form):
+    planes = even.shape[0] - 2
+    rows = even.shape[1]
+    total = None
+    for dx in range(3):
+        for dy in range(3):
+            at = pl.ds(q * (planes // 2) + dx, planes // 2)
+            left = even[at] if dy == 1 else odd[at, pl.ds(8 * dy, rows)]
+            right = right_of(dx * 3 + dy)
+            width = right.shape[1] if form is NT else right.shape[0]
+            left = left.reshape(planes // 2 * rows, left.shape[2])[:, :width]
+            term = lax.dot_general(left, right, form, preferred_element_type=jnp.float32)
+            total = term if total is None else total + term
+    return total
+
+
+def first_right(own, near, far):
+    g = lax.axis_index("groups")
     span, taps = (near.shape[0], own.shape[0])
-    other = []
-    for tap in range(taps):
+
+    def other(tap):
         if tap < span:
             lower, upper = (near[tap], far[tap])
         else:
             lower, upper = (far[tap - taps + span], near[tap - taps + span])
         if tap == span - 1:
             upper = near[0]
-        other.append(jnp.where(g == 0, lower, upper))
+        return jnp.where(g == 0, lower, upper)
+
+    def right_of(group):
+        tap = 3 * group
+        return jnp.concatenate(
+            [jnp.concatenate([own[tap + i], other(tap + i)], axis=0) for i in range(3)], axis=1
+        )
+
+    return right_of
+
+
+def first_out(total, out, q):
+    half = total.shape[1]
+    swap = half // 2
+    low, high = (total[: total.shape[0] // 2], total[total.shape[0] // 2 :])
+    lane = lax.broadcasted_iota(jnp.int32, low.shape, 1)
+    out[q, 0] = jnp.where(lane < swap, low, pltpu.roll(high, swap, 1)).astype(jnp.bfloat16)
+    out[q, 1] = jnp.where(lane < swap, pltpu.roll(low, swap, 1), high).astype(jnp.bfloat16)
+
+
+def first_kernel(mine, theirs, own, near, far, out, tile, even, odd):
+    s, c = (lax.axis_index(a) for a in ("space", "chan"))
+    rows = even.shape[1]
+    half = mine.shape[1]
+    cells = mine.shape[0] - 8
+    cell = lax.broadcasted_iota(jnp.int32, (rows, half), 0) % 8
+
+    def planes_of():
+        for x in range(cells // rows):
+            plane = mine[x * rows : (x + 1) * rows] + theirs[x * rows : (x + 1) * rows]
+            plane = plane.astype(jnp.bfloat16).astype(jnp.float32)
+            below = jnp.where(cell == 0, 0.0, pltpu.roll(plane, 1, 0))
+            above = jnp.where(cell == 7, 0.0, pltpu.roll(plane, rows - 1, 0))
+            yield x, jnp.concatenate([below, plane, above], axis=1)
+
+    build_taps(planes_of, even, odd)
+    right_of = first_right(own, near, far)
     for q in range(2):
-        total = None
-        for dx in range(3):
-            for dy in range(3):
-                at = pl.ds(q * 2 * quad + dx, 2 * quad)
-                if dy == 1:
-                    left = even[at]
-                else:
-                    left = odd[at, pl.ds(8 * dy, rows)]
-                left = left.reshape(2 * quad * rows, width)
-                tap = (dx * 3 + dy) * 3
-                right = jnp.concatenate(
-                    [jnp.concatenate([own[tap + dz], other[tap + dz]], axis=0) for dz in range(3)],
-                    axis=1,
-                )
-                term = lax.dot_general(left, right, NT, preferred_element_type=jnp.float32)
-                total = term if total is None else total + term
-        total = total + bias
-        low, high = (total[: quad * rows], total[quad * rows :])
-        lane = lax.broadcasted_iota(jnp.int32, low.shape, 1)
-        out[q, 0] = jnp.where(lane < swap, low, pltpu.roll(high, swap, 1)).astype(jnp.bfloat16)
-        out[q, 1] = jnp.where(lane < swap, pltpu.roll(low, swap, 1), high).astype(jnp.bfloat16)
-
-
-def first_conv(mine, theirs, own, near, far, held, planes):
-    cells, half = mine.shape
+        first_out(half_product(q, even, odd, right_of, NT), out, q)
+    bias = jnp.where(s // 2 == c, mine[pl.ds(cells, 8)], theirs[pl.ds(cells, 8)])
+    turned = pltpu.roll(bias, half // 2, 1)
+    lane = lax.broadcasted_iota(jnp.int32, bias.shape, 1)
+    tile[...] = jnp.where((lane < half // 2) == (s % 2 == 0), bias, turned)
+
+
+def first_conv(mine, theirs, own, near, far, planes):
+    cells, half = (mine.shape[0] - 8, mine.shape[1])
     rows = cells // planes
     return pl.pallas_call(
         first_kernel,
-        out_shape=jax.ShapeDtypeStruct((2, 2, cells // 4, half), jnp.bfloat16),
-        in_specs=[pl.BlockSpec(memory_space=pltpu.VMEM)] * 6,
-        out_specs=pl.BlockSpec(memory_space=pltpu.VMEM),
+        out_shape=(
+            jax.ShapeDtypeStruct((2, 2, cells // 4, half), jnp.bfloat16),
+            jax.ShapeDtypeStruct((8, half), jnp.float32),
+        ),
+        in_specs=[pl.BlockSpec(memory_space=pltpu.VMEM)] * 5,
+        out_specs=[pl.BlockSpec(memory_space=pltpu.VMEM)] * 2,
         scratch_shapes=[
             pltpu.VMEM((planes + 2, rows, 3 * half), jnp.bfloat16),
             pltpu.VMEM((planes + 2, rows + 16, 3 * half), jnp.bfloat16),
         ],
         compiler_params=pltpu.CompilerParams(vmem_limit_bytes=32 * 2**20),
-    )(mine, theirs, own, near, far, held)
-
-
-def second_kernel(hidden, own, other, held, out, even, odd):
-    planes = even.shape[0] - 2
-    rows, width = even.shape[1:]
+    )(mine, theirs, own, near, far)
+
+
+def second_far_kernel(hidden, own, other, held, out, tile, even, odd, rights):
+    s, d = (lax.axis_index(a) for a in ("space", "dp"))
+    rows = even.shape[1]
     lanes = hidden.shape[2]
-    k = lanes // 2
     swap = lanes // 2
-    d = lax.axis_index("dp")
-    blank = jnp.zeros((1,) + odd.shape[1:], odd.dtype)
-    odd[0:1] = blank
-    odd[planes + 1 : planes + 2] = blank
-    even[0:1] = blank[:, :rows]
-    even[planes + 1 : planes + 2] = blank[:, :rows]
     cell = lax.broadcasted_iota(jnp.int32, (rows, lanes), 0) % 8
-    lane = lax.broadcasted_iota(jnp.int32, (rows, lanes), 1)
-    low = lane < swap
-    edge = jnp.zeros((8, width), jnp.float32)
+    low = lax.broadcasted_iota(jnp.int32, (rows, lanes), 1) < swap
     per = hidden.shape[1] // rows
-    for q in range(2):
-        for r in range(per):
-            packed = hidden[q, r * rows : (r + 1) * rows].astype(jnp.float32)
-            turned = pltpu.roll(packed, swap, 1)
-            for u in range(2):
-                here, there = (packed, turned) if u == 0 else (turned, packed)
-                below = jnp.where(cell == 0, 0.0, pltpu.roll(here, 1, 0))
-                above = jnp.where(cell == 7, 0.0, pltpu.roll(here, rows - 1, 0))
-                taps = jnp.concatenate(
-                    [jnp.where(low, below, there), jnp.where(low, above, 0.0)], axis=1
-                )
-                x = (q * 2 + u) * per + r
-                even[x + 1] = taps.astype(jnp.bfloat16)
-                odd[x + 1] = jnp.concatenate([edge, taps, edge], axis=0).astype(jnp.bfloat16)
-    lane = lax.broadcasted_iota(jnp.int32, own.shape[1:], 1)
-    low = lane < swap
-    rights = []
-    for tap in range(0, own.shape[0], 3):
-        rows_in = []
-        for dz in range(3):
-            one = jnp.where(d == 0, own[tap + dz], other[tap + dz])
-            two = jnp.where(d == 0, other[tap + dz], own[tap + dz])
-            rows_in.append(jnp.where(low, one, pltpu.roll(two, swap, 1)))
-            rows_in.append(jnp.where(low, pltpu.roll(one, swap, 1), two))
-        rights.append(jnp.concatenate(rows_in, axis=0))
-    for q in range(2):
-        total = None
-        for dx in range(3):
-            for dy in range(3):
-                at = pl.ds(q * planes // 2 + dx, planes // 2)
-                if dy == 1:
-                    left = even[at]
-                else:
-                    left = odd[at, pl.ds(8 * dy, rows)]
-                left = left.reshape(planes // 2 * rows, width)[:, : 3 * k]
-                right = rights[dx * 3 + dy]
-                term = lax.dot_general(left, right, NN, preferred_element_type=jnp.float32)
-                total = term if total is None else total + term
-        total = total + held[2:3] * jnp.where(lax.axis_index("space") == 0, 1.0, 0.0)
-        n = planes // 2 * rows
-        out[q * n : (q + 1) * n] = total.astype(jnp.bfloat16)
-
-
-def second_conv(hidden, own, other, held, planes):
+
+    def planes_of():
+        for q in range(2):
+            for r in range(per):
+                packed = hidden[q, r * rows : (r + 1) * rows].astype(jnp.float32)
+                turned = pltpu.roll(packed, swap, 1)
+                for u in range(2):
+                    here, there = (packed, turned) if u == 0 else (turned, packed)
+                    below = jnp.where(cell == 0, 0.0, pltpu.roll(here, 1, 0))
+                    above = jnp.where(cell == 7, 0.0, pltpu.roll(here, rows - 1, 0))
+                    taps = [jnp.where(low, below, there), jnp.where(low, above, 0.0)]
+                    yield (q * 2 + u) * per + r, jnp.concatenate(taps, axis=1)
+
+    build_taps(planes_of, even, odd)
+    low = lax.broadcasted_iota(jnp.int32, own.shape[1:], 1) < swap
+    for group in range(own.shape[0] // 3):
+        pieces = []
+        for tap in range(3 * group, 3 * group + 3):
+            one = jnp.where(d == 0, own[tap], other[tap])
+            two = jnp.where(d == 0, other[tap], own[tap])
+            pieces.append(jnp.where(low, one, pltpu.roll(two, swap, 1)))
+            pieces.append(jnp.where(low, pltpu.roll(one, swap, 1), two))
+        rights[group] = jnp.concatenate(pieces, axis=0)
+    total = half_product(1 - s // 2, even, odd, lambda group: rights[group], NN)
+    out[...] = total.astype(jnp.bfloat16).reshape(out.shape)
+    tile[...] = jnp.broadcast_to(held[2:3], tile.shape)
+
+
+def second_near_kernel(even, odd, rights, out):
+    s = lax.axis_index("space")
+    total = half_product(s // 2, even, odd, lambda group: rights[group], NN)
+    out[...] = total.astype(jnp.bfloat16).reshape(out.shape)
+
+
+def second_far(hidden, own, other, held, planes):
     _, rows2, lanes = hidden.shape
-    cells = rows2 * 4
-    rows = cells // planes
+    rows = rows2 * 4 // planes
     return pl.pallas_call(
-        second_kernel,
-        out_shape=jax.ShapeDtypeStruct((cells, lanes), jnp.bfloat16),
+        second_far_kernel,
+        out_shape=(
+            jax.ShapeDtypeStruct((2, rows2, lanes), jnp.bfloat16),
+            jax.ShapeDtypeStruct((8, lanes), jnp.float32),
+            jax.ShapeDtypeStruct((planes + 2, rows, 2 * lanes), jnp.bfloat16),
+            jax.ShapeDtypeStruct((planes + 2, rows + 16, 2 * lanes), jnp.bfloat16),
+            jax.ShapeDtypeStruct((9, 6 * own.shape[1], lanes), jnp.bfloat16),
+        ),
         in_specs=[pl.BlockSpec(memory_space=pltpu.VMEM)] * 4,
-        out_specs=pl.BlockSpec(memory_space=pltpu.VMEM),
-        scratch_shapes=[
-            pltpu.VMEM((planes + 2, rows, 2 * lanes), jnp.bfloat16),
-            pltpu.VMEM((planes + 2, rows + 16, 2 * lanes), jnp.bfloat16),
-        ],
+        out_specs=[pl.BlockSpec(memory_space=pltpu.VMEM)] * 5,
         compiler_params=pltpu.CompilerParams(vmem_limit_bytes=32 * 2**20),
     )(hidden, own, other, held)
+
+
+def second_near(even, odd, rights):
+    planes, rows, _ = even.shape
+    return pl.pallas_call(
+        second_near_kernel,
+        out_shape=jax.ShapeDtypeStruct(
+            (2, (planes - 2) * rows // 4, rights.shape[2]), jnp.bfloat16
+        ),
+        in_specs=[pl.BlockSpec(memory_space=pltpu.VMEM)] * 3,
+        out_specs=pl.BlockSpec(memory_space=pltpu.VMEM),
+        compiler_params=pltpu.CompilerParams(vmem_limit_bytes=32 * 2**20),
+    )(even, odd, rights)
 
 
 def stationary(
@@ -458,20 +494,26 @@
     slabs = swapped(jnp.stack([early[up_rows:], late[up_rows:]]), "chan")
     part = up_part(early, late, early_other, late_other, slabs, held, fx * fy * fz)
     part, far = lax.optimization_barrier((part, far))
-    first = first_conv(part, swapped(part, "chan"), first_own, near, far, held, fx)
-    mine = lax.dynamic_index_in_dim(first, c, 0, keepdims=False)
-    theirs = lax.dynamic_index_in_dim(first, 1 - c, 0, keepdims=False)
-    chunks = jnp.stack([mine, swapped(theirs, "chan")]).reshape(4, block, half)
+    part_other = swapped(part, "chan")
+    first, tile = first_conv(part, part_other, first_own, near, far, fx)
+    mine, theirs = (pick(first, c), swapped(pick(first, 1 - c), "chan"))
+    chunks = jnp.stack([mine, theirs]).reshape(4, block, half)
 
     def chunk_for(plane):
-        place = 2 * ((plane // 2) ^ c) + ((plane % 2) ^ d)
-        return lax.dynamic_index_in_dim(chunks, place, 0, keepdims=False)
-
-    hidden = jax.nn.silu(reduced(chunk_for, s)).astype(jnp.bfloat16)
-    hidden, second_other = lax.optimization_barrier((hidden, second_other))
+        return pick(chunks, 2 * ((plane // 2) ^ c) + ((plane % 2) ^ d))
+
+    terms = terms_of([(step, chunk_for(s ^ step)) for step in (3, 2, 1)])
+    terms[0], second_other = lax.optimization_barrier((terms[0], second_other))
+    total = summed(chunk_for(s).astype(jnp.float32) + tile[:1], terms)
+    hidden = jax.nn.silu(total).astype(jnp.bfloat16)
     hidden = ordered(c, hidden, swapped(hidden, "chan"), 0)
-    second = second_conv(hidden, second_own, second_other, held, fx).reshape(4, block, half)
-    total = reduced(lambda plane: lax.dynamic_index_in_dim(second, plane, 0, keepdims=False), s)
+    away, tile, even, odd, rights = second_far(hidden, second_own, second_other, held, fx)
+    sends = [(3, pick(away, (s + 1) % 2)), (2, pick(away, s % 2))]
+    terms = terms_of(sends)
+    even, sends = lax.optimization_barrier((even, sends))
+    home = second_near(even, odd, rights)
+    terms += terms_of([(1, pick(home, (s + 1) % 2))])
+    total = summed(pick(home, s % 2).astype(jnp.float32) + tile[:1], terms)
     return total.astype(jnp.bfloat16).reshape(skip.shape)
 
 

time: 52.2 us -> 50.3 us (0.964)
  waiting for transfers between devices: 21.5 us -> 19.9 us
  starting transfers between devices: 23.1 us -> 22.4 us
    ppermute x8, waiting for transfers between devices: 10.5 us -> 9.19 us  [swapped(): return lax.ppermute(array, axis, [(0, 1), (1, 0)])]
    ppermute x6, starting transfers between devices: 8.9 us -> 8.07 us  [terms_of(): lax.ppermute(chunk, 'space', [(i, i ^ step) for i in range(4)])]
    pallas_call x3 -> x4, Pallas kernels: 4.08 us -> 4.4 us  [the longest x1 2.16 us: first_conv(): pl.pallas_call(first_kernel, out_shape=(jax.ShapeDtypeStruct((2, 2, cells...]
  transfers between devices with their start and end apart: 17 -> 17, of which waited for: 13 -> 11; matrix products, arithmetic and copies ran while one was open for 0% -> 0% of each run, Pallas kernels for 1% -> 3%
where the time goes in v5:
time: 50.3 us; the launch traced here: 50.2 us
  starting transfers between devices  22.4 us (45%)
  waiting for transfers between devices  19.9 us (40%)
  Pallas kernels  6.67 us (13%)
  other arithmetic  0.82 us (2%)
    ppermute x8, waiting for transfers between devices, swapped(): return lax.ppermute(array, axis, [(0, 1), (1, 0)])  9.19 us
    ppermute x6, starting transfers between devices, terms_of(): lax.ppermute(chunk, 'space', [(i, i ^ step) for i in range(4)])  8.07 us
    ppermute x6, waiting for transfers between devices, terms_of(): lax.ppermute(chunk, 'space', [(i, i ^ step) for i in range(4)])  7.49 us
    ppermute x8, starting transfers between devices, swapped(): return lax.ppermute(array, axis, [(0, 1), (1, 0)])  6.23 us
    ppermute x1, starting transfers between devices, stationary(): late = lax.ppermute(late, group, late_route)  4.13 us
    ppermute x1, waiting for transfers between devices, stationary(): late = lax.ppermute(late, group, late_route)  3.23 us
    ppermute x1, starting transfers between devices, stationary(): early_other = lax.ppermute(up_rows_own, group, cross_route)  2.43 us
    pallas_call x1, Pallas kernels, first_conv(): pl.pallas_call(first_kernel, out_shape=(jax.ShapeDtypeStruct((2, 2, cells...  2.16 us
  transfers between devices with their start and end apart: 17, of which 11 were waited for; matrix products, arithmetic and copies ran while one was open for 0% of the time, Pallas kernels for 3%

profile of v5, /device:TPU:0, one launch (start us, length us, event | category | flops | bytes accessed | tf_op | source)
XLA Modules:
  0.0 50.2 jit_solution(7996753954170103533)
XLA Ops:
  0.0 0.0 copy-start.3
  0.0 2.2 %shard_map.82 = (bf16[640,128]{1,0:T(8,128)(2,1)}, bf16[640,128]{1,0:T(8,128)(2,1)}, bf16[14,64,128]{2,1,0:T(8,128)(2,1)}, f32[3,128]{1,0:T(4,128)}) custom-call(bf16[512,128]{1,0:T(8,128)(2,1)} %bitcast.54, bf16[32,512]{1,0:T(8,128)(2,1)} %bitcast.58, bf16[256,128]{1,0:T(8,128)(2,1)} %bitcast.57, bf16[27,64,128]{2,1,0:T(8,128)(2,1)} %bitcast.49, ...), custom_call_target="tpu_custom_call" | custom-call | tf_op jit(solution)/shard_map/pallas_call | solution.py:148
  2.2 4.1 %collective-permute-start = (bf16[640,128]{1,0:T(8,128)(2,1)}, bf16[640,128]{1,0:T(8,128)(2,1)S(1)}, u32[]{:S(2)}, u32[]{:S(2)}) collective-permute-start(bf16[640,128]{1,0:T(8,128)(2,1)} %get-tuple-element.28), channel_id=1, source_target_pairs={{0,8},{1,12},{2,10},{3,14},{4,9},{5,13},{6,11},{7,15},{8,0},{9,4},... | collective-permute-start | bytes 491528 | tf_op jit(solution)/shard_map/ppermute | solution.py:483
  6.3 1.5 %collective-permute-start.5 = (bf16[14,64,128]{2,1,0:T(8,128)(2,1)}, bf16[14,64,128]{2,1,0:T(8,128)(2,1)S(1)}, u32[]{:S(2)}, u32[]{:S(2)}) collective-permute-start(bf16[14,64,128]{2,1,0:T(8,128)(2,1)} %get-tuple-element.37), channel_id=1, source_target_pairs={{0,2},{2,0},{1,3},{3,1},{4,6},{6,4},{5,7},{7,5},{8,10},{10,8},{9,1... | collective-permute-start | bytes 688136 | tf_op jit(solution)/shard_map/ppermute | solution.py:91
  7.8 1.6 %collective-permute-start.2 = (bf16[640,128]{1,0:T(8,128)(2,1)}, bf16[640,128]{1,0:T(8,128)(2,1)S(1)}, u32[]{:S(2)}, u32[]{:S(2)}) collective-permute-start(bf16[640,128]{1,0:T(8,128)(2,1)} %get-tuple-element.29), channel_id=1, source_target_pairs={{0,0},{1,4},{2,2},{3,6},{4,1},{5,5},{6,3},{7,7},{8,8},{9,12},{10,1... | collective-permute-start | bytes 491528 | tf_op jit(solution)/shard_map/ppermute | solution.py:485
  9.3 0.0 copy-done.3
  9.3 2.4 %collective-permute-start.3 = (bf16[512,128]{1,0:T(8,128)(2,1)S(1)}, bf16[512,128]{1,0:T(8,128)(2,1)S(1)}, u32[]{:S(2)}, u32[]{:S(2)}) collective-permute-start(bf16[512,128]{1,0:T(8,128)(2,1)S(1)} %bitcast.55), channel_id=1, source_target_pairs={{0,2},{1,6},{2,0},{3,4},{4,3},{5,7},{6,1},{7,5},{16,18},{17,22},{1... | collective-permute-start | bytes 393224 | tf_op jit(solution)/shard_map/ppermute | solution.py:486
  11.8 3.2 %collective-permute-done.late = bf16[640,128]{1,0:T(8,128)(2,1)S(1)} collective-permute-done((bf16[640,128]{1,0:T(8,128)(2,1)}, bf16[640,128]{1,0:T(8,128)(2,1)S(1)}, u32[]{:S(2)}, u32[]{:S(2)}) %collective-permute-start) | collective-permute-done | bytes 163872 | tf_op jit(solution)/shard_map/ppermute | solution.py:483
  15.0 1.6 %collective-permute-start.1 = (bf16[512,128]{1,0:T(8,128)(2,1)S(1)}, bf16[512,128]{1,0:T(8,128)(2,1)S(1)}, u32[]{:S(2)}, u32[]{:S(2)}) collective-permute-start(bf16[512,128]{1,0:T(8,128)(2,1)S(1)} %slice.20), channel_id=1, source_target_pairs={{0,2},{2,0},{1,3},{3,1},{4,6},{6,4},{5,7},{7,5},{8,10},{10,8},{9,1... | collective-permute-start | bytes 393224 | tf_op jit(solution)/shard_map/ppermute | solution.py:91
  16.6 0.0 collective-permute-done.5.near
  16.6 1.5 %collective-permute-start.6 = (bf16[14,64,128]{2,1,0:T(8,128)(2,1)S(1)}, bf16[14,64,128]{2,1,0:T(8,128)(2,1)S(1)}, u32[]{:S(2)}, u32[]{:S(2)}) collective-permute-start(bf16[14,64,128]{2,1,0:T(8,128)(2,1)S(1)} %collective-permute-done.5.near), channel_id=1, source_target_pairs={{0,16},{16,0},{1,17},{17,1},{2,18},{18,2},{3,19},{19,3},{4,20},{20... | collective-permute-start | bytes 688136 | tf_op jit(solution)/shard_map/ppermute | solution.py:91
  18.1 0.0 collective-permute-done.3.early_other
  18.1 0.0 collective-permute-done.2.early
  18.1 2.9 %collective-permute-done.1.late_other = bf16[512,128]{1,0:T(8,128)(2,1)S(1)} collective-permute-done((bf16[512,128]{1,0:T(8,128)(2,1)S(1)}, bf16[512,128]{1,0:T(8,128)(2,1)S(1)}, u32[]{:S(2)}, u32[]{:S(2)}) %collective-permute-start.1) | collective-permute-done | bytes 131104 | tf_op jit(solution)/shard_map/ppermute | solution.py:91
  21.0 0.1 collective-permute-start.4
  21.1 0.0 copy-done.1
  21.1 0.0 copy-start.2
  21.1 0.1 shard_map.83.own
  21.3 1.1 %collective-permute-done.4.slabs = bf16[2,128,128]{2,1,0:T(8,128)(2,1)S(1)} collective-permute-done((bf16[2,128,128]{2,1,0:T(8,128)(2,1)S(1)}, bf16[2,128,128]{2,1,0:T(8,128)(2,1)S(1)}, u32[]{:S(2)}, u32[]{:S(2)}) %collective-permute-start.4) | collective-permute-done | bytes 65568 | tf_op jit(solution)/shard_map/ppermute | solution.py:91
  22.3 0.0 copy-done.2
  22.3 0.4 shard_map.84.mine
  22.8 0.2 collective-permute-done.6.far
  23.0 0.0 collective-permute-start.7
  23.0 1.9 %collective-permute-done.7.theirs = f32[1032,128]{1,0:T(8,128)S(1)} collective-permute-done((f32[1032,128]{1,0:T(8,128)S(1)}, f32[1032,128]{1,0:T(8,128)S(1)}, u32[]{:S(2)}, u32[]{:S(2)}) %collective-permute-start.7) | collective-permute-done | bytes 528416 | tf_op jit(solution)/shard_map/ppermute | solution.py:91
  24.9 0.0 copy-done
  24.9 2.2 %shard_map.85 = (bf16[2,2,256,128]{3,2,1,0:T(8,128)(2,1)S(1)}, f32[8,128]{1,0:T(8,128)S(1)}) custom-call(f32[1032,128]{1,0:T(8,128)S(1)} %shard_map.84.mine, f32[1032,128]{1,0:T(8,128)S(1)} %collective-permute-done.7.theirs, bf16[27,64,128]{2,1,0:T(8,128)(2,1)S(1)} %bitcast.50, bf16[14,64,128]{2,1,0:T(8,128)(2,1)S(1)} %collective-permute-done.5.near, ...), custom_call_target="tpu_custom_call" | custom-call | tf_op jit(solution)/shard_map/pallas_call | solution.py:372
  27.1 0.2 collective-permute-start.8
  27.3 1.3 %collective-permute-start.10 = (bf16[27,32,128]{2,1,0:T(8,128)(2,1)S(1)}, bf16[27,32,128]{2,1,0:T(8,128)(2,1)S(1)}, u32[]{:S(2)}, u32[]{:S(2)}) collective-permute-start(bf16[27,32,128]{2,1,0:T(8,128)(2,1)S(1)} %shard_map.83.own), channel_id=1, source_target_pairs={{0,2},{2,0},{1,3},{3,1},{4,6},{6,4},{5,7},{7,5},{8,10},{10,8},{9,1... | collective-permute-start | bytes 663560 | tf_op jit(solution)/shard_map/ppermute | solution.py:91
  28.7 0.0 collective-permute-done.8
  28.7 2.2 %collective-permute-start.9 = (bf16[256,128]{1,0:T(8,128)(2,1)S(1)}, bf16[256,128]{1,0:T(8,128)(2,1)S(1)}, u32[]{:S(2)}, u32[]{:S(2)}) collective-permute-start(bf16[256,128]{1,0:T(8,128)(2,1)S(1)} %get-tuple-element.51), channel_id=1, source_target_pairs={{0,12},{4,8},{8,4},{12,0},{1,13},{5,9},{9,5},{13,1},{2,14},{6,10},... | collective-permute-start | bytes 196616 | tf_op jit(solution)/shard_map/ppermute | solution.py:250
  31.0 0.0 collective-permute-start.12
  31.0 2.2 %collective-permute-start.11 = (bf16[256,128]{1,0:T(8,128)(2,1)S(1)}, bf16[256,128]{1,0:T(8,128)(2,1)S(1)}, u32[]{:S(2)}, u32[]{:S(2)}) collective-permute-start(bf16[256,128]{1,0:T(8,128)(2,1)S(1)} %get-tuple-element.53), channel_id=1, source_target_pairs={{0,8},{4,12},{8,0},{12,4},{1,9},{5,13},{9,1},{13,5},{2,10},{6,14},... | collective-permute-start | bytes 196616 | tf_op jit(solution)/shard_map/ppermute | solution.py:250
  33.2 1.8 %collective-permute-done.10.other = bf16[27,32,128]{2,1,0:T(8,128)(2,1)S(1)} collective-permute-done((bf16[27,32,128]{2,1,0:T(8,128)(2,1)S(1)}, bf16[27,32,128]{2,1,0:T(8,128)(2,1)S(1)}, u32[]{:S(2)}, u32[]{:S(2)}) %collective-permute-start.10) | collective-permute-done | bytes 221216 | tf_op jit(solution)/shard_map/ppermute | solution.py:91
  35.0 0.4 collective-permute-done.9
  35.5 1.8 %collective-permute-done.12 = bf16[256,128]{1,0:T(8,128)(2,1)S(1)} collective-permute-done((bf16[256,128]{1,0:T(8,128)(2,1)S(1)}, bf16[256,128]{1,0:T(8,128)(2,1)S(1)}, u32[]{:S(2)}, u32[]{:S(2)}) %collective-permute-start.12) | collective-permute-done | bytes 65568 | tf_op jit(solution)/shard_map/ppermute | solution.py:250
  37.2 0.5 collective-permute-done.11
  37.7 0.1 multiply_convert_fusion
  37.8 0.1 collective-permute-start.13
  37.9 1.2 %collective-permute-done.13 = bf16[256,128]{1,0:T(8,128)(2,1)S(1)} collective-permute-done((bf16[256,128]{1,0:T(8,128)(2,1)S(1)}, bf16[256,128]{1,0:T(8,128)(2,1)S(1)}, u32[]{:S(2)}, u32[]{:S(2)}) %collective-permute-start.13) | collective-permute-done | bytes 65568 | tf_op jit(solution)/shard_map/ppermute | solution.py:91
  39.2 1.1 %shard_map.86 = (bf16[2,256,128]{2,1,0:T(8,128)(2,1)S(1)}, f32[8,128]{1,0:T(8,128)S(1)}, bf16[10,128,256]{2,1,0:T(8,128)(2,1)S(1)}, bf16[10,144,256]{2,1,0:T(8,128)(2,1)S(1)}, bf16[9,192,128]{2,1,0:T(8,128)(2,1)S(1)}) custom-call(bf16[2,256,128]{2,1,0:T(8,128)(2,1)S(1)} %pad_maximum_fusion.1.hidden, bf16[27,32,128]{2,1,0:T(8,128)(2,1)S(1)} %shard_map.83.own, ...), custom_call_target="tpu_custom_call" | custom-call | tf_op jit(solution)/shard_map/pallas_call | solution.py:433
  40.3 1.1 %collective-permute-start.15 = (bf16[256,128]{1,0:T(8,128)(2,1)S(1)}, bf16[256,128]{1,0:T(8,128)(2,1)S(1)}, u32[]{:S(2)}, u32[]{:S(2)}) collective-permute-start(bf16[256,128]{1,0:T(8,128)(2,1)S(1)} %get-tuple-element.56), channel_id=1, source_target_pairs={{0,8},{4,12},{8,0},{12,4},{1,9},{5,13},{9,1},{13,5},{2,10},{6,14},... | collective-permute-start | bytes 196616 | tf_op jit(solution)/shard_map/ppermute | solution.py:250
  41.4 1.7 %collective-permute-start.14 = (bf16[256,128]{1,0:T(8,128)(2,1)S(1)}, bf16[256,128]{1,0:T(8,128)(2,1)S(1)}, u32[]{:S(2)}, u32[]{:S(2)}) collective-permute-start(bf16[256,128]{1,0:T(8,128)(2,1)S(1)} %get-tuple-element.57), channel_id=1, source_target_pairs={{0,12},{4,8},{8,4},{12,0},{1,13},{5,9},{9,5},{13,1},{2,14},{6,10},... | collective-permute-start | bytes 196616 | tf_op jit(solution)/shard_map/ppermute | solution.py:250
  43.1 0.8 %shard_map.87 = bf16[2,256,128]{2,1,0:T(8,128)(2,1)S(1)} custom-call(bf16[10,128,256]{2,1,0:T(8,128)(2,1)S(1)} %get-tuple-element.47.even, bf16[10,144,256]{2,1,0:T(8,128)(2,1)S(1)} %get-tuple-element.48.odd, bf16[9,192,128]{2,1,0:T(8,128)(2,1)S(1)} %get-tuple-element.49.rights), custom_call_target="tpu_custom_call" | custom-call | tf_op jit(solution)/shard_map/pallas_call | solution.py:450
  43.9 0.8 %collective-permute-start.16 = (bf16[256,128]{1,0:T(8,128)(2,1)S(1)}, bf16[256,128]{1,0:T(8,128)(2,1)S(1)}, u32[]{:S(2)}, u32[]{:S(2)}) collective-permute-start(bf16[256,128]{1,0:T(8,128)(2,1)S(1)} %dynamic-slice_bitcast_fusion.1), channel_id=1, source_target_pairs={{0,4},{4,0},{8,12},{12,8},{1,5},{5,1},{9,13},{13,9},{2,6},{6,2},{1... | collective-permute-start | bytes 196616 | tf_op jit(solution)/shard_map/ppermute | solution.py:250
  44.7 4.8 %collective-permute-done.16 = bf16[256,128]{1,0:T(8,128)(2,1)S(1)} collective-permute-done((bf16[256,128]{1,0:T(8,128)(2,1)S(1)}, bf16[256,128]{1,0:T(8,128)(2,1)S(1)}, u32[]{:S(2)}, u32[]{:S(2)}) %collective-permute-start.16) | collective-permute-done | bytes 65568 | tf_op jit(solution)/shard_map/ppermute | solution.py:250
  49.5 0.0 collective-permute-done.15
  49.5 0.0 collective-permute-done.14
  49.5 0.7 %fusion.3 = bf16[256,128]{1,0:T(8,128)(2,1)} fusion(bf16[256,128]{1,0:T(8,128)(2,1)S(1)} %collective-permute-done.16, bf16[256,128]{1,0:T(8,128)(2,1)S(1)} %collective-permute-done.15, bf16[256,128]{1,0:T(8,128)(2,1)S(1)} %collective-permute-done.14, f32[128]{0:T(128)S(1)} %slice_bitcast_fusion.2, bf16[2,256,128]{2,1,0:T(8,128)(2,1)S(1)} %shard_map.87, ...), kind=kLoop, calls=%fused_computation.6 | loop fusion | flops 294912 | bytes 328196 | tf_op jit(solution)/shard_map/convert_element_type | solution.py:517
  (14 shorter events, 0.2 us)
Async XLA Ops:
  0.0 9.3 %copy-start.3 = (bf16[8,128,1,64]{1,3,2,0:T(8,128)(2,1)S(1)}, bf16[8,128,1,64]{1,3,2,0:T(8,128)(2,1)}, u32[]{:S(2)}) copy-start(bf16[8,128,1,64]{1,3,2,0:T(8,128)(2,1)} %param.10) | copy-start | bytes 393220
  0.0 21.1 %copy-start.1 = (bf16[27,64,1,64]{3,1,2,0:T(8,128)(2,1)S(1)}, bf16[27,64,1,64]{3,1,2,0:T(8,128)(2,1)}, u32[]{:S(2)}) copy-start(bf16[27,64,1,64]{3,1,2,0:T(8,128)(2,1)} %param.14) | copy-start | bytes 663556
  2.2 12.9 %collective-permute-start = (bf16[640,128]{1,0:T(8,128)(2,1)}, bf16[640,128]{1,0:T(8,128)(2,1)S(1)}, u32[]{:S(2)}, u32[]{:S(2)}) collective-permute-start(bf16[640,128]{1,0:T(8,128)(2,1)} %get-tuple-element.28), channel_id=1, source_target_pairs={{0,8},{1,12},{2,10},{3,14},{4,9},{5,13},{6,11},{7,15},{8,0},{9,4},... | collective-permute-start | bytes 491528 | tf_op jit(solution)/shard_map/ppermute | solution.py:483
  6.3 10.3 %collective-permute-start.5 = (bf16[14,64,128]{2,1,0:T(8,128)(2,1)}, bf16[14,64,128]{2,1,0:T(8,128)(2,1)S(1)}, u32[]{:S(2)}, u32[]{:S(2)}) collective-permute-start(bf16[14,64,128]{2,1,0:T(8,128)(2,1)} %get-tuple-element.37), channel_id=1, source_target_pairs={{0,2},{2,0},{1,3},{3,1},{4,6},{6,4},{5,7},{7,5},{8,10},{10,8},{9,1... | collective-permute-start | bytes 688136 | tf_op jit(solution)/shard_map/ppermute | solution.py:91
  7.8 10.3 %collective-permute-start.2 = (bf16[640,128]{1,0:T(8,128)(2,1)}, bf16[640,128]{1,0:T(8,128)(2,1)S(1)}, u32[]{:S(2)}, u32[]{:S(2)}) collective-permute-start(bf16[640,128]{1,0:T(8,128)(2,1)} %get-tuple-element.29), channel_id=1, source_target_pairs={{0,0},{1,4},{2,2},{3,6},{4,1},{5,5},{6,3},{7,7},{8,8},{9,12},{10,1... | collective-permute-start | bytes 491528 | tf_op jit(solution)/shard_map/ppermute | solution.py:485
  9.3 8.8 %collective-permute-start.3 = (bf16[512,128]{1,0:T(8,128)(2,1)S(1)}, bf16[512,128]{1,0:T(8,128)(2,1)S(1)}, u32[]{:S(2)}, u32[]{:S(2)}) collective-permute-start(bf16[512,128]{1,0:T(8,128)(2,1)S(1)} %bitcast.55), channel_id=1, source_target_pairs={{0,2},{1,6},{2,0},{3,4},{4,3},{5,7},{6,1},{7,5},{16,18},{17,22},{1... | collective-permute-start | bytes 393224 | tf_op jit(solution)/shard_map/ppermute | solution.py:486
  15.0 6.0 %collective-permute-start.1 = (bf16[512,128]{1,0:T(8,128)(2,1)S(1)}, bf16[512,128]{1,0:T(8,128)(2,1)S(1)}, u32[]{:S(2)}, u32[]{:S(2)}) collective-permute-start(bf16[512,128]{1,0:T(8,128)(2,1)S(1)} %slice.20), channel_id=1, source_target_pairs={{0,2},{2,0},{1,3},{3,1},{4,6},{6,4},{5,7},{7,5},{8,10},{10,8},{9,1... | collective-permute-start | bytes 393224 | tf_op jit(solution)/shard_map/ppermute | solution.py:91
  16.6 6.4 %collective-permute-start.6 = (bf16[14,64,128]{2,1,0:T(8,128)(2,1)S(1)}, bf16[14,64,128]{2,1,0:T(8,128)(2,1)S(1)}, u32[]{:S(2)}, u32[]{:S(2)}) collective-permute-start(bf16[14,64,128]{2,1,0:T(8,128)(2,1)S(1)} %collective-permute-done.5.near), channel_id=1, source_target_pairs={{0,16},{16,0},{1,17},{17,1},{2,18},{18,2},{3,19},{19,3},{4,20},{20... | collective-permute-start | bytes 688136 | tf_op jit(solution)/shard_map/ppermute | solution.py:91
  21.0 1.3 %collective-permute-start.4 = (bf16[2,128,128]{2,1,0:T(8,128)(2,1)S(1)}, bf16[2,128,128]{2,1,0:T(8,128)(2,1)S(1)}, u32[]{:S(2)}, u32[]{:S(2)}) collective-permute-start(bf16[2,128,128]{2,1,0:T(8,128)(2,1)S(1)} %pad_maximum_fusion.2), channel_id=1, source_target_pairs={{0,1},{1,0},{2,3},{3,2},{4,5},{5,4},{6,7},{7,6},{8,9},{9,8},{10,11... | collective-permute-start | bytes 196616 | tf_op jit(solution)/shard_map/ppermute | solution.py:91
  21.1 1.2 %copy-start.2 = (f32[3,128]{1,0:T(4,128)S(1)}, f32[3,128]{1,0:T(4,128)}, u32[]{:S(2)}) copy-start(f32[3,128]{1,0:T(4,128)} %get-tuple-element.36.held) | copy-start | bytes 4612
  22.3 2.6 %copy-start = (bf16[27,128,1,64]{1,3,2,0:T(8,128)(2,1)S(1)}, bf16[27,128,1,64]{1,3,2,0:T(8,128)(2,1)}, u32[]{:S(2)}) copy-start(bf16[27,128,1,64]{1,3,2,0:T(8,128)(2,1)} %param.12) | copy-start | bytes 1327108
  23.0 1.9 %collective-permute-start.7 = (f32[1032,128]{1,0:T(8,128)S(1)}, f32[1032,128]{1,0:T(8,128)S(1)}, u32[]{:S(2)}, u32[]{:S(2)}) collective-permute-start(f32[1032,128]{1,0:T(8,128)S(1)} %shard_map.84.mine), channel_id=1, source_target_pairs={{0,1},{1,0},{2,3},{3,2},{4,5},{5,4},{6,7},{7,6},{8,9},{9,8},{10,11... | collective-permute-start | bytes 1585160 | tf_op jit(solution)/shard_map/ppermute | solution.py:91
  27.1 1.5 %collective-permute-start.8 = (bf16[2,256,128]{2,1,0:T(8,128)(2,1)S(1)}, bf16[2,256,128]{2,1,0:T(8,128)(2,1)S(1)}, u32[]{:S(2)}, u32[]{:S(2)}) collective-permute-start(bf16[2,256,128]{2,1,0:T(8,128)(2,1)S(1)} %get-tuple-element.55), channel_id=1, source_target_pairs={{0,1},{1,0},{2,3},{3,2},{4,5},{5,4},{6,7},{7,6},{8,9},{9,8},{10,11... | collective-permute-start | bytes 393224 | tf_op jit(solution)/shard_map/ppermute | solution.py:91
  27.3 7.7 %collective-permute-start.10 = (bf16[27,32,128]{2,1,0:T(8,128)(2,1)S(1)}, bf16[27,32,128]{2,1,0:T(8,128)(2,1)S(1)}, u32[]{:S(2)}, u32[]{:S(2)}) collective-permute-start(bf16[27,32,128]{2,1,0:T(8,128)(2,1)S(1)} %shard_map.83.own), channel_id=1, source_target_pairs={{0,2},{2,0},{1,3},{3,1},{4,6},{6,4},{5,7},{7,5},{8,10},{10,8},{9,1... | collective-permute-start | bytes 663560 | tf_op jit(solution)/shard_map/ppermute | solution.py:91
  28.7 6.7 %collective-permute-start.9 = (bf16[256,128]{1,0:T(8,128)(2,1)S(1)}, bf16[256,128]{1,0:T(8,128)(2,1)S(1)}, u32[]{:S(2)}, u32[]{:S(2)}) collective-permute-start(bf16[256,128]{1,0:T(8,128)(2,1)S(1)} %get-tuple-element.51), channel_id=1, source_target_pairs={{0,12},{4,8},{8,4},{12,0},{1,13},{5,9},{9,5},{13,1},{2,14},{6,10},... | collective-permute-start | bytes 196616 | tf_op jit(solution)/shard_map/ppermute | solution.py:250
  31.0 6.3 %collective-permute-start.12 = (bf16[256,128]{1,0:T(8,128)(2,1)S(1)}, bf16[256,128]{1,0:T(8,128)(2,1)S(1)}, u32[]{:S(2)}, u32[]{:S(2)}) collective-permute-start(bf16[256,128]{1,0:T(8,128)(2,1)S(1)} %get-tuple-element.52), channel_id=1, source_target_pairs={{0,4},{4,0},{8,12},{12,8},{1,5},{5,1},{9,13},{13,9},{2,6},{6,2},{1... | collective-permute-start | bytes 196616 | tf_op jit(solution)/shard_map/ppermute | solution.py:250
  31.0 6.8 %collective-permute-start.11 = (bf16[256,128]{1,0:T(8,128)(2,1)S(1)}, bf16[256,128]{1,0:T(8,128)(2,1)S(1)}, u32[]{:S(2)}, u32[]{:S(2)}) collective-permute-start(bf16[256,128]{1,0:T(8,128)(2,1)S(1)} %get-tuple-element.53), channel_id=1, source_target_pairs={{0,8},{4,12},{8,0},{12,4},{1,9},{5,13},{9,1},{13,5},{2,10},{6,14},... | collective-permute-start | bytes 196616 | tf_op jit(solution)/shard_map/ppermute | solution.py:250
  37.8 1.3 %collective-permute-start.13 = (bf16[256,128]{1,0:T(8,128)(2,1)S(1)}, bf16[256,128]{1,0:T(8,128)(2,1)S(1)}, u32[]{:S(2)}, u32[]{:S(2)}) collective-permute-start(bf16[256,128]{1,0:T(8,128)(2,1)S(1)} %multiply_convert_fusion), channel_id=1, source_target_pairs={{0,1},{1,0},{2,3},{3,2},{4,5},{5,4},{6,7},{7,6},{8,9},{9,8},{10,11... | collective-permute-start | bytes 196616 | tf_op jit(solution)/shard_map/ppermute | solution.py:91
  40.3 9.2 %collective-permute-start.15 = (bf16[256,128]{1,0:T(8,128)(2,1)S(1)}, bf16[256,128]{1,0:T(8,128)(2,1)S(1)}, u32[]{:S(2)}, u32[]{:S(2)}) collective-permute-start(bf16[256,128]{1,0:T(8,128)(2,1)S(1)} %get-tuple-element.56), channel_id=1, source_target_pairs={{0,8},{4,12},{8,0},{12,4},{1,9},{5,13},{9,1},{13,5},{2,10},{6,14},... | collective-permute-start | bytes 196616 | tf_op jit(solution)/shard_map/ppermute | solution.py:250
  41.4 8.0 %collective-permute-start.14 = (bf16[256,128]{1,0:T(8,128)(2,1)S(1)}, bf16[256,128]{1,0:T(8,128)(2,1)S(1)}, u32[]{:S(2)}, u32[]{:S(2)}) collective-permute-start(bf16[256,128]{1,0:T(8,128)(2,1)S(1)} %get-tuple-element.57), channel_id=1, source_target_pairs={{0,12},{4,8},{8,4},{12,0},{1,13},{5,9},{9,5},{13,1},{2,14},{6,10},... | collective-permute-start | bytes 196616 | tf_op jit(solution)/shard_map/ppermute | solution.py:250
  43.9 5.6 %collective-permute-start.16 = (bf16[256,128]{1,0:T(8,128)(2,1)S(1)}, bf16[256,128]{1,0:T(8,128)(2,1)S(1)}, u32[]{:S(2)}, u32[]{:S(2)}) collective-permute-start(bf16[256,128]{1,0:T(8,128)(2,1)S(1)} %dynamic-slice_bitcast_fusion.1), channel_id=1, source_target_pairs={{0,4},{4,0},{8,12},{12,8},{1,5},{5,1},{9,13},{13,9},{2,6},{6,2},{1... | collective-permute-start | bytes 196616 | tf_op jit(solution)/shard_map/ppermute | solution.py:250

commit v6 on v5

--- a/solution.py
+++ b/solution.py
@@ -95,64 +95,6 @@
     first = jnp.where(index == 0, own, other)
     second = jnp.where(index == 0, other, own)
     return jnp.stack([first, second], axis=axis)
-
-
-def pack_kernel(weight, coarse, skip, first, biases, early, late, half, held, sems):
-    s = lax.axis_index("space")
-    g = lax.axis_index("groups")
-    kb = early.shape[1]
-    rows, deep = (weight.shape[0], coarse.shape[0])
-    span = half.shape[0]
-
-    def fill(up_packet, skip_packet):
-        moves = [(weight, up_packet.at[pl.ds(0, rows)])]
-        for i in range(coarse.shape[1] // kb):
-            place = up_packet.at[pl.ds(rows + i * deep, deep)]
-            moves.append((coarse.at[:, pl.ds(i * kb, kb)], place))
-        moves.append((skip, skip_packet.at[pl.ds(0, skip.shape[0])]))
-        rest = skip_packet.shape[0] - skip.shape[0]
-        moves.append((weight.at[pl.ds(0, rest)], skip_packet.at[pl.ds(skip.shape[0], rest)]))
-        moves.append((first.at[pl.ds(g * (first.shape[0] - span), span)], half))
-        for i, bias in enumerate(biases):
-            moves.append((bias, held.at[pl.ds(i, 1)]))
-        copies = [
-            pltpu.make_async_copy(source, place, sems.at[i])
-            for i, (source, place) in enumerate(moves)
-        ]
-        for copy in copies:
-            copy.start()
-        for copy in copies:
-            copy.wait()
-
-    @pl.when(s < 2)
-    def _():
-        fill(early, late)
-
-    @pl.when(s >= 2)
-    def _():
-        fill(late, early)
-
-
-def packed(weight, coarse, skip, first, biases):
-    rows, kb = weight.shape
-    deep, cin = coarse.shape
-    count = len(biases)
-    packet = jax.ShapeDtypeStruct((rows + deep * (cin // kb), kb), jnp.bfloat16)
-    span = (first.shape[0] + 1) // 2
-    half = jax.ShapeDtypeStruct((span,) + first.shape[1:], jnp.bfloat16)
-    held = jax.ShapeDtypeStruct((count,) + biases[0].shape[1:], jnp.float32)
-
-    def kernel(*refs):
-        pack_kernel(*refs[:4], refs[4 : 4 + count], *refs[4 + count :])
-
-    return pl.pallas_call(
-        kernel,
-        out_shape=(packet, packet, half, held),
-        in_specs=[pl.BlockSpec(memory_space=pltpu.HBM)] * (4 + count),
-        out_specs=[pl.BlockSpec(memory_space=pltpu.VMEM)] * 4,
-        scratch_shapes=[pltpu.SemaphoreType.DMA((4 + cin // kb + count,))],
-        compiler_params=pltpu.CompilerParams(vmem_limit_bytes=60 * 2**20),
-    )(weight, coarse, skip, first, *biases)
 
 
 def dense_kernel(weight, out):
@@ -472,13 +414,17 @@
     up_rows = taps * own_n
     first_own = first_weight[:, :, 0, :].transpose(0, 2, 1)
     up_rows_own = up_weight[:, :, 0, :].transpose(0, 2, 1).reshape(up_rows, kb)
-    early, late, near, held = packed(
-        up_rows_own,
-        coarse.reshape(cells, cin),
-        skip.reshape(block, half),
-        first_own,
-        [bias.reshape(1, half) for bias in (up_bias, first_bias, second_bias)],
-    )
+    columns = coarse.reshape(cells, cin)
+    columns = [columns[:, i : i + kb] for i in range(0, cin, kb)]
+    up_packet = jnp.concatenate([up_rows_own] + columns, axis=0)
+    skip_rows = skip.reshape(block, half)
+    skip_packet = jnp.pad(skip_rows, ((0, up_packet.shape[0] - block), (0, 0)))
+    early = jnp.where(s < 2, up_packet, skip_packet)
+    late = jnp.where(s < 2, skip_packet, up_packet)
+    span = (first_own.shape[0] + 1) // 2
+    start = lax.axis_index("groups") * (first_own.shape[0] - span)
+    near = lax.dynamic_slice_in_dim(first_own, start, span, 0)
+    held = jnp.stack([up_bias, first_bias, second_bias])
     early_route, late_route, cross_route = line_routes()
     late = lax.ppermute(late, group, late_route)
     late_other = swapped(late[:up_rows], "dp")

time: 50.3 us -> 49.2 us (0.978)
  Pallas kernels: 6.67 us -> 4.52 us
  local copies, waits for them, and re-layouts: 0.12 us -> 1.81 us
  starting transfers between devices: 22.4 us -> 21.4 us
    pallas_call x1 -> x0, Pallas kernels: 2.15 us -> none  [packed(): pl.pallas_call(kernel, out_shape=(packet, packet, half, held), in_specs=[...]
    unnamed x8 -> x20, local copies, waits for them, and re-layouts: 0.02 us -> 1.69 us
    ppermute x1, starting transfers between devices: 1.56 us -> 0.66 us  [stationary(): early = lax.ppermute(early, group, early_route)]
    ppermute x1, waiting for transfers between devices: 3.23 us -> 3.83 us  [stationary(): late = lax.ppermute(late, group, late_route)]
  transfers between devices with their start and end apart: 17 -> 17, of which waited for: 11 -> 12; matrix products, arithmetic and copies ran while one was open for 0% -> 0% of each run, Pallas kernels for 3% -> 3%
where the time goes in v6:
time: 49.2 us; the launch traced here: 49 us
  starting transfers between devices  21.4 us (43%)
  waiting for transfers between devices  20.1 us (41%)
  Pallas kernels  4.52 us (9%)
  local copies, waits for them, and re-layouts  1.81 us (4%)
  other arithmetic  0.89 us (2%)
    ppermute x8, waiting for transfers between devices, swapped(): return lax.ppermute(array, axis, [(0, 1), (1, 0)])  9 us
    ppermute x6, starting transfers between devices, terms_of(): lax.ppermute(chunk, 'space', [(i, i ^ step) for i in range(4)])  8.07 us
    ppermute x6, waiting for transfers between devices, terms_of(): lax.ppermute(chunk, 'space', [(i, i ^ step) for i in range(4)])  7.3 us
    ppermute x8, starting transfers between devices, swapped(): return lax.ppermute(array, axis, [(0, 1), (1, 0)])  6.09 us
    ppermute x1, starting transfers between devices, stationary(): late = lax.ppermute(late, group, late_route)  4.11 us
    ppermute x1, waiting for transfers between devices, stationary(): late = lax.ppermute(late, group, late_route)  3.83 us
    ppermute x1, starting transfers between devices, stationary(): early_other = lax.ppermute(up_rows_own, group, cross_route)  2.44 us
    pallas_call x1, Pallas kernels, first_conv(): pl.pallas_call(first_kernel, out_shape=(jax.ShapeDtypeStruct((2, 2, cells...  2.16 us
  transfers between devices with their start and end apart: 17, of which 12 were waited for; matrix products, arithmetic and copies ran while one was open for 0% of the time, Pallas kernels for 3%

profile of v6, /device:TPU:0, one launch (start us, length us, event | category | flops | bytes accessed | tf_op | source)
XLA Modules:
  0.0 49.0 jit_solution(6312818303342337115)
XLA Ops:
  0.0 1.0 %constant_dynamic-update-slice_fusion.4 = bf16[640,128]{1,0:T(8,128)(2,1)S(1)} fusion(bf16[512,128]{1,0:T(8,128)(2,1)} %bitcast.57), kind=kLoop, calls=%fused_computation.31 | loop fusion | bytes 262144
  1.1 0.1 pad_select_fusion
  1.1 0.0 copy-start.2
  1.1 4.1 %collective-permute-start = (bf16[640,128]{1,0:T(8,128)(2,1)S(1)}, bf16[640,128]{1,0:T(8,128)(2,1)S(1)}, u32[]{:S(2)}, u32[]{:S(2)}) collective-permute-start(bf16[640,128]{1,0:T(8,128)(2,1)S(1)} %get-tuple-element.49), channel_id=1, source_target_pairs={{0,8},{1,12},{2,10},{3,14},{4,9},{5,13},{6,11},{7,15},{8,0},{9,4},... | collective-permute-start | bytes 491528 | tf_op jit(solution)/shard_map/ppermute | solution.py:429
  5.3 1.6 %collective-permute-start.5 = (bf16[14,64,128]{2,1,0:T(8,128)(2,1)S(1)}, bf16[14,64,128]{2,1,0:T(8,128)(2,1)S(1)}, u32[]{:S(2)}, u32[]{:S(2)}) collective-permute-start(bf16[14,64,128]{2,1,0:T(8,128)(2,1)S(1)} %dynamic-slice_bitcast_fusion), channel_id=1, source_target_pairs={{0,2},{2,0},{1,3},{3,1},{4,6},{6,4},{5,7},{7,5},{8,10},{10,8},{9,1... | collective-permute-start | bytes 688136 | tf_op jit(solution)/shard_map/ppermute | solution.py:91
  6.8 0.7 %collective-permute-start.2 = (bf16[640,128]{1,0:T(8,128)(2,1)S(1)}, bf16[640,128]{1,0:T(8,128)(2,1)S(1)}, u32[]{:S(2)}, u32[]{:S(2)}) collective-permute-start(bf16[640,128]{1,0:T(8,128)(2,1)S(1)} %get-tuple-element.48), channel_id=1, source_target_pairs={{0,0},{1,4},{2,2},{3,6},{4,1},{5,5},{6,3},{7,7},{8,8},{9,12},{10,1... | collective-permute-start | bytes 491528 | tf_op jit(solution)/shard_map/ppermute | solution.py:431
  7.5 2.4 %collective-permute-start.3 = (bf16[512,128]{1,0:T(8,128)(2,1)S(1)}, bf16[512,128]{1,0:T(8,128)(2,1)S(1)}, u32[]{:S(2)}, u32[]{:S(2)}) collective-permute-start(bf16[512,128]{1,0:T(8,128)(2,1)S(1)} %bitcast.58), channel_id=1, source_target_pairs={{0,2},{1,6},{2,0},{3,4},{4,3},{5,7},{6,1},{7,5},{16,18},{17,22},{1... | collective-permute-start | bytes 393224 | tf_op jit(solution)/shard_map/ppermute | solution.py:432
  10.0 3.8 %collective-permute-done.late = bf16[640,128]{1,0:T(8,128)(2,1)S(1)} collective-permute-done((bf16[640,128]{1,0:T(8,128)(2,1)S(1)}, bf16[640,128]{1,0:T(8,128)(2,1)S(1)}, u32[]{:S(2)}, u32[]{:S(2)}) %collective-permute-start) | collective-permute-done | bytes 163872 | tf_op jit(solution)/shard_map/ppermute | solution.py:429
  13.8 1.6 %collective-permute-start.1 = (bf16[512,128]{1,0:T(8,128)(2,1)S(1)}, bf16[512,128]{1,0:T(8,128)(2,1)S(1)}, u32[]{:S(2)}, u32[]{:S(2)}) collective-permute-start(bf16[512,128]{1,0:T(8,128)(2,1)S(1)} %slice.40), channel_id=1, source_target_pairs={{0,2},{2,0},{1,3},{3,1},{4,6},{6,4},{5,7},{7,5},{8,10},{10,8},{9,1... | collective-permute-start | bytes 393224 | tf_op jit(solution)/shard_map/ppermute | solution.py:91
  15.4 0.0 collective-permute-done.5.near
  15.4 1.5 %collective-permute-start.6 = (bf16[14,64,128]{2,1,0:T(8,128)(2,1)S(1)}, bf16[14,64,128]{2,1,0:T(8,128)(2,1)S(1)}, u32[]{:S(2)}, u32[]{:S(2)}) collective-permute-start(bf16[14,64,128]{2,1,0:T(8,128)(2,1)S(1)} %collective-permute-done.5.near), channel_id=1, source_target_pairs={{0,16},{16,0},{1,17},{17,1},{2,18},{18,2},{3,19},{19,3},{4,20},{20... | collective-permute-start | bytes 688136 | tf_op jit(solution)/shard_map/ppermute | solution.py:91
  16.9 0.0 collective-permute-done.3.early_other
  16.9 0.0 collective-permute-done.2.early
  16.9 2.9 %collective-permute-done.1.late_other = bf16[512,128]{1,0:T(8,128)(2,1)S(1)} collective-permute-done((bf16[512,128]{1,0:T(8,128)(2,1)S(1)}, bf16[512,128]{1,0:T(8,128)(2,1)S(1)}, u32[]{:S(2)}, u32[]{:S(2)}) %collective-permute-start.1) | collective-permute-done | bytes 131104 | tf_op jit(solution)/shard_map/ppermute | solution.py:91
  19.8 0.1 collective-permute-start.4
  19.9 0.0 copy-start.5
  19.9 0.0 copy-start.6
  19.9 0.0 copy-start.7
  19.9 0.6 %copy-done.5 = f32[128]{0:T(128)S(1)} copy-done((f32[128]{0:T(128)S(1)}, f32[128]{0:T(128)}, u32[]{:S(2)}) %copy-start.5) | copy-done | bytes 536
  20.6 0.0 copy-done.6
  20.6 0.0 copy-done.7
  20.6 0.1 shard_map.82.own
  20.7 0.4 collective-permute-done.4.slabs
  21.1 0.4 shard_map.83.mine
  21.5 0.5 %collective-permute-done.6.far = bf16[14,64,128]{2,1,0:T(8,128)(2,1)S(1)} collective-permute-done((bf16[14,64,128]{2,1,0:T(8,128)(2,1)S(1)}, bf16[14,64,128]{2,1,0:T(8,128)(2,1)S(1)}, u32[]{:S(2)}, u32[]{:S(2)}) %collective-permute-start.6) | collective-permute-done | bytes 229408 | tf_op jit(solution)/shard_map/ppermute | solution.py:91
  22.0 1.9 %collective-permute-done.7.theirs = f32[1032,128]{1,0:T(8,128)S(1)} collective-permute-done((f32[1032,128]{1,0:T(8,128)S(1)}, f32[1032,128]{1,0:T(8,128)S(1)}, u32[]{:S(2)}, u32[]{:S(2)}) %collective-permute-start.7) | collective-permute-done | bytes 528416 | tf_op jit(solution)/shard_map/ppermute | solution.py:91
  24.0 2.2 %shard_map.84 = (bf16[2,2,256,128]{3,2,1,0:T(8,128)(2,1)S(1)}, f32[8,128]{1,0:T(8,128)S(1)}) custom-call(f32[1032,128]{1,0:T(8,128)S(1)} %shard_map.83.mine, f32[1032,128]{1,0:T(8,128)S(1)} %collective-permute-done.7.theirs, bf16[27,64,128]{2,1,0:T(8,128)(2,1)S(1)} %bitcast.53, bf16[14,64,128]{2,1,0:T(8,128)(2,1)S(1)} %collective-permute-done.5.near, ...), custom_call_target="tpu_custom_call" | custom-call | tf_op jit(solution)/shard_map/pallas_call | solution.py:314
  26.2 0.2 collective-permute-start.8
  26.4 1.1 %collective-permute-start.10 = (bf16[27,32,128]{2,1,0:T(8,128)(2,1)S(1)}, bf16[27,32,128]{2,1,0:T(8,128)(2,1)S(1)}, u32[]{:S(2)}, u32[]{:S(2)}) collective-permute-start(bf16[27,32,128]{2,1,0:T(8,128)(2,1)S(1)} %shard_map.82.own), channel_id=1, source_target_pairs={{0,2},{2,0},{1,3},{3,1},{4,6},{6,4},{5,7},{7,5},{8,10},{10,8},{9,1... | collective-permute-start | bytes 663560 | tf_op jit(solution)/shard_map/ppermute | solution.py:91
  27.5 0.1 collective-permute-done.8
  27.6 2.1 %collective-permute-start.9 = (bf16[256,128]{1,0:T(8,128)(2,1)S(1)}, bf16[256,128]{1,0:T(8,128)(2,1)S(1)}, u32[]{:S(2)}, u32[]{:S(2)}) collective-permute-start(bf16[256,128]{1,0:T(8,128)(2,1)S(1)} %get-tuple-element.43), channel_id=1, source_target_pairs={{0,12},{4,8},{8,4},{12,0},{1,13},{5,9},{9,5},{13,1},{2,14},{6,10},... | collective-permute-start | bytes 196616 | tf_op jit(solution)/shard_map/ppermute | solution.py:192
  29.7 2.4 %collective-permute-start.11 = (bf16[256,128]{1,0:T(8,128)(2,1)S(1)}, bf16[256,128]{1,0:T(8,128)(2,1)S(1)}, u32[]{:S(2)}, u32[]{:S(2)}) collective-permute-start(bf16[256,128]{1,0:T(8,128)(2,1)S(1)} %get-tuple-element.45), channel_id=1, source_target_pairs={{0,8},{4,12},{8,0},{12,4},{1,9},{5,13},{9,1},{13,5},{2,10},{6,14},... | collective-permute-start | bytes 196616 | tf_op jit(solution)/shard_map/ppermute | solution.py:192
  32.1 2.0 %collective-permute-done.10.other = bf16[27,32,128]{2,1,0:T(8,128)(2,1)S(1)} collective-permute-done((bf16[27,32,128]{2,1,0:T(8,128)(2,1)S(1)}, bf16[27,32,128]{2,1,0:T(8,128)(2,1)S(1)}, u32[]{:S(2)}, u32[]{:S(2)}) %collective-permute-start.10) | collective-permute-done | bytes 221216 | tf_op jit(solution)/shard_map/ppermute | solution.py:91
  34.1 0.4 collective-permute-done.9
  34.4 1.8 %collective-permute-done.12 = bf16[256,128]{1,0:T(8,128)(2,1)S(1)} collective-permute-done((bf16[256,128]{1,0:T(8,128)(2,1)S(1)}, bf16[256,128]{1,0:T(8,128)(2,1)S(1)}, u32[]{:S(2)}, u32[]{:S(2)}) %collective-permute-start.12) | collective-permute-done | bytes 65568 | tf_op jit(solution)/shard_map/ppermute | solution.py:192
  36.3 0.3 collective-permute-done.11
  36.6 0.1 multiply_convert_fusion
  36.6 0.1 collective-permute-start.13
  36.8 1.2 %collective-permute-done.13 = bf16[256,128]{1,0:T(8,128)(2,1)S(1)} collective-permute-done((bf16[256,128]{1,0:T(8,128)(2,1)S(1)}, bf16[256,128]{1,0:T(8,128)(2,1)S(1)}, u32[]{:S(2)}, u32[]{:S(2)}) %collective-permute-start.13) | collective-permute-done | bytes 65568 | tf_op jit(solution)/shard_map/ppermute | solution.py:91
  38.0 1.1 %shard_map.85 = (bf16[2,256,128]{2,1,0:T(8,128)(2,1)S(1)}, f32[8,128]{1,0:T(8,128)S(1)}, bf16[10,128,256]{2,1,0:T(8,128)(2,1)S(1)}, bf16[10,144,256]{2,1,0:T(8,128)(2,1)S(1)}, bf16[9,192,128]{2,1,0:T(8,128)(2,1)S(1)}) custom-call(bf16[2,256,128]{2,1,0:T(8,128)(2,1)S(1)} %pad_maximum_fusion.1.hidden, bf16[27,32,128]{2,1,0:T(8,128)(2,1)S(1)} %shard_map.82.own, ...), custom_call_target="tpu_custom_call" | custom-call | tf_op jit(solution)/shard_map/pallas_call | solution.py:375
  39.1 1.1 %collective-permute-start.15 = (bf16[256,128]{1,0:T(8,128)(2,1)S(1)}, bf16[256,128]{1,0:T(8,128)(2,1)S(1)}, u32[]{:S(2)}, u32[]{:S(2)}) collective-permute-start(bf16[256,128]{1,0:T(8,128)(2,1)S(1)} %get-tuple-element.50), channel_id=1, source_target_pairs={{0,8},{4,12},{8,0},{12,4},{1,9},{5,13},{9,1},{13,5},{2,10},{6,14},... | collective-permute-start | bytes 196616 | tf_op jit(solution)/shard_map/ppermute | solution.py:192
  40.2 1.8 %collective-permute-start.14 = (bf16[256,128]{1,0:T(8,128)(2,1)S(1)}, bf16[256,128]{1,0:T(8,128)(2,1)S(1)}, u32[]{:S(2)}, u32[]{:S(2)}) collective-permute-start(bf16[256,128]{1,0:T(8,128)(2,1)S(1)} %get-tuple-element.51), channel_id=1, source_target_pairs={{0,12},{4,8},{8,4},{12,0},{1,13},{5,9},{9,5},{13,1},{2,14},{6,10},... | collective-permute-start | bytes 196616 | tf_op jit(solution)/shard_map/ppermute | solution.py:192
  42.0 0.8 %shard_map.86 = bf16[2,256,128]{2,1,0:T(8,128)(2,1)S(1)} custom-call(bf16[10,128,256]{2,1,0:T(8,128)(2,1)S(1)} %get-tuple-element.39.even, bf16[10,144,256]{2,1,0:T(8,128)(2,1)S(1)} %get-tuple-element.40.odd, bf16[9,192,128]{2,1,0:T(8,128)(2,1)S(1)} %get-tuple-element.41.rights), custom_call_target="tpu_custom_call" | custom-call | tf_op jit(solution)/shard_map/pallas_call | solution.py:392
  42.8 0.8 %collective-permute-start.16 = (bf16[256,128]{1,0:T(8,128)(2,1)S(1)}, bf16[256,128]{1,0:T(8,128)(2,1)S(1)}, u32[]{:S(2)}, u32[]{:S(2)}) collective-permute-start(bf16[256,128]{1,0:T(8,128)(2,1)S(1)} %dynamic-slice_bitcast_fusion.2), channel_id=1, source_target_pairs={{0,4},{4,0},{8,12},{12,8},{1,5},{5,1},{9,13},{13,9},{2,6},{6,2},{1... | collective-permute-start | bytes 196616 | tf_op jit(solution)/shard_map/ppermute | solution.py:192
  43.5 4.8 %collective-permute-done.16 = bf16[256,128]{1,0:T(8,128)(2,1)S(1)} collective-permute-done((bf16[256,128]{1,0:T(8,128)(2,1)S(1)}, bf16[256,128]{1,0:T(8,128)(2,1)S(1)}, u32[]{:S(2)}, u32[]{:S(2)}) %collective-permute-start.16) | collective-permute-done | bytes 65568 | tf_op jit(solution)/shard_map/ppermute | solution.py:192
  48.3 0.0 collective-permute-done.15
  48.3 0.0 collective-permute-done.14
  48.3 0.7 %fusion.3 = bf16[256,128]{1,0:T(8,128)(2,1)} fusion(bf16[256,128]{1,0:T(8,128)(2,1)S(1)} %collective-permute-done.16, bf16[256,128]{1,0:T(8,128)(2,1)S(1)} %collective-permute-done.15, bf16[256,128]{1,0:T(8,128)(2,1)S(1)} %collective-permute-done.14, f32[128]{0:T(128)S(1)} %slice_bitcast_fusion.2, bf16[2,256,128]{2,1,0:T(8,128)(2,1)S(1)} %shard_map.86, ...), kind=kLoop, calls=%fused_computation.9 | loop fusion | flops 294912 | bytes 328196 | tf_op jit(solution)/shard_map/convert_element_type | solution.py:463
  (29 shorter events, 0.3 us)
Async XLA Ops:
  0.0 1.0 %copy-start.4 = (bf16[1,1,4,8,512]{4,3,2,1,0:T(8,128)(2,1)S(1)}, bf16[1,1,4,8,512]{4,3,2,1,0:T(8,128)(2,1)}, u32[]{:S(2)}) copy-start(bf16[1,1,4,8,512]{4,3,2,1,0:T(8,128)(2,1)} %param.8) | copy-start | bytes 98308
  0.0 1.0 %copy-start.3 = (bf16[1,2,16,8,128]{4,3,2,1,0:T(8,128)(2,1)S(1)}, bf16[1,2,16,8,128]{4,3,2,1,0:T(8,128)(2,1)}, u32[]{:S(2)}) copy-start(bf16[1,2,16,8,128]{4,3,2,1,0:T(8,128)(2,1)} %param.9) | copy-start | bytes 196612
  0.0 5.2 %copy-start = (bf16[27,128,1,64]{1,3,2,0:T(8,128)(2,1)S(1)}, bf16[27,128,1,64]{1,3,2,0:T(8,128)(2,1)}, u32[]{:S(2)}) copy-start(bf16[27,128,1,64]{1,3,2,0:T(8,128)(2,1)} %param.12) | copy-start | bytes 1327108
  1.1 6.4 %copy-start.2 = (bf16[8,128,1,64]{1,3,2,0:T(8,128)(2,1)S(1)}, bf16[8,128,1,64]{1,3,2,0:T(8,128)(2,1)}, u32[]{:S(2)}) copy-start(bf16[8,128,1,64]{1,3,2,0:T(8,128)(2,1)} %param.10) | copy-start | bytes 393220
  1.1 12.7 %collective-permute-start = (bf16[640,128]{1,0:T(8,128)(2,1)S(1)}, bf16[640,128]{1,0:T(8,128)(2,1)S(1)}, u32[]{:S(2)}, u32[]{:S(2)}) collective-permute-start(bf16[640,128]{1,0:T(8,128)(2,1)S(1)} %get-tuple-element.49), channel_id=1, source_target_pairs={{0,8},{1,12},{2,10},{3,14},{4,9},{5,13},{6,11},{7,15},{8,0},{9,4},... | collective-permute-start | bytes 491528 | tf_op jit(solution)/shard_map/ppermute | solution.py:429
  5.2 15.4 %copy-start.1 = (bf16[27,64,1,64]{3,1,2,0:T(8,128)(2,1)S(1)}, bf16[27,64,1,64]{3,1,2,0:T(8,128)(2,1)}, u32[]{:S(2)}) copy-start(bf16[27,64,1,64]{3,1,2,0:T(8,128)(2,1)} %param.14) | copy-start | bytes 663556
  5.3 10.1 %collective-permute-start.5 = (bf16[14,64,128]{2,1,0:T(8,128)(2,1)S(1)}, bf16[14,64,128]{2,1,0:T(8,128)(2,1)S(1)}, u32[]{:S(2)}, u32[]{:S(2)}) collective-permute-start(bf16[14,64,128]{2,1,0:T(8,128)(2,1)S(1)} %dynamic-slice_bitcast_fusion), channel_id=1, source_target_pairs={{0,2},{2,0},{1,3},{3,1},{4,6},{6,4},{5,7},{7,5},{8,10},{10,8},{9,1... | collective-permute-start | bytes 688136 | tf_op jit(solution)/shard_map/ppermute | solution.py:91
  6.8 10.1 %collective-permute-start.2 = (bf16[640,128]{1,0:T(8,128)(2,1)S(1)}, bf16[640,128]{1,0:T(8,128)(2,1)S(1)}, u32[]{:S(2)}, u32[]{:S(2)}) collective-permute-start(bf16[640,128]{1,0:T(8,128)(2,1)S(1)} %get-tuple-element.48), channel_id=1, source_target_pairs={{0,0},{1,4},{2,2},{3,6},{4,1},{5,5},{6,3},{7,7},{8,8},{9,12},{10,1... | collective-permute-start | bytes 491528 | tf_op jit(solution)/shard_map/ppermute | solution.py:431
  7.5 9.4 %collective-permute-start.3 = (bf16[512,128]{1,0:T(8,128)(2,1)S(1)}, bf16[512,128]{1,0:T(8,128)(2,1)S(1)}, u32[]{:S(2)}, u32[]{:S(2)}) collective-permute-start(bf16[512,128]{1,0:T(8,128)(2,1)S(1)} %bitcast.58), channel_id=1, source_target_pairs={{0,2},{1,6},{2,0},{3,4},{4,3},{5,7},{6,1},{7,5},{16,18},{17,22},{1... | collective-permute-start | bytes 393224 | tf_op jit(solution)/shard_map/ppermute | solution.py:432
  13.8 6.0 %collective-permute-start.1 = (bf16[512,128]{1,0:T(8,128)(2,1)S(1)}, bf16[512,128]{1,0:T(8,128)(2,1)S(1)}, u32[]{:S(2)}, u32[]{:S(2)}) collective-permute-start(bf16[512,128]{1,0:T(8,128)(2,1)S(1)} %slice.40), channel_id=1, source_target_pairs={{0,2},{2,0},{1,3},{3,1},{4,6},{6,4},{5,7},{7,5},{8,10},{10,8},{9,1... | collective-permute-start | bytes 393224 | tf_op jit(solution)/shard_map/ppermute | solution.py:91
  15.4 6.7 %collective-permute-start.6 = (bf16[14,64,128]{2,1,0:T(8,128)(2,1)S(1)}, bf16[14,64,128]{2,1,0:T(8,128)(2,1)S(1)}, u32[]{:S(2)}, u32[]{:S(2)}) collective-permute-start(bf16[14,64,128]{2,1,0:T(8,128)(2,1)S(1)} %collective-permute-done.5.near), channel_id=1, source_target_pairs={{0,16},{16,0},{1,17},{17,1},{2,18},{18,2},{3,19},{19,3},{4,20},{20... | collective-permute-start | bytes 688136 | tf_op jit(solution)/shard_map/ppermute | solution.py:91
  19.8 1.3 %collective-permute-start.4 = (bf16[2,128,128]{2,1,0:T(8,128)(2,1)S(1)}, bf16[2,128,128]{2,1,0:T(8,128)(2,1)S(1)}, u32[]{:S(2)}, u32[]{:S(2)}) collective-permute-start(bf16[2,128,128]{2,1,0:T(8,128)(2,1)S(1)} %pad_maximum_fusion.2), channel_id=1, source_target_pairs={{0,1},{1,0},{2,3},{3,2},{4,5},{5,4},{6,7},{7,6},{8,9},{9,8},{10,11... | collective-permute-start | bytes 196616 | tf_op jit(solution)/shard_map/ppermute | solution.py:91
  19.9 0.7 %copy-start.5 = (f32[128]{0:T(128)S(1)}, f32[128]{0:T(128)}, u32[]{:S(2)}) copy-start(f32[128]{0:T(128)} %param.15) | copy-start | bytes 1540
  19.9 0.7 %copy-start.6 = (f32[128]{0:T(128)S(1)}, f32[128]{0:T(128)}, u32[]{:S(2)}) copy-start(f32[128]{0:T(128)} %param.13) | copy-start | bytes 1540
  19.9 0.7 %copy-start.7 = (f32[128]{0:T(128)S(1)}, f32[128]{0:T(128)}, u32[]{:S(2)}) copy-start(f32[128]{0:T(128)} %param.11) | copy-start | bytes 1540
  22.0 1.9 %collective-permute-start.7 = (f32[1032,128]{1,0:T(8,128)S(1)}, f32[1032,128]{1,0:T(8,128)S(1)}, u32[]{:S(2)}, u32[]{:S(2)}) collective-permute-start(f32[1032,128]{1,0:T(8,128)S(1)} %shard_map.83.mine), channel_id=1, source_target_pairs={{0,1},{1,0},{2,3},{3,2},{4,5},{5,4},{6,7},{7,6},{8,9},{9,8},{10,11... | collective-permute-start | bytes 1585160 | tf_op jit(solution)/shard_map/ppermute | solution.py:91
  26.2 1.4 %collective-permute-start.8 = (bf16[2,256,128]{2,1,0:T(8,128)(2,1)S(1)}, bf16[2,256,128]{2,1,0:T(8,128)(2,1)S(1)}, u32[]{:S(2)}, u32[]{:S(2)}) collective-permute-start(bf16[2,256,128]{2,1,0:T(8,128)(2,1)S(1)} %get-tuple-element.47), channel_id=1, source_target_pairs={{0,1},{1,0},{2,3},{3,2},{4,5},{5,4},{6,7},{7,6},{8,9},{9,8},{10,11... | collective-permute-start | bytes 393224 | tf_op jit(solution)/shard_map/ppermute | solution.py:91
  26.4 7.7 %collective-permute-start.10 = (bf16[27,32,128]{2,1,0:T(8,128)(2,1)S(1)}, bf16[27,32,128]{2,1,0:T(8,128)(2,1)S(1)}, u32[]{:S(2)}, u32[]{:S(2)}) collective-permute-start(bf16[27,32,128]{2,1,0:T(8,128)(2,1)S(1)} %shard_map.82.own), channel_id=1, source_target_pairs={{0,2},{2,0},{1,3},{3,1},{4,6},{6,4},{5,7},{7,5},{8,10},{10,8},{9,1... | collective-permute-start | bytes 663560 | tf_op jit(solution)/shard_map/ppermute | solution.py:91
  27.6 6.8 %collective-permute-start.9 = (bf16[256,128]{1,0:T(8,128)(2,1)S(1)}, bf16[256,128]{1,0:T(8,128)(2,1)S(1)}, u32[]{:S(2)}, u32[]{:S(2)}) collective-permute-start(bf16[256,128]{1,0:T(8,128)(2,1)S(1)} %get-tuple-element.43), channel_id=1, source_target_pairs={{0,12},{4,8},{8,4},{12,0},{1,13},{5,9},{9,5},{13,1},{2,14},{6,10},... | collective-permute-start | bytes 196616 | tf_op jit(solution)/shard_map/ppermute | solution.py:192
  29.7 6.6 %collective-permute-start.12 = (bf16[256,128]{1,0:T(8,128)(2,1)S(1)}, bf16[256,128]{1,0:T(8,128)(2,1)S(1)}, u32[]{:S(2)}, u32[]{:S(2)}) collective-permute-start(bf16[256,128]{1,0:T(8,128)(2,1)S(1)} %get-tuple-element.44), channel_id=1, source_target_pairs={{0,4},{4,0},{8,12},{12,8},{1,5},{5,1},{9,13},{13,9},{2,6},{6,2},{1... | collective-permute-start | bytes 196616 | tf_op jit(solution)/shard_map/ppermute | solution.py:192
  29.7 6.9 %collective-permute-start.11 = (bf16[256,128]{1,0:T(8,128)(2,1)S(1)}, bf16[256,128]{1,0:T(8,128)(2,1)S(1)}, u32[]{:S(2)}, u32[]{:S(2)}) collective-permute-start(bf16[256,128]{1,0:T(8,128)(2,1)S(1)} %get-tuple-element.45), channel_id=1, source_target_pairs={{0,8},{4,12},{8,0},{12,4},{1,9},{5,13},{9,1},{13,5},{2,10},{6,14},... | collective-permute-start | bytes 196616 | tf_op jit(solution)/shard_map/ppermute | solution.py:192
  36.6 1.3 %collective-permute-start.13 = (bf16[256,128]{1,0:T(8,128)(2,1)S(1)}, bf16[256,128]{1,0:T(8,128)(2,1)S(1)}, u32[]{:S(2)}, u32[]{:S(2)}) collective-permute-start(bf16[256,128]{1,0:T(8,128)(2,1)S(1)} %multiply_convert_fusion), channel_id=1, source_target_pairs={{0,1},{1,0},{2,3},{3,2},{4,5},{5,4},{6,7},{7,6},{8,9},{9,8},{10,11... | collective-permute-start | bytes 196616 | tf_op jit(solution)/shard_map/ppermute | solution.py:91
  39.1 9.2 %collective-permute-start.15 = (bf16[256,128]{1,0:T(8,128)(2,1)S(1)}, bf16[256,128]{1,0:T(8,128)(2,1)S(1)}, u32[]{:S(2)}, u32[]{:S(2)}) collective-permute-start(bf16[256,128]{1,0:T(8,128)(2,1)S(1)} %get-tuple-element.50), channel_id=1, source_target_pairs={{0,8},{4,12},{8,0},{12,4},{1,9},{5,13},{9,1},{13,5},{2,10},{6,14},... | collective-permute-start | bytes 196616 | tf_op jit(solution)/shard_map/ppermute | solution.py:192
  40.2 8.2 %collective-permute-start.14 = (bf16[256,128]{1,0:T(8,128)(2,1)S(1)}, bf16[256,128]{1,0:T(8,128)(2,1)S(1)}, u32[]{:S(2)}, u32[]{:S(2)}) collective-permute-start(bf16[256,128]{1,0:T(8,128)(2,1)S(1)} %get-tuple-element.51), channel_id=1, source_target_pairs={{0,12},{4,8},{8,4},{12,0},{1,13},{5,9},{9,5},{13,1},{2,14},{6,10},... | collective-permute-start | bytes 196616 | tf_op jit(solution)/shard_map/ppermute | solution.py:192
  42.8 5.6 %collective-permute-start.16 = (bf16[256,128]{1,0:T(8,128)(2,1)S(1)}, bf16[256,128]{1,0:T(8,128)(2,1)S(1)}, u32[]{:S(2)}, u32[]{:S(2)}) collective-permute-start(bf16[256,128]{1,0:T(8,128)(2,1)S(1)} %dynamic-slice_bitcast_fusion.2), channel_id=1, source_target_pairs={{0,4},{4,0},{8,12},{12,8},{1,5},{5,1},{9,13},{13,9},{2,6},{6,2},{1... | collective-permute-start | bytes 196616 | tf_op jit(solution)/shard_map/ppermute | solution.py:192

commit v7 on v6

--- a/solution.py
+++ b/solution.py
@@ -183,6 +183,7 @@
         in_specs=[pl.BlockSpec(memory_space=pltpu.VMEM)] * 6,
         out_specs=pl.BlockSpec(memory_space=pltpu.VMEM),
         compiler_params=pltpu.CompilerParams(vmem_limit_bytes=32 * 2**20),
+        cost_estimate=pl.CostEstimate(flops=1000, bytes_accessed=1000, transcendentals=0),
     )(early, late, early_other, late_other, slabs, held)
 
 
@@ -252,24 +253,34 @@
     return total
 
 
-def first_right(own, near, far):
+def other_kernel(near, far, out):
     g = lax.axis_index("groups")
-    span, taps = (near.shape[0], own.shape[0])
-
-    def other(tap):
+    span, taps = (near.shape[0], out.shape[0])
+    for tap in range(taps):
         if tap < span:
             lower, upper = (near[tap], far[tap])
         else:
             lower, upper = (far[tap - taps + span], near[tap - taps + span])
         if tap == span - 1:
             upper = near[0]
-        return jnp.where(g == 0, lower, upper)
-
+        out[tap] = jnp.where(g == 0, lower, upper)
+
+
+def other_weights(near, far, taps):
+    return pl.pallas_call(
+        other_kernel,
+        out_shape=jax.ShapeDtypeStruct((taps,) + near.shape[1:], near.dtype),
+        in_specs=[pl.BlockSpec(memory_space=pltpu.VMEM)] * 2,
+        out_specs=pl.BlockSpec(memory_space=pltpu.VMEM),
+        compiler_params=pltpu.CompilerParams(vmem_limit_bytes=16 * 2**20),
+        cost_estimate=pl.CostEstimate(flops=10000000000, bytes_accessed=0, transcendentals=0),
+    )(near, far)
+
+
+def first_right(own, other):
     def right_of(group):
-        tap = 3 * group
-        return jnp.concatenate(
-            [jnp.concatenate([own[tap + i], other(tap + i)], axis=0) for i in range(3)], axis=1
-        )
+        pairs = [jnp.concatenate([own[i], other[i]], axis=0) for i in range(3 * group, 3 * group + 3)]
+        return jnp.concatenate(pairs, axis=1)
 
     return right_of
 
@@ -283,7 +294,7 @@
     out[q, 1] = jnp.where(lane < swap, pltpu.roll(low, swap, 1), high).astype(jnp.bfloat16)
 
 
-def first_kernel(mine, theirs, own, near, far, out, tile, even, odd):
+def first_kernel(mine, theirs, own, other, out, tile, even, odd):
     s, c = (lax.axis_index(a) for a in ("space", "chan"))
     rows = even.shape[1]
     half = mine.shape[1]
@@ -299,7 +310,7 @@
             yield x, jnp.concatenate([below, plane, above], axis=1)
 
     build_taps(planes_of, even, odd)
-    right_of = first_right(own, near, far)
+    right_of = first_right(own, other)
     for q in range(2):
         first_out(half_product(q, even, odd, right_of, NT), out, q)
     bias = jnp.where(s // 2 == c, mine[pl.ds(cells, 8)], theirs[pl.ds(cells, 8)])
@@ -308,7 +319,7 @@
     tile[...] = jnp.where((lane < half // 2) == (s % 2 == 0), bias, turned)
 
 
-def first_conv(mine, theirs, own, near, far, planes):
+def first_conv(mine, theirs, own, other, planes):
     cells, half = (mine.shape[0] - 8, mine.shape[1])
     rows = cells // planes
     return pl.pallas_call(
@@ -317,14 +328,14 @@
             jax.ShapeDtypeStruct((2, 2, cells // 4, half), jnp.bfloat16),
             jax.ShapeDtypeStruct((8, half), jnp.float32),
         ),
-        in_specs=[pl.BlockSpec(memory_space=pltpu.VMEM)] * 5,
+        in_specs=[pl.BlockSpec(memory_space=pltpu.VMEM)] * 4,
         out_specs=[pl.BlockSpec(memory_space=pltpu.VMEM)] * 2,
         scratch_shapes=[
             pltpu.VMEM((planes + 2, rows, 3 * half), jnp.bfloat16),
             pltpu.VMEM((planes + 2, rows + 16, 3 * half), jnp.bfloat16),
         ],
         compiler_params=pltpu.CompilerParams(vmem_limit_bytes=32 * 2**20),
-    )(mine, theirs, own, near, far)
+    )(mine, theirs, own, other)
 
 
 def second_far_kernel(hidden, own, other, held, out, tile, even, odd, rights):
@@ -431,7 +442,6 @@
     early = lax.ppermute(early, group, early_route)
     early_other = lax.ppermute(up_rows_own, group, cross_route)
     near = swapped(near, "dp")
-    late_other, early, early_other = lax.optimization_barrier((late_other, early, early_other))
     far = swapped(near, "groups")
     second_raw, late = lax.optimization_barrier((second_weight[:, :, 0, :], late))
     second_own = dense(second_raw)
@@ -439,9 +449,9 @@
     second_other = swapped(second_own, "dp")
     slabs = swapped(jnp.stack([early[up_rows:], late[up_rows:]]), "chan")
     part = up_part(early, late, early_other, late_other, slabs, held, fx * fy * fz)
-    part, far = lax.optimization_barrier((part, far))
     part_other = swapped(part, "chan")
-    first, tile = first_conv(part, part_other, first_own, near, far, fx)
+    first_other = other_weights(near, far, first_own.shape[0])
+    first, tile = first_conv(part, part_other, first_own, first_other, fx)
     mine, theirs = (pick(first, c), swapped(pick(first, 1 - c), "chan"))
     chunks = jnp.stack([mine, theirs]).reshape(4, block, half)
 

time: 49.2 us -> 48.6 us (0.988)
  waiting for transfers between devices: 20.1 us -> 17.9 us
  starting transfers between devices: 21.4 us -> 22.7 us
    ppermute x8, waiting for transfers between devices: 9 us -> 6.31 us  [swapped(): return lax.ppermute(array, axis, [(0, 1), (1, 0)])]
    ppermute x8, starting transfers between devices: 6.09 us -> 7.44 us  [swapped(): return lax.ppermute(array, axis, [(0, 1), (1, 0)])]
  transfers between devices with their start and end apart: 17 -> 17, of which waited for: 12 -> 9; matrix products, arithmetic and copies ran while one was open for 0% -> 0% of each run, Pallas kernels for 3% -> 3%
where the time goes in v7:
time: 48.6 us; the launch traced here: 48.4 us
  starting transfers between devices  22.7 us (47%)
  waiting for transfers between devices  17.9 us (37%)
  Pallas kernels  4.61 us (9%)
  local copies, waits for them, and re-layouts  1.81 us (4%)
  other arithmetic  0.89 us (2%)
    ppermute x6, starting transfers between devices, terms_of(): lax.ppermute(chunk, 'space', [(i, i ^ step) for i in range(4)])  8.07 us
    ppermute x6, waiting for transfers between devices, terms_of(): lax.ppermute(chunk, 'space', [(i, i ^ step) for i in range(4)])  7.79 us
    ppermute x8, starting transfers between devices, swapped(): return lax.ppermute(array, axis, [(0, 1), (1, 0)])  7.44 us
    ppermute x8, waiting for transfers between devices, swapped(): return lax.ppermute(array, axis, [(0, 1), (1, 0)])  6.31 us
    ppermute x1, starting transfers between devices, stationary(): late = lax.ppermute(late, group, late_route)  4.11 us
    ppermute x1, waiting for transfers between devices, stationary(): late = lax.ppermute(late, group, late_route)  3.83 us
    ppermute x1, starting transfers between devices, stationary(): early_other = lax.ppermute(up_rows_own, group, cross_route)  2.43 us
    pallas_call x1, Pallas kernels, first_conv(): pl.pallas_call(first_kernel, out_shape=(jax.ShapeDtypeStruct((2, 2, cells...  2.15 us
  transfers between devices with their start and end apart: 17, of which 9 were waited for; matrix products, arithmetic and copies ran while one was open for 0% of the time, Pallas kernels for 3%

profile of v7, /device:TPU:0, one launch (start us, length us, event | category | flops | bytes accessed | tf_op | source)
XLA Modules:
  0.0 48.4 jit_solution(6191468818788177906)
XLA Ops:
  0.0 1.0 %constant_dynamic-update-slice_fusion.4 = bf16[640,128]{1,0:T(8,128)(2,1)S(1)} fusion(bf16[512,128]{1,0:T(8,128)(2,1)} %bitcast.57), kind=kLoop, calls=%fused_computation.31 | loop fusion | bytes 262144
  1.1 0.1 pad_select_fusion
  1.1 0.0 copy-start.2
  1.1 4.1 %collective-permute-start.1 = (bf16[640,128]{1,0:T(8,128)(2,1)S(1)}, bf16[640,128]{1,0:T(8,128)(2,1)S(1)}, u32[]{:S(2)}, u32[]{:S(2)}) collective-permute-start(bf16[640,128]{1,0:T(8,128)(2,1)S(1)} %get-tuple-element.38), channel_id=1, source_target_pairs={{0,8},{1,12},{2,10},{3,14},{4,9},{5,13},{6,11},{7,15},{8,0},{9,4},... | collective-permute-start | bytes 491528 | tf_op jit(solution)/shard_map/ppermute | solution.py:440
  5.3 1.6 %collective-permute-start.6 = (bf16[14,64,128]{2,1,0:T(8,128)(2,1)S(1)}, bf16[14,64,128]{2,1,0:T(8,128)(2,1)S(1)}, u32[]{:S(2)}, u32[]{:S(2)}) collective-permute-start(bf16[14,64,128]{2,1,0:T(8,128)(2,1)S(1)} %dynamic-slice_bitcast_fusion), channel_id=1, source_target_pairs={{0,2},{2,0},{1,3},{3,1},{4,6},{6,4},{5,7},{7,5},{8,10},{10,8},{9,1... | collective-permute-start | bytes 688136 | tf_op jit(solution)/shard_map/ppermute | solution.py:91
  6.8 2.4 %collective-permute-start.2 = (bf16[512,128]{1,0:T(8,128)(2,1)S(1)}, bf16[512,128]{1,0:T(8,128)(2,1)S(1)}, u32[]{:S(2)}, u32[]{:S(2)}) collective-permute-start(bf16[512,128]{1,0:T(8,128)(2,1)S(1)} %bitcast.58), channel_id=1, source_target_pairs={{0,2},{1,6},{2,0},{3,4},{4,3},{5,7},{6,1},{7,5},{16,18},{17,22},{1... | collective-permute-start | bytes 393224 | tf_op jit(solution)/shard_map/ppermute | solution.py:443
  9.3 0.7 %collective-permute-start = (bf16[640,128]{1,0:T(8,128)(2,1)S(1)}, bf16[640,128]{1,0:T(8,128)(2,1)S(1)}, u32[]{:S(2)}, u32[]{:S(2)}) collective-permute-start(bf16[640,128]{1,0:T(8,128)(2,1)S(1)} %get-tuple-element.39), channel_id=1, source_target_pairs={{0,0},{1,4},{2,2},{3,6},{4,1},{5,5},{6,3},{7,7},{8,8},{9,12},{10,1... | collective-permute-start | bytes 491528 | tf_op jit(solution)/shard_map/ppermute | solution.py:442
  10.0 3.8 %collective-permute-done.1.late = bf16[640,128]{1,0:T(8,128)(2,1)S(1)} collective-permute-done((bf16[640,128]{1,0:T(8,128)(2,1)S(1)}, bf16[640,128]{1,0:T(8,128)(2,1)S(1)}, u32[]{:S(2)}, u32[]{:S(2)}) %collective-permute-start.1) | collective-permute-done | bytes 163872 | tf_op jit(solution)/shard_map/ppermute | solution.py:440
  13.8 1.6 %collective-permute-start.3 = (bf16[512,128]{1,0:T(8,128)(2,1)S(1)}, bf16[512,128]{1,0:T(8,128)(2,1)S(1)}, u32[]{:S(2)}, u32[]{:S(2)}) collective-permute-start(bf16[512,128]{1,0:T(8,128)(2,1)S(1)} %slice.40), channel_id=1, source_target_pairs={{0,2},{2,0},{1,3},{3,1},{4,6},{6,4},{5,7},{7,5},{8,10},{10,8},{9,1... | collective-permute-start | bytes 393224 | tf_op jit(solution)/shard_map/ppermute | solution.py:91
  15.4 0.0 collective-permute-done.6.near
  15.4 1.5 %collective-permute-start.7 = (bf16[14,64,128]{2,1,0:T(8,128)(2,1)S(1)}, bf16[14,64,128]{2,1,0:T(8,128)(2,1)S(1)}, u32[]{:S(2)}, u32[]{:S(2)}) collective-permute-start(bf16[14,64,128]{2,1,0:T(8,128)(2,1)S(1)} %collective-permute-done.6.near), channel_id=1, source_target_pairs={{0,16},{16,0},{1,17},{17,1},{2,18},{18,2},{3,19},{19,3},{4,20},{20... | collective-permute-start | bytes 688136 | tf_op jit(solution)/shard_map/ppermute | solution.py:91
  16.9 0.0 collective-permute-done.early
  16.9 0.1 collective-permute-start.4
  17.0 0.0 copy-start.5
  17.0 0.0 copy-start.6
  17.0 0.0 copy-start.7
  17.0 0.6 %copy-done.5 = f32[128]{0:T(128)S(1)} copy-done((f32[128]{0:T(128)S(1)}, f32[128]{0:T(128)}, u32[]{:S(2)}) %copy-start.5) | copy-done | bytes 536
  17.6 0.0 copy-done.6
  17.7 0.0 copy-done.7
  17.7 0.1 shard_map.82.own
  17.8 1.6 %collective-permute-done.3.late_other = bf16[512,128]{1,0:T(8,128)(2,1)S(1)} collective-permute-done((bf16[512,128]{1,0:T(8,128)(2,1)S(1)}, bf16[512,128]{1,0:T(8,128)(2,1)S(1)}, u32[]{:S(2)}, u32[]{:S(2)}) %collective-permute-start.3) | collective-permute-done | bytes 131104 | tf_op jit(solution)/shard_map/ppermute | solution.py:91
  19.4 0.0 collective-permute-done.2.early_other
  19.4 0.4 shard_map.83.mine
  19.8 0.1 collective-permute-start.5
  19.9 2.1 %collective-permute-done.7.far = bf16[14,64,128]{2,1,0:T(8,128)(2,1)S(1)} collective-permute-done((bf16[14,64,128]{2,1,0:T(8,128)(2,1)S(1)}, bf16[14,64,128]{2,1,0:T(8,128)(2,1)S(1)}, u32[]{:S(2)}, u32[]{:S(2)}) %collective-permute-start.7) | collective-permute-done | bytes 229408 | tf_op jit(solution)/shard_map/ppermute | solution.py:91
  22.0 0.1 shard_map.84.other
  22.1 0.0 collective-permute-done.5.theirs
  22.1 2.2 %shard_map.85 = (bf16[2,2,256,128]{3,2,1,0:T(8,128)(2,1)S(1)}, f32[8,128]{1,0:T(8,128)S(1)}) custom-call(f32[1032,128]{1,0:T(8,128)S(1)} %shard_map.83.mine, f32[1032,128]{1,0:T(8,128)S(1)} %collective-permute-done.5.theirs, bf16[27,64,128]{2,1,0:T(8,128)(2,1)S(1)} %bitcast.53, bf16[27,64,128]{2,1,0:T(8,128)(2,1)S(1)} %shard_map.84.other), custom_call_target="tpu_custom_call" | custom-call | tf_op jit(solution)/shard_map/pallas_call | solution.py:325
  24.3 0.1 collective-permute-start.8
  24.6 2.5 %collective-permute-start.10 = (bf16[27,32,128]{2,1,0:T(8,128)(2,1)S(1)}, bf16[27,32,128]{2,1,0:T(8,128)(2,1)S(1)}, u32[]{:S(2)}, u32[]{:S(2)}) collective-permute-start(bf16[27,32,128]{2,1,0:T(8,128)(2,1)S(1)} %shard_map.82.own), channel_id=1, source_target_pairs={{0,2},{2,0},{1,3},{3,1},{4,6},{6,4},{5,7},{7,5},{8,10},{10,8},{9,1... | collective-permute-start | bytes 663560 | tf_op jit(solution)/shard_map/ppermute | solution.py:91
  27.2 0.7 %collective-permute-start.9 = (bf16[256,128]{1,0:T(8,128)(2,1)S(1)}, bf16[256,128]{1,0:T(8,128)(2,1)S(1)}, u32[]{:S(2)}, u32[]{:S(2)}) collective-permute-start(bf16[256,128]{1,0:T(8,128)(2,1)S(1)} %get-tuple-element.33), channel_id=1, source_target_pairs={{0,12},{4,8},{8,4},{12,0},{1,13},{5,9},{9,5},{13,1},{2,14},{6,10},... | collective-permute-start | bytes 196616 | tf_op jit(solution)/shard_map/ppermute | solution.py:193
  27.8 3.8 %collective-permute-start.11 = (bf16[256,128]{1,0:T(8,128)(2,1)S(1)}, bf16[256,128]{1,0:T(8,128)(2,1)S(1)}, u32[]{:S(2)}, u32[]{:S(2)}) collective-permute-start(bf16[256,128]{1,0:T(8,128)(2,1)S(1)} %get-tuple-element.35), channel_id=1, source_target_pairs={{0,8},{4,12},{8,0},{12,4},{1,9},{5,13},{9,1},{13,5},{2,10},{6,14},... | collective-permute-start | bytes 196616 | tf_op jit(solution)/shard_map/ppermute | solution.py:193
  31.6 1.4 %collective-permute-done.10.other = bf16[27,32,128]{2,1,0:T(8,128)(2,1)S(1)} collective-permute-done((bf16[27,32,128]{2,1,0:T(8,128)(2,1)S(1)}, bf16[27,32,128]{2,1,0:T(8,128)(2,1)S(1)}, u32[]{:S(2)}, u32[]{:S(2)}) %collective-permute-start.10) | collective-permute-done | bytes 221216 | tf_op jit(solution)/shard_map/ppermute | solution.py:91
  33.0 1.0 %collective-permute-done.9 = bf16[256,128]{1,0:T(8,128)(2,1)S(1)} collective-permute-done((bf16[256,128]{1,0:T(8,128)(2,1)S(1)}, bf16[256,128]{1,0:T(8,128)(2,1)S(1)}, u32[]{:S(2)}, u32[]{:S(2)}) %collective-permute-start.9) | collective-permute-done | bytes 65568 | tf_op jit(solution)/shard_map/ppermute | solution.py:193
  34.0 0.4 collective-permute-done.12
  34.3 1.5 %collective-permute-done.11 = bf16[256,128]{1,0:T(8,128)(2,1)S(1)} collective-permute-done((bf16[256,128]{1,0:T(8,128)(2,1)S(1)}, bf16[256,128]{1,0:T(8,128)(2,1)S(1)}, u32[]{:S(2)}, u32[]{:S(2)}) %collective-permute-start.11) | collective-permute-done | bytes 65568 | tf_op jit(solution)/shard_map/ppermute | solution.py:193
  35.9 0.1 multiply_convert_fusion
  36.0 0.1 collective-permute-start.13
  36.1 1.2 %collective-permute-done.13 = bf16[256,128]{1,0:T(8,128)(2,1)S(1)} collective-permute-done((bf16[256,128]{1,0:T(8,128)(2,1)S(1)}, bf16[256,128]{1,0:T(8,128)(2,1)S(1)}, u32[]{:S(2)}, u32[]{:S(2)}) %collective-permute-start.13) | collective-permute-done | bytes 65568 | tf_op jit(solution)/shard_map/ppermute | solution.py:91
  37.3 1.1 %shard_map.86 = (bf16[2,256,128]{2,1,0:T(8,128)(2,1)S(1)}, f32[8,128]{1,0:T(8,128)S(1)}, bf16[10,128,256]{2,1,0:T(8,128)(2,1)S(1)}, bf16[10,144,256]{2,1,0:T(8,128)(2,1)S(1)}, bf16[9,192,128]{2,1,0:T(8,128)(2,1)S(1)}) custom-call(bf16[2,256,128]{2,1,0:T(8,128)(2,1)S(1)} %pad_maximum_fusion.1.hidden, bf16[27,32,128]{2,1,0:T(8,128)(2,1)S(1)} %shard_map.82.own, ...), custom_call_target="tpu_custom_call" | custom-call | tf_op jit(solution)/shard_map/pallas_call | solution.py:386
  38.4 1.0 %collective-permute-start.15 = (bf16[256,128]{1,0:T(8,128)(2,1)S(1)}, bf16[256,128]{1,0:T(8,128)(2,1)S(1)}, u32[]{:S(2)}, u32[]{:S(2)}) collective-permute-start(bf16[256,128]{1,0:T(8,128)(2,1)S(1)} %get-tuple-element.40), channel_id=1, source_target_pairs={{0,8},{4,12},{8,0},{12,4},{1,9},{5,13},{9,1},{13,5},{2,10},{6,14},... | collective-permute-start | bytes 196616 | tf_op jit(solution)/shard_map/ppermute | solution.py:193
  39.4 2.0 %collective-permute-start.14 = (bf16[256,128]{1,0:T(8,128)(2,1)S(1)}, bf16[256,128]{1,0:T(8,128)(2,1)S(1)}, u32[]{:S(2)}, u32[]{:S(2)}) collective-permute-start(bf16[256,128]{1,0:T(8,128)(2,1)S(1)} %get-tuple-element.41), channel_id=1, source_target_pairs={{0,12},{4,8},{8,4},{12,0},{1,13},{5,9},{9,5},{13,1},{2,14},{6,10},... | collective-permute-start | bytes 196616 | tf_op jit(solution)/shard_map/ppermute | solution.py:193
  41.4 0.8 %shard_map.87 = bf16[2,256,128]{2,1,0:T(8,128)(2,1)S(1)} custom-call(bf16[10,128,256]{2,1,0:T(8,128)(2,1)S(1)} %get-tuple-element.29.even, bf16[10,144,256]{2,1,0:T(8,128)(2,1)S(1)} %get-tuple-element.30.odd, bf16[9,192,128]{2,1,0:T(8,128)(2,1)S(1)} %get-tuple-element.31.rights), custom_call_target="tpu_custom_call" | custom-call | tf_op jit(solution)/shard_map/pallas_call | solution.py:403
  42.2 0.7 %collective-permute-start.16 = (bf16[256,128]{1,0:T(8,128)(2,1)S(1)}, bf16[256,128]{1,0:T(8,128)(2,1)S(1)}, u32[]{:S(2)}, u32[]{:S(2)}) collective-permute-start(bf16[256,128]{1,0:T(8,128)(2,1)S(1)} %dynamic-slice_bitcast_fusion.2), channel_id=1, source_target_pairs={{0,4},{4,0},{8,12},{12,8},{1,5},{5,1},{9,13},{13,9},{2,6},{6,2},{1... | collective-permute-start | bytes 196616 | tf_op jit(solution)/shard_map/ppermute | solution.py:193
  42.8 4.9 %collective-permute-done.16 = bf16[256,128]{1,0:T(8,128)(2,1)S(1)} collective-permute-done((bf16[256,128]{1,0:T(8,128)(2,1)S(1)}, bf16[256,128]{1,0:T(8,128)(2,1)S(1)}, u32[]{:S(2)}, u32[]{:S(2)}) %collective-permute-start.16) | collective-permute-done | bytes 65568 | tf_op jit(solution)/shard_map/ppermute | solution.py:193
  47.7 0.0 collective-permute-done.15
  47.7 0.0 collective-permute-done.14
  47.7 0.7 %fusion.3 = bf16[256,128]{1,0:T(8,128)(2,1)} fusion(bf16[256,128]{1,0:T(8,128)(2,1)S(1)} %collective-permute-done.16, bf16[256,128]{1,0:T(8,128)(2,1)S(1)} %collective-permute-done.15, bf16[256,128]{1,0:T(8,128)(2,1)S(1)} %collective-permute-done.14, f32[128]{0:T(128)S(1)} %slice_bitcast_fusion.2, bf16[2,256,128]{2,1,0:T(8,128)(2,1)S(1)} %shard_map.87, ...), kind=kLoop, calls=%fused_computation.9 | loop fusion | flops 294912 | bytes 328196 | tf_op jit(solution)/shard_map/convert_element_type | solution.py:473
  (31 shorter events, 0.3 us)
Async XLA Ops:
  0.0 1.0 %copy-start.4 = (bf16[1,1,4,8,512]{4,3,2,1,0:T(8,128)(2,1)S(1)}, bf16[1,1,4,8,512]{4,3,2,1,0:T(8,128)(2,1)}, u32[]{:S(2)}) copy-start(bf16[1,1,4,8,512]{4,3,2,1,0:T(8,128)(2,1)} %param.8) | copy-start | bytes 98308
  0.0 1.0 %copy-start.3 = (bf16[1,2,16,8,128]{4,3,2,1,0:T(8,128)(2,1)S(1)}, bf16[1,2,16,8,128]{4,3,2,1,0:T(8,128)(2,1)}, u32[]{:S(2)}) copy-start(bf16[1,2,16,8,128]{4,3,2,1,0:T(8,128)(2,1)} %param.9) | copy-start | bytes 196612
  0.0 5.2 %copy-start = (bf16[27,128,1,64]{1,3,2,0:T(8,128)(2,1)S(1)}, bf16[27,128,1,64]{1,3,2,0:T(8,128)(2,1)}, u32[]{:S(2)}) copy-start(bf16[27,128,1,64]{1,3,2,0:T(8,128)(2,1)} %param.12) | copy-start | bytes 1327108
  1.1 5.7 %copy-start.2 = (bf16[8,128,1,64]{1,3,2,0:T(8,128)(2,1)S(1)}, bf16[8,128,1,64]{1,3,2,0:T(8,128)(2,1)}, u32[]{:S(2)}) copy-start(bf16[8,128,1,64]{1,3,2,0:T(8,128)(2,1)} %param.10) | copy-start | bytes 393220
  1.1 12.6 %collective-permute-start.1 = (bf16[640,128]{1,0:T(8,128)(2,1)S(1)}, bf16[640,128]{1,0:T(8,128)(2,1)S(1)}, u32[]{:S(2)}, u32[]{:S(2)}) collective-permute-start(bf16[640,128]{1,0:T(8,128)(2,1)S(1)} %get-tuple-element.38), channel_id=1, source_target_pairs={{0,8},{1,12},{2,10},{3,14},{4,9},{5,13},{6,11},{7,15},{8,0},{9,4},... | collective-permute-start | bytes 491528 | tf_op jit(solution)/shard_map/ppermute | solution.py:440
  5.2 12.4 %copy-start.1 = (bf16[27,64,1,64]{3,1,2,0:T(8,128)(2,1)S(1)}, bf16[27,64,1,64]{3,1,2,0:T(8,128)(2,1)}, u32[]{:S(2)}) copy-start(bf16[27,64,1,64]{3,1,2,0:T(8,128)(2,1)} %param.14) | copy-start | bytes 663556
  5.3 10.1 %collective-permute-start.6 = (bf16[14,64,128]{2,1,0:T(8,128)(2,1)S(1)}, bf16[14,64,128]{2,1,0:T(8,128)(2,1)S(1)}, u32[]{:S(2)}, u32[]{:S(2)}) collective-permute-start(bf16[14,64,128]{2,1,0:T(8,128)(2,1)S(1)} %dynamic-slice_bitcast_fusion), channel_id=1, source_target_pairs={{0,2},{2,0},{1,3},{3,1},{4,6},{6,4},{5,7},{7,5},{8,10},{10,8},{9,1... | collective-permute-start | bytes 688136 | tf_op jit(solution)/shard_map/ppermute | solution.py:91
  6.8 12.6 %collective-permute-start.2 = (bf16[512,128]{1,0:T(8,128)(2,1)S(1)}, bf16[512,128]{1,0:T(8,128)(2,1)S(1)}, u32[]{:S(2)}, u32[]{:S(2)}) collective-permute-start(bf16[512,128]{1,0:T(8,128)(2,1)S(1)} %bitcast.58), channel_id=1, source_target_pairs={{0,2},{1,6},{2,0},{3,4},{4,3},{5,7},{6,1},{7,5},{16,18},{17,22},{1... | collective-permute-start | bytes 393224 | tf_op jit(solution)/shard_map/ppermute | solution.py:443
  9.3 7.6 %collective-permute-start = (bf16[640,128]{1,0:T(8,128)(2,1)S(1)}, bf16[640,128]{1,0:T(8,128)(2,1)S(1)}, u32[]{:S(2)}, u32[]{:S(2)}) collective-permute-start(bf16[640,128]{1,0:T(8,128)(2,1)S(1)} %get-tuple-element.39), channel_id=1, source_target_pairs={{0,0},{1,4},{2,2},{3,6},{4,1},{5,5},{6,3},{7,7},{8,8},{9,12},{10,1... | collective-permute-start | bytes 491528 | tf_op jit(solution)/shard_map/ppermute | solution.py:442
  13.8 5.6 %collective-permute-start.3 = (bf16[512,128]{1,0:T(8,128)(2,1)S(1)}, bf16[512,128]{1,0:T(8,128)(2,1)S(1)}, u32[]{:S(2)}, u32[]{:S(2)}) collective-permute-start(bf16[512,128]{1,0:T(8,128)(2,1)S(1)} %slice.40), channel_id=1, source_target_pairs={{0,2},{2,0},{1,3},{3,1},{4,6},{6,4},{5,7},{7,5},{8,10},{10,8},{9,1... | collective-permute-start | bytes 393224 | tf_op jit(solution)/shard_map/ppermute | solution.py:91
  15.4 6.7 %collective-permute-start.7 = (bf16[14,64,128]{2,1,0:T(8,128)(2,1)S(1)}, bf16[14,64,128]{2,1,0:T(8,128)(2,1)S(1)}, u32[]{:S(2)}, u32[]{:S(2)}) collective-permute-start(bf16[14,64,128]{2,1,0:T(8,128)(2,1)S(1)} %collective-permute-done.6.near), channel_id=1, source_target_pairs={{0,16},{16,0},{1,17},{17,1},{2,18},{18,2},{3,19},{19,3},{4,20},{20... | collective-permute-start | bytes 688136 | tf_op jit(solution)/shard_map/ppermute | solution.py:91
  16.9 2.5 %collective-permute-start.4 = (bf16[2,128,128]{2,1,0:T(8,128)(2,1)S(1)}, bf16[2,128,128]{2,1,0:T(8,128)(2,1)S(1)}, u32[]{:S(2)}, u32[]{:S(2)}) collective-permute-start(bf16[2,128,128]{2,1,0:T(8,128)(2,1)S(1)} %pad_maximum_fusion.2), channel_id=1, source_target_pairs={{0,1},{1,0},{2,3},{3,2},{4,5},{5,4},{6,7},{7,6},{8,9},{9,8},{10,11... | collective-permute-start | bytes 196616 | tf_op jit(solution)/shard_map/ppermute | solution.py:91
  17.0 0.7 %copy-start.5 = (f32[128]{0:T(128)S(1)}, f32[128]{0:T(128)}, u32[]{:S(2)}) copy-start(f32[128]{0:T(128)} %param.15) | copy-start | bytes 1540
  17.0 0.7 %copy-start.6 = (f32[128]{0:T(128)S(1)}, f32[128]{0:T(128)}, u32[]{:S(2)}) copy-start(f32[128]{0:T(128)} %param.13) | copy-start | bytes 1540
  17.0 0.7 %copy-start.7 = (f32[128]{0:T(128)S(1)}, f32[128]{0:T(128)}, u32[]{:S(2)}) copy-start(f32[128]{0:T(128)} %param.11) | copy-start | bytes 1540
  19.8 2.3 %collective-permute-start.5 = (f32[1032,128]{1,0:T(8,128)S(1)}, f32[1032,128]{1,0:T(8,128)S(1)}, u32[]{:S(2)}, u32[]{:S(2)}) collective-permute-start(f32[1032,128]{1,0:T(8,128)S(1)} %shard_map.83.mine), channel_id=1, source_target_pairs={{0,1},{1,0},{2,3},{3,2},{4,5},{5,4},{6,7},{7,6},{8,9},{9,8},{10,11... | collective-permute-start | bytes 1585160 | tf_op jit(solution)/shard_map/ppermute | solution.py:91
  24.3 2.8 %collective-permute-start.8 = (bf16[2,256,128]{2,1,0:T(8,128)(2,1)S(1)}, bf16[2,256,128]{2,1,0:T(8,128)(2,1)S(1)}, u32[]{:S(2)}, u32[]{:S(2)}) collective-permute-start(bf16[2,256,128]{2,1,0:T(8,128)(2,1)S(1)} %get-tuple-element.37), channel_id=1, source_target_pairs={{0,1},{1,0},{2,3},{3,2},{4,5},{5,4},{6,7},{7,6},{8,9},{9,8},{10,11... | collective-permute-start | bytes 393224 | tf_op jit(solution)/shard_map/ppermute | solution.py:91
  24.6 8.4 %collective-permute-start.10 = (bf16[27,32,128]{2,1,0:T(8,128)(2,1)S(1)}, bf16[27,32,128]{2,1,0:T(8,128)(2,1)S(1)}, u32[]{:S(2)}, u32[]{:S(2)}) collective-permute-start(bf16[27,32,128]{2,1,0:T(8,128)(2,1)S(1)} %shard_map.82.own), channel_id=1, source_target_pairs={{0,2},{2,0},{1,3},{3,1},{4,6},{6,4},{5,7},{7,5},{8,10},{10,8},{9,1... | collective-permute-start | bytes 663560 | tf_op jit(solution)/shard_map/ppermute | solution.py:91
  27.2 6.8 %collective-permute-start.9 = (bf16[256,128]{1,0:T(8,128)(2,1)S(1)}, bf16[256,128]{1,0:T(8,128)(2,1)S(1)}, u32[]{:S(2)}, u32[]{:S(2)}) collective-permute-start(bf16[256,128]{1,0:T(8,128)(2,1)S(1)} %get-tuple-element.33), channel_id=1, source_target_pairs={{0,12},{4,8},{8,4},{12,0},{1,13},{5,9},{9,5},{13,1},{2,14},{6,10},... | collective-permute-start | bytes 196616 | tf_op jit(solution)/shard_map/ppermute | solution.py:193
  27.8 6.5 %collective-permute-start.12 = (bf16[256,128]{1,0:T(8,128)(2,1)S(1)}, bf16[256,128]{1,0:T(8,128)(2,1)S(1)}, u32[]{:S(2)}, u32[]{:S(2)}) collective-permute-start(bf16[256,128]{1,0:T(8,128)(2,1)S(1)} %get-tuple-element.34), channel_id=1, source_target_pairs={{0,4},{4,0},{8,12},{12,8},{1,5},{5,1},{9,13},{13,9},{2,6},{6,2},{1... | collective-permute-start | bytes 196616 | tf_op jit(solution)/shard_map/ppermute | solution.py:193
  27.8 8.0 %collective-permute-start.11 = (bf16[256,128]{1,0:T(8,128)(2,1)S(1)}, bf16[256,128]{1,0:T(8,128)(2,1)S(1)}, u32[]{:S(2)}, u32[]{:S(2)}) collective-permute-start(bf16[256,128]{1,0:T(8,128)(2,1)S(1)} %get-tuple-element.35), channel_id=1, source_target_pairs={{0,8},{4,12},{8,0},{12,4},{1,9},{5,13},{9,1},{13,5},{2,10},{6,14},... | collective-permute-start | bytes 196616 | tf_op jit(solution)/shard_map/ppermute | solution.py:193
  36.0 1.3 %collective-permute-start.13 = (bf16[256,128]{1,0:T(8,128)(2,1)S(1)}, bf16[256,128]{1,0:T(8,128)(2,1)S(1)}, u32[]{:S(2)}, u32[]{:S(2)}) collective-permute-start(bf16[256,128]{1,0:T(8,128)(2,1)S(1)} %multiply_convert_fusion), channel_id=1, source_target_pairs={{0,1},{1,0},{2,3},{3,2},{4,5},{5,4},{6,7},{7,6},{8,9},{9,8},{10,11... | collective-permute-start | bytes 196616 | tf_op jit(solution)/shard_map/ppermute | solution.py:91
  38.4 9.3 %collective-permute-start.15 = (bf16[256,128]{1,0:T(8,128)(2,1)S(1)}, bf16[256,128]{1,0:T(8,128)(2,1)S(1)}, u32[]{:S(2)}, u32[]{:S(2)}) collective-permute-start(bf16[256,128]{1,0:T(8,128)(2,1)S(1)} %get-tuple-element.40), channel_id=1, source_target_pairs={{0,8},{4,12},{8,0},{12,4},{1,9},{5,13},{9,1},{13,5},{2,10},{6,14},... | collective-permute-start | bytes 196616 | tf_op jit(solution)/shard_map/ppermute | solution.py:193
  39.4 8.3 %collective-permute-start.14 = (bf16[256,128]{1,0:T(8,128)(2,1)S(1)}, bf16[256,128]{1,0:T(8,128)(2,1)S(1)}, u32[]{:S(2)}, u32[]{:S(2)}) collective-permute-start(bf16[256,128]{1,0:T(8,128)(2,1)S(1)} %get-tuple-element.41), channel_id=1, source_target_pairs={{0,12},{4,8},{8,4},{12,0},{1,13},{5,9},{9,5},{13,1},{2,14},{6,10},... | collective-permute-start | bytes 196616 | tf_op jit(solution)/shard_map/ppermute | solution.py:193
  42.2 5.6 %collective-permute-start.16 = (bf16[256,128]{1,0:T(8,128)(2,1)S(1)}, bf16[256,128]{1,0:T(8,128)(2,1)S(1)}, u32[]{:S(2)}, u32[]{:S(2)}) collective-permute-start(bf16[256,128]{1,0:T(8,128)(2,1)S(1)} %dynamic-slice_bitcast_fusion.2), channel_id=1, source_target_pairs={{0,4},{4,0},{8,12},{12,8},{1,5},{5,1},{9,13},{13,9},{2,6},{6,2},{1... | collective-permute-start | bytes 196616 | tf_op jit(solution)/shard_map/ppermute | solution.py:193

commit v8 on v7

--- a/solution.py
+++ b/solution.py
@@ -453,13 +453,13 @@
     first_other = other_weights(near, far, first_own.shape[0])
     first, tile = first_conv(part, part_other, first_own, first_other, fx)
     mine, theirs = (pick(first, c), swapped(pick(first, 1 - c), "chan"))
+    theirs, second_other = lax.optimization_barrier((theirs, second_other))
     chunks = jnp.stack([mine, theirs]).reshape(4, block, half)
 
     def chunk_for(plane):
         return pick(chunks, 2 * ((plane // 2) ^ c) + ((plane % 2) ^ d))
 
     terms = terms_of([(step, chunk_for(s ^ step)) for step in (3, 2, 1)])
-    terms[0], second_other = lax.optimization_barrier((terms[0], second_other))
     total = summed(chunk_for(s).astype(jnp.float32) + tile[:1], terms)
     hidden = jax.nn.silu(total).astype(jnp.bfloat16)
     hidden = ordered(c, hidden, swapped(hidden, "chan"), 0)

time: 48.6 us -> 48.6 us (level)
  waiting for transfers between devices: 17.9 us -> 19 us
  starting transfers between devices: 22.7 us -> 21.8 us
    ppermute x6, waiting for transfers between devices: 7.79 us -> 9.3 us  [terms_of(): lax.ppermute(chunk, 'space', [(i, i ^ step) for i in range(4)])]
    ppermute x8, starting transfers between devices: 7.44 us -> 6.54 us  [swapped(): return lax.ppermute(array, axis, [(0, 1), (1, 0)])]
  transfers between devices with their start and end apart: 17 -> 17, of which waited for: 9 -> 11; matrix products, arithmetic and copies ran while one was open for 0% -> 0% of each run, Pallas kernels for 3% -> 7%
where the time goes in v8:
time: 48.6 us; the launch traced here: 48.4 us
  starting transfers between devices  21.8 us (45%)
  waiting for transfers between devices  19 us (39%)
  Pallas kernels  4.6 us (9%)
  local copies, waits for them, and re-layouts  1.81 us (4%)
  other arithmetic  0.89 us (2%)
    ppermute x6, waiting for transfers between devices, terms_of(): lax.ppermute(chunk, 'space', [(i, i ^ step) for i in range(4)])  9.3 us
    ppermute x6, starting transfers between devices, terms_of(): lax.ppermute(chunk, 'space', [(i, i ^ step) for i in range(4)])  8.07 us
    ppermute x8, starting transfers between devices, swapped(): return lax.ppermute(array, axis, [(0, 1), (1, 0)])  6.54 us
    ppermute x8, waiting for transfers between devices, swapped(): return lax.ppermute(array, axis, [(0, 1), (1, 0)])  5.83 us
    ppermute x1, starting transfers between devices, stationary(): late = lax.ppermute(late, group, late_route)  4.11 us
    ppermute x1, waiting for transfers between devices, stationary(): late = lax.ppermute(late, group, late_route)  3.83 us
    ppermute x1, starting transfers between devices, stationary(): early_other = lax.ppermute(up_rows_own, group, cross_route)  2.43 us
    pallas_call x1, Pallas kernels, first_conv(): pl.pallas_call(first_kernel, out_shape=(jax.ShapeDtypeStruct((2, 2, cells...  2.15 us
  transfers between devices with their start and end apart: 17, of which 11 were waited for; matrix products, arithmetic and copies ran while one was open for 0% of the time, Pallas kernels for 7%

profile of v8, /device:TPU:0, one launch (start us, length us, event | category | flops | bytes accessed | tf_op | source)
XLA Modules:
  0.0 48.4 jit_solution(11246178801075211867)
XLA Ops:
  0.0 1.0 %constant_dynamic-update-slice_fusion.4 = bf16[640,128]{1,0:T(8,128)(2,1)S(1)} fusion(bf16[512,128]{1,0:T(8,128)(2,1)} %bitcast.57), kind=kLoop, calls=%fused_computation.31 | loop fusion | bytes 262144
  1.1 0.1 pad_select_fusion
  1.1 0.0 copy-start.2
  1.1 4.1 %collective-permute-start.1 = (bf16[640,128]{1,0:T(8,128)(2,1)S(1)}, bf16[640,128]{1,0:T(8,128)(2,1)S(1)}, u32[]{:S(2)}, u32[]{:S(2)}) collective-permute-start(bf16[640,128]{1,0:T(8,128)(2,1)S(1)} %get-tuple-element.38), channel_id=1, source_target_pairs={{0,8},{1,12},{2,10},{3,14},{4,9},{5,13},{6,11},{7,15},{8,0},{9,4},... | collective-permute-start | bytes 491528 | tf_op jit(solution)/shard_map/ppermute | solution.py:440
  5.3 1.6 %collective-permute-start.6 = (bf16[14,64,128]{2,1,0:T(8,128)(2,1)S(1)}, bf16[14,64,128]{2,1,0:T(8,128)(2,1)S(1)}, u32[]{:S(2)}, u32[]{:S(2)}) collective-permute-start(bf16[14,64,128]{2,1,0:T(8,128)(2,1)S(1)} %dynamic-slice_bitcast_fusion), channel_id=1, source_target_pairs={{0,2},{2,0},{1,3},{3,1},{4,6},{6,4},{5,7},{7,5},{8,10},{10,8},{9,1... | collective-permute-start | bytes 688136 | tf_op jit(solution)/shard_map/ppermute | solution.py:91
  6.8 2.4 %collective-permute-start.2 = (bf16[512,128]{1,0:T(8,128)(2,1)S(1)}, bf16[512,128]{1,0:T(8,128)(2,1)S(1)}, u32[]{:S(2)}, u32[]{:S(2)}) collective-permute-start(bf16[512,128]{1,0:T(8,128)(2,1)S(1)} %bitcast.58), channel_id=1, source_target_pairs={{0,2},{1,6},{2,0},{3,4},{4,3},{5,7},{6,1},{7,5},{16,18},{17,22},{1... | collective-permute-start | bytes 393224 | tf_op jit(solution)/shard_map/ppermute | solution.py:443
  9.3 0.7 %collective-permute-start = (bf16[640,128]{1,0:T(8,128)(2,1)S(1)}, bf16[640,128]{1,0:T(8,128)(2,1)S(1)}, u32[]{:S(2)}, u32[]{:S(2)}) collective-permute-start(bf16[640,128]{1,0:T(8,128)(2,1)S(1)} %get-tuple-element.39), channel_id=1, source_target_pairs={{0,0},{1,4},{2,2},{3,6},{4,1},{5,5},{6,3},{7,7},{8,8},{9,12},{10,1... | collective-permute-start | bytes 491528 | tf_op jit(solution)/shard_map/ppermute | solution.py:442
  10.0 3.8 %collective-permute-done.1.late = bf16[640,128]{1,0:T(8,128)(2,1)S(1)} collective-permute-done((bf16[640,128]{1,0:T(8,128)(2,1)S(1)}, bf16[640,128]{1,0:T(8,128)(2,1)S(1)}, u32[]{:S(2)}, u32[]{:S(2)}) %collective-permute-start.1) | collective-permute-done | bytes 163872 | tf_op jit(solution)/shard_map/ppermute | solution.py:440
  13.8 1.6 %collective-permute-start.3 = (bf16[512,128]{1,0:T(8,128)(2,1)S(1)}, bf16[512,128]{1,0:T(8,128)(2,1)S(1)}, u32[]{:S(2)}, u32[]{:S(2)}) collective-permute-start(bf16[512,128]{1,0:T(8,128)(2,1)S(1)} %slice.40), channel_id=1, source_target_pairs={{0,2},{2,0},{1,3},{3,1},{4,6},{6,4},{5,7},{7,5},{8,10},{10,8},{9,1... | collective-permute-start | bytes 393224 | tf_op jit(solution)/shard_map/ppermute | solution.py:91
  15.4 0.0 collective-permute-done.6.near
  15.4 1.5 %collective-permute-start.7 = (bf16[14,64,128]{2,1,0:T(8,128)(2,1)S(1)}, bf16[14,64,128]{2,1,0:T(8,128)(2,1)S(1)}, u32[]{:S(2)}, u32[]{:S(2)}) collective-permute-start(bf16[14,64,128]{2,1,0:T(8,128)(2,1)S(1)} %collective-permute-done.6.near), channel_id=1, source_target_pairs={{0,16},{16,0},{1,17},{17,1},{2,18},{18,2},{3,19},{19,3},{4,20},{20... | collective-permute-start | bytes 688136 | tf_op jit(solution)/shard_map/ppermute | solution.py:91
  16.9 0.1 collective-permute-start.4
  17.0 0.0 copy-start.5
  17.0 0.0 copy-start.6
  17.0 0.0 copy-start.7
  17.0 0.6 %copy-done.5 = f32[128]{0:T(128)S(1)} copy-done((f32[128]{0:T(128)S(1)}, f32[128]{0:T(128)}, u32[]{:S(2)}) %copy-start.5) | copy-done | bytes 536
  17.6 0.0 copy-done.6
  17.7 0.0 copy-done.7
  17.7 0.1 shard_map.82.own
  17.8 1.6 %collective-permute-done.3.late_other = bf16[512,128]{1,0:T(8,128)(2,1)S(1)} collective-permute-done((bf16[512,128]{1,0:T(8,128)(2,1)S(1)}, bf16[512,128]{1,0:T(8,128)(2,1)S(1)}, u32[]{:S(2)}, u32[]{:S(2)}) %collective-permute-start.3) | collective-permute-done | bytes 131104 | tf_op jit(solution)/shard_map/ppermute | solution.py:91
  19.4 1.5 %collective-permute-start.9 = (bf16[27,32,128]{2,1,0:T(8,128)(2,1)S(1)}, bf16[27,32,128]{2,1,0:T(8,128)(2,1)S(1)}, u32[]{:S(2)}, u32[]{:S(2)}) collective-permute-start(bf16[27,32,128]{2,1,0:T(8,128)(2,1)S(1)} %shard_map.82.own), channel_id=1, source_target_pairs={{0,2},{2,0},{1,3},{3,1},{4,6},{6,4},{5,7},{7,5},{8,10},{10,8},{9,1... | collective-permute-start | bytes 663560 | tf_op jit(solution)/shard_map/ppermute | solution.py:91
  20.9 0.0 collective-permute-done.2.early_other
  20.9 0.0 collective-permute-done.4.slabs
  20.9 0.4 shard_map.83.mine
  21.3 0.1 collective-permute-start.5
  21.4 0.6 %collective-permute-done.7.far = bf16[14,64,128]{2,1,0:T(8,128)(2,1)S(1)} collective-permute-done((bf16[14,64,128]{2,1,0:T(8,128)(2,1)S(1)}, bf16[14,64,128]{2,1,0:T(8,128)(2,1)S(1)}, u32[]{:S(2)}, u32[]{:S(2)}) %collective-permute-start.7) | collective-permute-done | bytes 229408 | tf_op jit(solution)/shard_map/ppermute | solution.py:91
  22.0 0.1 shard_map.84.other
  22.1 1.2 %collective-permute-done.5.theirs = f32[1032,128]{1,0:T(8,128)S(1)} collective-permute-done((f32[1032,128]{1,0:T(8,128)S(1)}, f32[1032,128]{1,0:T(8,128)S(1)}, u32[]{:S(2)}, u32[]{:S(2)}) %collective-permute-start.5) | collective-permute-done | bytes 528416 | tf_op jit(solution)/shard_map/ppermute | solution.py:91
  23.3 2.1 %shard_map.85 = (bf16[2,2,256,128]{3,2,1,0:T(8,128)(2,1)S(1)}, f32[8,128]{1,0:T(8,128)S(1)}) custom-call(f32[1032,128]{1,0:T(8,128)S(1)} %shard_map.83.mine, f32[1032,128]{1,0:T(8,128)S(1)} %collective-permute-done.5.theirs, bf16[27,64,128]{2,1,0:T(8,128)(2,1)S(1)} %bitcast.53, bf16[27,64,128]{2,1,0:T(8,128)(2,1)S(1)} %shard_map.84.other), custom_call_target="tpu_custom_call" | custom-call | tf_op jit(solution)/shard_map/pallas_call | solution.py:325
  25.5 0.2 collective-permute-start.8
  25.7 0.3 collective-permute-done.9.other
  26.0 0.9 %collective-permute-done.8 = bf16[2,256,128]{2,1,0:T(8,128)(2,1)S(1)} collective-permute-done((bf16[2,256,128]{2,1,0:T(8,128)(2,1)S(1)}, bf16[2,256,128]{2,1,0:T(8,128)(2,1)S(1)}, u32[]{:S(2)}, u32[]{:S(2)}) %collective-permute-start.8) | collective-permute-done | bytes 131104 | tf_op jit(solution)/shard_map/ppermute | solution.py:91
  27.0 1.4 %collective-permute-start.10 = (bf16[256,128]{1,0:T(8,128)(2,1)S(1)}, bf16[256,128]{1,0:T(8,128)(2,1)S(1)}, u32[]{:S(2)}, u32[]{:S(2)}) collective-permute-start(bf16[256,128]{1,0:T(8,128)(2,1)S(1)} %get-tuple-element.33), channel_id=1, source_target_pairs={{0,12},{4,8},{8,4},{12,0},{1,13},{5,9},{9,5},{13,1},{2,14},{6,10},... | collective-permute-start | bytes 196616 | tf_op jit(solution)/shard_map/ppermute | solution.py:193
  28.4 3.1 %collective-permute-start.11 = (bf16[256,128]{1,0:T(8,128)(2,1)S(1)}, bf16[256,128]{1,0:T(8,128)(2,1)S(1)}, u32[]{:S(2)}, u32[]{:S(2)}) collective-permute-start(bf16[256,128]{1,0:T(8,128)(2,1)S(1)} %get-tuple-element.35), channel_id=1, source_target_pairs={{0,8},{4,12},{8,0},{12,4},{1,9},{5,13},{9,1},{13,5},{2,10},{6,14},... | collective-permute-start | bytes 196616 | tf_op jit(solution)/shard_map/ppermute | solution.py:193
  31.4 2.3 %collective-permute-done.10 = bf16[256,128]{1,0:T(8,128)(2,1)S(1)} collective-permute-done((bf16[256,128]{1,0:T(8,128)(2,1)S(1)}, bf16[256,128]{1,0:T(8,128)(2,1)S(1)}, u32[]{:S(2)}, u32[]{:S(2)}) %collective-permute-start.10) | collective-permute-done | bytes 65568 | tf_op jit(solution)/shard_map/ppermute | solution.py:193
  33.8 1.2 %collective-permute-done.12 = bf16[256,128]{1,0:T(8,128)(2,1)S(1)} collective-permute-done((bf16[256,128]{1,0:T(8,128)(2,1)S(1)}, bf16[256,128]{1,0:T(8,128)(2,1)S(1)}, u32[]{:S(2)}, u32[]{:S(2)}) %collective-permute-start.12) | collective-permute-done | bytes 65568 | tf_op jit(solution)/shard_map/ppermute | solution.py:193
  35.0 0.9 %collective-permute-done.11 = bf16[256,128]{1,0:T(8,128)(2,1)S(1)} collective-permute-done((bf16[256,128]{1,0:T(8,128)(2,1)S(1)}, bf16[256,128]{1,0:T(8,128)(2,1)S(1)}, u32[]{:S(2)}, u32[]{:S(2)}) %collective-permute-start.11) | collective-permute-done | bytes 65568 | tf_op jit(solution)/shard_map/ppermute | solution.py:193
  35.8 0.1 multiply_convert_fusion
  35.9 0.1 collective-permute-start.13
  36.0 1.2 %collective-permute-done.13 = bf16[256,128]{1,0:T(8,128)(2,1)S(1)} collective-permute-done((bf16[256,128]{1,0:T(8,128)(2,1)S(1)}, bf16[256,128]{1,0:T(8,128)(2,1)S(1)}, u32[]{:S(2)}, u32[]{:S(2)}) %collective-permute-start.13) | collective-permute-done | bytes 65568 | tf_op jit(solution)/shard_map/ppermute | solution.py:91
  37.3 1.1 %shard_map.86 = (bf16[2,256,128]{2,1,0:T(8,128)(2,1)S(1)}, f32[8,128]{1,0:T(8,128)S(1)}, bf16[10,128,256]{2,1,0:T(8,128)(2,1)S(1)}, bf16[10,144,256]{2,1,0:T(8,128)(2,1)S(1)}, bf16[9,192,128]{2,1,0:T(8,128)(2,1)S(1)}) custom-call(bf16[2,256,128]{2,1,0:T(8,128)(2,1)S(1)} %pad_maximum_fusion.1.hidden, bf16[27,32,128]{2,1,0:T(8,128)(2,1)S(1)} %shard_map.82.own, ...), custom_call_target="tpu_custom_call" | custom-call | tf_op jit(solution)/shard_map/pallas_call | solution.py:386
  38.4 0.9 %collective-permute-start.15 = (bf16[256,128]{1,0:T(8,128)(2,1)S(1)}, bf16[256,128]{1,0:T(8,128)(2,1)S(1)}, u32[]{:S(2)}, u32[]{:S(2)}) collective-permute-start(bf16[256,128]{1,0:T(8,128)(2,1)S(1)} %get-tuple-element.40), channel_id=1, source_target_pairs={{0,8},{4,12},{8,0},{12,4},{1,9},{5,13},{9,1},{13,5},{2,10},{6,14},... | collective-permute-start | bytes 196616 | tf_op jit(solution)/shard_map/ppermute | solution.py:193
  39.2 2.1 %collective-permute-start.14 = (bf16[256,128]{1,0:T(8,128)(2,1)S(1)}, bf16[256,128]{1,0:T(8,128)(2,1)S(1)}, u32[]{:S(2)}, u32[]{:S(2)}) collective-permute-start(bf16[256,128]{1,0:T(8,128)(2,1)S(1)} %get-tuple-element.41), channel_id=1, source_target_pairs={{0,12},{4,8},{8,4},{12,0},{1,13},{5,9},{9,5},{13,1},{2,14},{6,10},... | collective-permute-start | bytes 196616 | tf_op jit(solution)/shard_map/ppermute | solution.py:193
  41.4 0.8 %shard_map.87 = bf16[2,256,128]{2,1,0:T(8,128)(2,1)S(1)} custom-call(bf16[10,128,256]{2,1,0:T(8,128)(2,1)S(1)} %get-tuple-element.29.even, bf16[10,144,256]{2,1,0:T(8,128)(2,1)S(1)} %get-tuple-element.30.odd, bf16[9,192,128]{2,1,0:T(8,128)(2,1)S(1)} %get-tuple-element.31.rights), custom_call_target="tpu_custom_call" | custom-call | tf_op jit(solution)/shard_map/pallas_call | solution.py:403
  42.1 0.6 %collective-permute-start.16 = (bf16[256,128]{1,0:T(8,128)(2,1)S(1)}, bf16[256,128]{1,0:T(8,128)(2,1)S(1)}, u32[]{:S(2)}, u32[]{:S(2)}) collective-permute-start(bf16[256,128]{1,0:T(8,128)(2,1)S(1)} %dynamic-slice_bitcast_fusion.2), channel_id=1, source_target_pairs={{0,4},{4,0},{8,12},{12,8},{1,5},{5,1},{9,13},{13,9},{2,6},{6,2},{1... | collective-permute-start | bytes 196616 | tf_op jit(solution)/shard_map/ppermute | solution.py:193
  42.8 4.9 %collective-permute-done.16 = bf16[256,128]{1,0:T(8,128)(2,1)S(1)} collective-permute-done((bf16[256,128]{1,0:T(8,128)(2,1)S(1)}, bf16[256,128]{1,0:T(8,128)(2,1)S(1)}, u32[]{:S(2)}, u32[]{:S(2)}) %collective-permute-start.16) | collective-permute-done | bytes 65568 | tf_op jit(solution)/shard_map/ppermute | solution.py:193
  47.7 0.0 collective-permute-done.15
  47.7 0.7 %fusion.3 = bf16[256,128]{1,0:T(8,128)(2,1)} fusion(bf16[256,128]{1,0:T(8,128)(2,1)S(1)} %collective-permute-done.16, bf16[256,128]{1,0:T(8,128)(2,1)S(1)} %collective-permute-done.15, bf16[256,128]{1,0:T(8,128)(2,1)S(1)} %collective-permute-done.14, f32[128]{0:T(128)S(1)} %slice_bitcast_fusion.2, bf16[2,256,128]{2,1,0:T(8,128)(2,1)S(1)} %shard_map.87, ...), kind=kLoop, calls=%fused_computation.9 | loop fusion | flops 294912 | bytes 328196 | tf_op jit(solution)/shard_map/convert_element_type | solution.py:473
  (31 shorter events, 0.3 us)
Async XLA Ops:
  0.0 1.0 %copy-start.4 = (bf16[1,1,4,8,512]{4,3,2,1,0:T(8,128)(2,1)S(1)}, bf16[1,1,4,8,512]{4,3,2,1,0:T(8,128)(2,1)}, u32[]{:S(2)}) copy-start(bf16[1,1,4,8,512]{4,3,2,1,0:T(8,128)(2,1)} %param.8) | copy-start | bytes 98308
  0.0 1.0 %copy-start.3 = (bf16[1,2,16,8,128]{4,3,2,1,0:T(8,128)(2,1)S(1)}, bf16[1,2,16,8,128]{4,3,2,1,0:T(8,128)(2,1)}, u32[]{:S(2)}) copy-start(bf16[1,2,16,8,128]{4,3,2,1,0:T(8,128)(2,1)} %param.9) | copy-start | bytes 196612
  0.0 5.2 %copy-start = (bf16[27,128,1,64]{1,3,2,0:T(8,128)(2,1)S(1)}, bf16[27,128,1,64]{1,3,2,0:T(8,128)(2,1)}, u32[]{:S(2)}) copy-start(bf16[27,128,1,64]{1,3,2,0:T(8,128)(2,1)} %param.12) | copy-start | bytes 1327108
  1.1 5.7 %copy-start.2 = (bf16[8,128,1,64]{1,3,2,0:T(8,128)(2,1)S(1)}, bf16[8,128,1,64]{1,3,2,0:T(8,128)(2,1)}, u32[]{:S(2)}) copy-start(bf16[8,128,1,64]{1,3,2,0:T(8,128)(2,1)} %param.10) | copy-start | bytes 393220
  1.1 12.6 %collective-permute-start.1 = (bf16[640,128]{1,0:T(8,128)(2,1)S(1)}, bf16[640,128]{1,0:T(8,128)(2,1)S(1)}, u32[]{:S(2)}, u32[]{:S(2)}) collective-permute-start(bf16[640,128]{1,0:T(8,128)(2,1)S(1)} %get-tuple-element.38), channel_id=1, source_target_pairs={{0,8},{1,12},{2,10},{3,14},{4,9},{5,13},{6,11},{7,15},{8,0},{9,4},... | collective-permute-start | bytes 491528 | tf_op jit(solution)/shard_map/ppermute | solution.py:440
  5.2 12.4 %copy-start.1 = (bf16[27,64,1,64]{3,1,2,0:T(8,128)(2,1)S(1)}, bf16[27,64,1,64]{3,1,2,0:T(8,128)(2,1)}, u32[]{:S(2)}) copy-start(bf16[27,64,1,64]{3,1,2,0:T(8,128)(2,1)} %param.14) | copy-start | bytes 663556
  5.3 10.1 %collective-permute-start.6 = (bf16[14,64,128]{2,1,0:T(8,128)(2,1)S(1)}, bf16[14,64,128]{2,1,0:T(8,128)(2,1)S(1)}, u32[]{:S(2)}, u32[]{:S(2)}) collective-permute-start(bf16[14,64,128]{2,1,0:T(8,128)(2,1)S(1)} %dynamic-slice_bitcast_fusion), channel_id=1, source_target_pairs={{0,2},{2,0},{1,3},{3,1},{4,6},{6,4},{5,7},{7,5},{8,10},{10,8},{9,1... | collective-permute-start | bytes 688136 | tf_op jit(solution)/shard_map/ppermute | solution.py:91
  6.8 14.1 %collective-permute-start.2 = (bf16[512,128]{1,0:T(8,128)(2,1)S(1)}, bf16[512,128]{1,0:T(8,128)(2,1)S(1)}, u32[]{:S(2)}, u32[]{:S(2)}) collective-permute-start(bf16[512,128]{1,0:T(8,128)(2,1)S(1)} %bitcast.58), channel_id=1, source_target_pairs={{0,2},{1,6},{2,0},{3,4},{4,3},{5,7},{6,1},{7,5},{16,18},{17,22},{1... | collective-permute-start | bytes 393224 | tf_op jit(solution)/shard_map/ppermute | solution.py:443
  9.3 7.6 %collective-permute-start = (bf16[640,128]{1,0:T(8,128)(2,1)S(1)}, bf16[640,128]{1,0:T(8,128)(2,1)S(1)}, u32[]{:S(2)}, u32[]{:S(2)}) collective-permute-start(bf16[640,128]{1,0:T(8,128)(2,1)S(1)} %get-tuple-element.39), channel_id=1, source_target_pairs={{0,0},{1,4},{2,2},{3,6},{4,1},{5,5},{6,3},{7,7},{8,8},{9,12},{10,1... | collective-permute-start | bytes 491528 | tf_op jit(solution)/shard_map/ppermute | solution.py:442
  13.8 5.6 %collective-permute-start.3 = (bf16[512,128]{1,0:T(8,128)(2,1)S(1)}, bf16[512,128]{1,0:T(8,128)(2,1)S(1)}, u32[]{:S(2)}, u32[]{:S(2)}) collective-permute-start(bf16[512,128]{1,0:T(8,128)(2,1)S(1)} %slice.40), channel_id=1, source_target_pairs={{0,2},{2,0},{1,3},{3,1},{4,6},{6,4},{5,7},{7,5},{8,10},{10,8},{9,1... | collective-permute-start | bytes 393224 | tf_op jit(solution)/shard_map/ppermute | solution.py:91
  15.4 6.7 %collective-permute-start.7 = (bf16[14,64,128]{2,1,0:T(8,128)(2,1)S(1)}, bf16[14,64,128]{2,1,0:T(8,128)(2,1)S(1)}, u32[]{:S(2)}, u32[]{:S(2)}) collective-permute-start(bf16[14,64,128]{2,1,0:T(8,128)(2,1)S(1)} %collective-permute-done.6.near), channel_id=1, source_target_pairs={{0,16},{16,0},{1,17},{17,1},{2,18},{18,2},{3,19},{19,3},{4,20},{20... | collective-permute-start | bytes 688136 | tf_op jit(solution)/shard_map/ppermute | solution.py:91
  16.9 4.0 %collective-permute-start.4 = (bf16[2,128,128]{2,1,0:T(8,128)(2,1)S(1)}, bf16[2,128,128]{2,1,0:T(8,128)(2,1)S(1)}, u32[]{:S(2)}, u32[]{:S(2)}) collective-permute-start(bf16[2,128,128]{2,1,0:T(8,128)(2,1)S(1)} %pad_maximum_fusion.2), channel_id=1, source_target_pairs={{0,1},{1,0},{2,3},{3,2},{4,5},{5,4},{6,7},{7,6},{8,9},{9,8},{10,11... | collective-permute-start | bytes 196616 | tf_op jit(solution)/shard_map/ppermute | solution.py:91
  17.0 0.7 %copy-start.5 = (f32[128]{0:T(128)S(1)}, f32[128]{0:T(128)}, u32[]{:S(2)}) copy-start(f32[128]{0:T(128)} %param.15) | copy-start | bytes 1540
  17.0 0.7 %copy-start.6 = (f32[128]{0:T(128)S(1)}, f32[128]{0:T(128)}, u32[]{:S(2)}) copy-start(f32[128]{0:T(128)} %param.13) | copy-start | bytes 1540
  17.0 0.7 %copy-start.7 = (f32[128]{0:T(128)S(1)}, f32[128]{0:T(128)}, u32[]{:S(2)}) copy-start(f32[128]{0:T(128)} %param.11) | copy-start | bytes 1540
  19.4 6.6 %collective-permute-start.9 = (bf16[27,32,128]{2,1,0:T(8,128)(2,1)S(1)}, bf16[27,32,128]{2,1,0:T(8,128)(2,1)S(1)}, u32[]{:S(2)}, u32[]{:S(2)}) collective-permute-start(bf16[27,32,128]{2,1,0:T(8,128)(2,1)S(1)} %shard_map.82.own), channel_id=1, source_target_pairs={{0,2},{2,0},{1,3},{3,1},{4,6},{6,4},{5,7},{7,5},{8,10},{10,8},{9,1... | collective-permute-start | bytes 663560 | tf_op jit(solution)/shard_map/ppermute | solution.py:91
  21.3 2.0 %collective-permute-start.5 = (f32[1032,128]{1,0:T(8,128)S(1)}, f32[1032,128]{1,0:T(8,128)S(1)}, u32[]{:S(2)}, u32[]{:S(2)}) collective-permute-start(f32[1032,128]{1,0:T(8,128)S(1)} %shard_map.83.mine), channel_id=1, source_target_pairs={{0,1},{1,0},{2,3},{3,2},{4,5},{5,4},{6,7},{7,6},{8,9},{9,8},{10,11... | collective-permute-start | bytes 1585160 | tf_op jit(solution)/shard_map/ppermute | solution.py:91
  25.5 1.4 %collective-permute-start.8 = (bf16[2,256,128]{2,1,0:T(8,128)(2,1)S(1)}, bf16[2,256,128]{2,1,0:T(8,128)(2,1)S(1)}, u32[]{:S(2)}, u32[]{:S(2)}) collective-permute-start(bf16[2,256,128]{2,1,0:T(8,128)(2,1)S(1)} %get-tuple-element.37), channel_id=1, source_target_pairs={{0,1},{1,0},{2,3},{3,2},{4,5},{5,4},{6,7},{7,6},{8,9},{9,8},{10,11... | collective-permute-start | bytes 393224 | tf_op jit(solution)/shard_map/ppermute | solution.py:91
  27.0 6.8 %collective-permute-start.10 = (bf16[256,128]{1,0:T(8,128)(2,1)S(1)}, bf16[256,128]{1,0:T(8,128)(2,1)S(1)}, u32[]{:S(2)}, u32[]{:S(2)}) collective-permute-start(bf16[256,128]{1,0:T(8,128)(2,1)S(1)} %get-tuple-element.33), channel_id=1, source_target_pairs={{0,12},{4,8},{8,4},{12,0},{1,13},{5,9},{9,5},{13,1},{2,14},{6,10},... | collective-permute-start | bytes 196616 | tf_op jit(solution)/shard_map/ppermute | solution.py:193
  28.4 6.6 %collective-permute-start.12 = (bf16[256,128]{1,0:T(8,128)(2,1)S(1)}, bf16[256,128]{1,0:T(8,128)(2,1)S(1)}, u32[]{:S(2)}, u32[]{:S(2)}) collective-permute-start(bf16[256,128]{1,0:T(8,128)(2,1)S(1)} %get-tuple-element.34), channel_id=1, source_target_pairs={{0,4},{4,0},{8,12},{12,8},{1,5},{5,1},{9,13},{13,9},{2,6},{6,2},{1... | collective-permute-start | bytes 196616 | tf_op jit(solution)/shard_map/ppermute | solution.py:193
  28.4 7.5 %collective-permute-start.11 = (bf16[256,128]{1,0:T(8,128)(2,1)S(1)}, bf16[256,128]{1,0:T(8,128)(2,1)S(1)}, u32[]{:S(2)}, u32[]{:S(2)}) collective-permute-start(bf16[256,128]{1,0:T(8,128)(2,1)S(1)} %get-tuple-element.35), channel_id=1, source_target_pairs={{0,8},{4,12},{8,0},{12,4},{1,9},{5,13},{9,1},{13,5},{2,10},{6,14},... | collective-permute-start | bytes 196616 | tf_op jit(solution)/shard_map/ppermute | solution.py:193
  35.9 1.3 %collective-permute-start.13 = (bf16[256,128]{1,0:T(8,128)(2,1)S(1)}, bf16[256,128]{1,0:T(8,128)(2,1)S(1)}, u32[]{:S(2)}, u32[]{:S(2)}) collective-permute-start(bf16[256,128]{1,0:T(8,128)(2,1)S(1)} %multiply_convert_fusion), channel_id=1, source_target_pairs={{0,1},{1,0},{2,3},{3,2},{4,5},{5,4},{6,7},{7,6},{8,9},{9,8},{10,11... | collective-permute-start | bytes 196616 | tf_op jit(solution)/shard_map/ppermute | solution.py:91
  38.4 9.3 %collective-permute-start.15 = (bf16[256,128]{1,0:T(8,128)(2,1)S(1)}, bf16[256,128]{1,0:T(8,128)(2,1)S(1)}, u32[]{:S(2)}, u32[]{:S(2)}) collective-permute-start(bf16[256,128]{1,0:T(8,128)(2,1)S(1)} %get-tuple-element.40), channel_id=1, source_target_pairs={{0,8},{4,12},{8,0},{12,4},{1,9},{5,13},{9,1},{13,5},{2,10},{6,14},... | collective-permute-start | bytes 196616 | tf_op jit(solution)/shard_map/ppermute | solution.py:193
  39.2 8.5 %collective-permute-start.14 = (bf16[256,128]{1,0:T(8,128)(2,1)S(1)}, bf16[256,128]{1,0:T(8,128)(2,1)S(1)}, u32[]{:S(2)}, u32[]{:S(2)}) collective-permute-start(bf16[256,128]{1,0:T(8,128)(2,1)S(1)} %get-tuple-element.41), channel_id=1, source_target_pairs={{0,12},{4,8},{8,4},{12,0},{1,13},{5,9},{9,5},{13,1},{2,14},{6,10},... | collective-permute-start | bytes 196616 | tf_op jit(solution)/shard_map/ppermute | solution.py:193
  42.1 5.6 %collective-permute-start.16 = (bf16[256,128]{1,0:T(8,128)(2,1)S(1)}, bf16[256,128]{1,0:T(8,128)(2,1)S(1)}, u32[]{:S(2)}, u32[]{:S(2)}) collective-permute-start(bf16[256,128]{1,0:T(8,128)(2,1)S(1)} %dynamic-slice_bitcast_fusion.2), channel_id=1, source_target_pairs={{0,4},{4,0},{8,12},{12,8},{1,5},{5,1},{9,13},{13,9},{2,6},{6,2},{1... | collective-permute-start | bytes 196616 | tf_op jit(solution)/shard_map/ppermute | solution.py:193
